TPU v7x, 32 devices: a whole 2x2x4 slice. The times are simulated.
32 devices in a mesh: dp: 8 (over y, x, core), tensor: 4 (over z).
Axes of the slice: x: 2, y: 2, z: 4, core: 2. Of those that a mesh axis runs over, the one named last changes fastest.
Arguments:
- activations: float32 [8, 1024, 2048], P('dp'), may hold values from -6 to 6
- gain_one: float32 [2048], replicated, may hold values from 0.25 to 1.75
- gelu_branch: bfloat16 [2048, 2560], P('dp', 'tensor'), may hold values from -0.125 to 0.125
- lru_branch: bfloat16 [2048, 2560], P('dp', 'tensor'), may hold values from -0.125 to 0.125
- conv_weight: float32 [4, 2560], P(None, 'tensor'), may hold values from -3 to 3
- conv_bias: float32 [2560], P('tensor'), may hold values from -3 to 3
- recur_weight: bfloat16 [2560, 160], P('tensor', 'dp'), may hold values from -0.5 to 0.5
- inlet_weight: bfloat16 [2560, 160], P('tensor', 'dp'), may hold values from -0.5 to 0.5
- recur_bias: float32 [2560], P('tensor'), may hold values from -3 to 3
- inlet_bias: float32 [2560], P('tensor'), may hold values from -3 to 3
- decay_param: float32 [2560], P('tensor'), may hold values from 4.3 to 9
- out_weight: bfloat16 [2560, 2048], P('tensor', 'dp'), may hold values from -0.125 to 0.125
- gain_two: float32 [2048], replicated, may hold values from 0.25 to 1.75
- ffn_gate: bfloat16 [2048, 6144], P('dp', 'tensor'), may hold values from -0.125 to 0.125
- ffn_value: bfloat16 [2048, 6144], P('dp', 'tensor'), may hold values from -0.125 to 0.125
- ffn_down: bfloat16 [6144, 2048], P('tensor', 'dp'), may hold values from -0.078125 to 0.078125
- doc_starts: int32 [8, 3], P('dp'), may hold values from 1 to 1023, as said below
- recur_state: float32 [8, 2560], P('dp', 'tensor'), may hold values from -5 to 5
- conv_state: float32 [8, 3, 2560], P('dp', None, 'tensor'), may hold values from -5 to 5
- cotangent: float32 [8, 1024, 2048], P('dp'), may hold values from -6 to 6
Outputs:
- block_output: float32 [8, 1024, 2048], P('dp')
- recur_final: float32 [8, 2560], P('dp', 'tensor')
- conv_final: float32 [8, 3, 2560], P('dp', None, 'tensor')
- input_grad: float32 [8, 1024, 2048], P('dp')
- gain_one_grad: float32 [2048], replicated
- gelu_branch_grad: float32 [2048, 2560], P('dp', 'tensor')
- lru_branch_grad: float32 [2048, 2560], P('dp', 'tensor')
- conv_weight_grad: float32 [4, 2560], P(None, 'tensor')
- conv_bias_grad: float32 [2560], P('tensor')
- recur_weight_grad: float32 [2560, 160], P('tensor', 'dp')
- inlet_weight_grad: float32 [2560, 160], P('tensor', 'dp')
- recur_bias_grad: float32 [2560], P('tensor')
- inlet_bias_grad: float32 [2560], P('tensor')
- decay_param_grad: float32 [2560], P('tensor')
- out_weight_grad: float32 [2560, 2048], P('tensor', 'dp')
- gain_two_grad: float32 [2048], replicated
- ffn_gate_grad: float32 [2048, 6144], P('dp', 'tensor')
- ffn_value_grad: float32 [2048, 6144], P('dp', 'tensor')
- ffn_down_grad: float32 [6144, 2048], P('tensor', 'dp')
Inputs may be any that keep to these rules, and one draw needn't show every extreme that they name: `doc_starts`: each row holds exactly 3 distinct positions in increasing order.
All inputs are finite; a program needn't handle non-finite values.
Results may differ from a plain program's by a relative error of at most 0.012.
The roundings to bfloat16 on the way count: a program that leaves them out, or rounds other values in their place, can miss the bound.
Values may be sent and summed in bfloat16 or wider, within the bound.
No kernel may reach another device: no remote copies, remote signals or barrier semaphores. Data moves between devices by JAX's collectives and lax.ppermute only.
A program may use at most 384 MiB of HBM per device.

v0:
```python
import jax
import jax.numpy as jnp
from jax import lax
from jax.sharding import PartitionSpec as P

EPS = 1e-06


def gelu_fn(values):
    return jax.nn.gelu(values, approximate=True)


def rms_norm(values, gain):
    return values * lax.rsqrt(jnp.mean(values * values, axis=-1, keepdims=True) + EPS) * gain


def positions(starts, length):
    places = jnp.arange(length, dtype=jnp.int32)
    resets = jnp.any(places[:, None] == starts[None, :], axis=1)
    begins = jnp.max(jnp.where(starts[None, :] <= places[:, None], starts[None, :], -3), axis=1)
    return (resets, begins)


def convolve(inputs, history, begins, weight, bias):
    length = inputs.shape[0]
    extended = jnp.concatenate([history, inputs], axis=0)
    places = jnp.arange(length, dtype=jnp.int32)
    total = jnp.zeros_like(inputs) + bias
    for lag in range(4):
        usable = (places - lag >= begins)[:, None]
        total = total + weight[lag] * jnp.where(usable, extended[3 - lag : 3 - lag + length], 0.0)
    return total


def combine(earlier, later):
    return (earlier[0] * later[0], later[0] * earlier[1] + later[1])


def recurrence(mixed, recur_pre, inlet_pre, recur_bias, inlet_bias, decays, resets, start_state):
    rates = jax.nn.sigmoid(recur_pre + recur_bias)
    inlet = jax.nn.sigmoid(inlet_pre + inlet_bias)
    log_decay = -8.0 * rates * jax.nn.softplus(-decays)
    factor = jnp.exp(log_decay)
    scales = jnp.where(
        resets[:, None], 1.0, jnp.sqrt(jnp.maximum(-jnp.expm1(2.0 * log_decay), 0.001))
    )
    carries = jnp.where(resets[:, None], 0.0, factor)
    drive = scales * inlet * mixed
    first = (jnp.arange(mixed.shape[0]) == 0)[:, None]
    drive = drive + jnp.where(first, carries * start_state[None, :], 0.0)
    _, states = lax.associative_scan(combine, (carries, drive), axis=0)
    return states


def contract_rows(left, right):
    return lax.dot_general(
        left, right, (((0,), (0,)), ((), ())), preferred_element_type=jnp.float32
    )


def contract_cols(left, right):
    return lax.dot_general(
        left, right, (((1,), (1,)), ((), ())), preferred_element_type=jnp.float32
    )


def heads_fwd(values, weight, head_size):
    count = weight.shape[0] // head_size
    tokens = values.shape[0]
    shaped = values.reshape(tokens, count, head_size)
    blocks = weight.reshape(count, head_size, head_size)
    return jnp.einsum("thi,hij->thj", shaped, blocks, preferred_element_type=jnp.float32).reshape(
        tokens, count * head_size
    )


def heads_back(grads, weight, head_size):
    count = weight.shape[0] // head_size
    tokens = grads.shape[0]
    shaped = grads.reshape(tokens, count, head_size)
    blocks = weight.reshape(count, head_size, head_size)
    return jnp.einsum("thj,hij->thi", shaped, blocks, preferred_element_type=jnp.float32).reshape(
        tokens, count * head_size
    )


def heads_weight(values, grads, head_size):
    tokens = values.shape[0]
    count = values.shape[1] // head_size
    shaped = values.reshape(tokens, count, head_size)
    grad_shaped = grads.reshape(tokens, count, head_size)
    return jnp.einsum(
        "thi,thj->hij", shaped, grad_shaped, preferred_element_type=jnp.float32
    ).reshape(count * head_size, head_size)


def tensor_reduce(partial_sum):
    return lax.psum(partial_sum, "tensor")


def per_device(
    activations,
    gain_one,
    gelu_branch,
    lru_branch,
    conv_weight,
    conv_bias,
    recur_weight,
    inlet_weight,
    recur_bias,
    inlet_bias,
    decay_param,
    out_weight,
    gain_two,
    ffn_gate,
    ffn_value,
    ffn_down,
    doc_starts,
    recur_state,
    conv_state,
    cotangent,
):
    rows, length, width = activations.shape
    tokens = rows * length
    flat = activations.reshape(tokens, width)
    gelu_full, lru_full, recur_full, inlet_full, out_full = (
        lax.all_gather(gelu_branch, "dp", axis=0, tiled=True),
        lax.all_gather(lru_branch, "dp", axis=0, tiled=True),
        lax.all_gather(recur_weight, "dp", axis=1, tiled=True),
        lax.all_gather(inlet_weight, "dp", axis=1, tiled=True),
        lax.all_gather(out_weight, "dp", axis=1, tiled=True),
    )
    head_size = recur_full.shape[1]
    resets, begins = jax.vmap(positions, in_axes=(0, None))(doc_starts, length)
    normed, norm_pull = jax.vjp(rms_norm, flat, gain_one)
    normed_low = normed.astype(jnp.bfloat16)
    gate_pre = jnp.dot(normed_low, gelu_full, preferred_element_type=jnp.float32)
    branch = jnp.dot(normed_low, lru_full, preferred_element_type=jnp.float32)
    channels = branch.shape[1]
    branch_rows = branch.reshape(rows, length, channels)

    def conv_rows(inputs, weight, bias):
        return jax.vmap(convolve, in_axes=(0, 0, 0, None, None))(
            inputs, conv_state, begins, weight, bias
        )

    mixed, conv_pull = jax.vjp(conv_rows, branch_rows, conv_weight, conv_bias)
    mixed_low = mixed.astype(jnp.bfloat16).reshape(tokens, channels)
    mixed_round = mixed_low.astype(jnp.float32).reshape(rows, length, channels)
    recur_pre = heads_fwd(mixed_low, recur_full, head_size).reshape(rows, length, channels)
    inlet_pre = heads_fwd(mixed_low, inlet_full, head_size).reshape(rows, length, channels)

    def run_lru(values, recur_in, inlet_in, bias_recur, bias_inlet, decays):
        return jax.vmap(recurrence, in_axes=(0, 0, 0, None, None, None, 0, 0))(
            values, recur_in, inlet_in, bias_recur, bias_inlet, decays, resets, recur_state
        )

    states, lru_pull = jax.vjp(
        run_lru, mixed_round, recur_pre, inlet_pre, recur_bias, inlet_bias, decay_param
    )
    states_flat = states.reshape(tokens, channels)
    gate_act, gelu_pull = jax.vjp(gelu_fn, gate_pre)
    product_low = (states_flat * gate_act).astype(jnp.bfloat16)
    recur_out = tensor_reduce(jnp.dot(product_low, out_full, preferred_element_type=jnp.float32))
    gate_full, value_full, down_full = (
        lax.all_gather(ffn_gate, "dp", axis=0, tiled=True),
        lax.all_gather(ffn_value, "dp", axis=0, tiled=True),
        lax.all_gather(ffn_down, "dp", axis=1, tiled=True),
    )
    middle_part = flat + recur_out
    normed_two, norm_two_pull = jax.vjp(rms_norm, middle_part, gain_two)
    normed_two_low = normed_two.astype(jnp.bfloat16)
    gate_two = jnp.dot(normed_two_low, gate_full, preferred_element_type=jnp.float32)
    value_two = jnp.dot(normed_two_low, value_full, preferred_element_type=jnp.float32)
    gate_two_act, gelu_two_pull = jax.vjp(gelu_fn, gate_two)
    inner_low = (gate_two_act * value_two).astype(jnp.bfloat16)
    ffn_out = tensor_reduce(jnp.dot(inner_low, down_full, preferred_element_type=jnp.float32))
    output_part = middle_part + ffn_out
    recur_final = states[:, length - 1, :]
    places = length - 3 + jnp.arange(3, dtype=jnp.int32)
    conv_keep = (places[None, :] >= begins[:, length - 1 : length])[:, :, None]
    conv_final = jnp.where(conv_keep, branch_rows[:, length - 3 :, :], 0.0)
    gate_full, value_full, down_full = (
        lax.all_gather(ffn_gate, "dp", axis=0, tiled=True),
        lax.all_gather(ffn_value, "dp", axis=0, tiled=True),
        lax.all_gather(ffn_down, "dp", axis=1, tiled=True),
    )
    gelu_full, lru_full, recur_full, inlet_full, out_full = (
        lax.all_gather(gelu_branch, "dp", axis=0, tiled=True),
        lax.all_gather(lru_branch, "dp", axis=0, tiled=True),
        lax.all_gather(recur_weight, "dp", axis=1, tiled=True),
        lax.all_gather(inlet_weight, "dp", axis=1, tiled=True),
        lax.all_gather(out_weight, "dp", axis=1, tiled=True),
    )
    incoming = cotangent.reshape(tokens, width)
    incoming_low = incoming.astype(jnp.bfloat16)
    down_grad = contract_rows(inner_low, incoming_low)
    inner_grad = contract_cols(incoming_low, down_full)
    gate_two_grad = gelu_two_pull(inner_grad * value_two)[0].astype(jnp.bfloat16)
    value_two_grad = (inner_grad * gate_two_act).astype(jnp.bfloat16)
    gate_w_grad = contract_rows(normed_two_low, gate_two_grad)
    value_w_grad = contract_rows(normed_two_low, value_two_grad)
    ffn_grads = (
        lax.psum_scatter(gate_w_grad, "dp", scatter_dimension=0, tiled=True),
        lax.psum_scatter(value_w_grad, "dp", scatter_dimension=0, tiled=True),
        lax.psum_scatter(down_grad, "dp", scatter_dimension=1, tiled=True),
    )
    normed_two_grad = tensor_reduce(
        contract_cols(gate_two_grad, gate_full) + contract_cols(value_two_grad, value_full)
    )
    middle_back, gain_two_grad = norm_two_pull(normed_two_grad)
    middle_grad_part = incoming + middle_back
    middle_low = middle_grad_part.astype(jnp.bfloat16)
    out_w_grad = contract_rows(product_low, middle_low)
    product_grad = contract_cols(middle_low, out_full)
    gate_pre_grad = gelu_pull(product_grad * states_flat)[0].astype(jnp.bfloat16)
    states_grad = (product_grad * gate_act).reshape(rows, length, channels)
    mixed_part, recur_in_grad, inlet_in_grad, recur_bias_grad, inlet_bias_grad, decay_grad = (
        lru_pull(states_grad)
    )
    recur_low = recur_in_grad.reshape(tokens, channels).astype(jnp.bfloat16)
    inlet_low = inlet_in_grad.reshape(tokens, channels).astype(jnp.bfloat16)
    mixed_grad = (
        mixed_part.reshape(tokens, channels)
        + heads_back(recur_low, recur_full, head_size)
        + heads_back(inlet_low, inlet_full, head_size)
    )
    recur_w_grad = heads_weight(mixed_low, recur_low, head_size)
    inlet_w_grad = heads_weight(mixed_low, inlet_low, head_size)
    branch_grad_rows, conv_w_grad, conv_b_grad = conv_pull(
        mixed_grad.reshape(rows, length, channels)
    )
    branch_low = branch_grad_rows.reshape(tokens, channels).astype(jnp.bfloat16)
    gelu_w_grad = contract_rows(normed_low, gate_pre_grad)
    lru_w_grad = contract_rows(normed_low, branch_low)
    recur_grads = (
        lax.psum_scatter(gelu_w_grad, "dp", scatter_dimension=0, tiled=True),
        lax.psum_scatter(lru_w_grad, "dp", scatter_dimension=0, tiled=True),
        lax.psum_scatter(recur_w_grad, "dp", scatter_dimension=1, tiled=True),
        lax.psum_scatter(inlet_w_grad, "dp", scatter_dimension=1, tiled=True),
        lax.psum_scatter(out_w_grad, "dp", scatter_dimension=1, tiled=True),
    )
    normed_grad = tensor_reduce(
        contract_cols(gate_pre_grad, gelu_full) + contract_cols(branch_low, lru_full)
    )
    flat_back, gain_one_grad = norm_pull(normed_grad)
    input_flat = middle_grad_part + flat_back
    gain_one_sum, conv_w_sum, conv_b_sum, recur_b_sum, inlet_b_sum, decay_sum, gain_two_sum = (
        lax.psum(
            (
                gain_one_grad,
                conv_w_grad,
                conv_b_grad,
                recur_bias_grad,
                inlet_bias_grad,
                decay_grad,
                gain_two_grad,
            ),
            "dp",
        )
    )
    output = output_part.reshape(rows, length, width)
    input_grad = input_flat.reshape(rows, length, width)
    return (
        output,
        recur_final,
        conv_final,
        input_grad,
        gain_one_sum,
        recur_grads[0],
        recur_grads[1],
        conv_w_sum,
        conv_b_sum,
        recur_grads[2],
        recur_grads[3],
        recur_b_sum,
        inlet_b_sum,
        decay_sum,
        recur_grads[4],
        gain_two_sum,
        ffn_grads[0],
        ffn_grads[1],
        ffn_grads[2],
    )


def solution(mesh):
    in_specs = (
        P("dp", None, None),
        P(),
        P("dp", "tensor"),
        P("dp", "tensor"),
        P(None, "tensor"),
        P("tensor"),
        P("tensor", "dp"),
        P("tensor", "dp"),
        P("tensor"),
        P("tensor"),
        P("tensor"),
        P("tensor", "dp"),
        P(),
        P("dp", "tensor"),
        P("dp", "tensor"),
        P("tensor", "dp"),
        P("dp", None),
        P("dp", "tensor"),
        P("dp", None, "tensor"),
        P("dp", None, None),
    )
    out_specs = (
        P("dp", None, None),
        P("dp", "tensor"),
        P("dp", None, "tensor"),
        P("dp", None, None),
        P(),
        P("dp", "tensor"),
        P("dp", "tensor"),
        P(None, "tensor"),
        P("tensor"),
        P("tensor", "dp"),
        P("tensor", "dp"),
        P("tensor"),
        P("tensor"),
        P("tensor"),
        P("tensor", "dp"),
        P(),
        P("dp", "tensor"),
        P("dp", "tensor"),
        P("tensor", "dp"),
    )
    return jax.shard_map(
        per_device, mesh=mesh, in_specs=in_specs, out_specs=out_specs, check_vma=False
    )
```

profile of v0, /device:TPU:0, one launch (start us, length us, event | category | flops | bytes accessed | tf_op | source)
XLA Modules:
  0.0 2275.8 jit_solution(10320078940920256868)
XLA Ops:
  15.7 11.5 all-gather
  206.5 289.4 %all-reduce.113.cloned.1.call-done = f32[1024,2048]{1,0:T(8,128)} async-done(((f32[1024,2048]{1,0:T(8,128)}), f32[1024,2048]{1,0:T(8,128)}) %all-reduce.113.cloned.1.call-update) | async-done | bytes 8388624 | tf_op jit(solution)/shard_map/psum | solution.py:98
  512.1 30.1 %all-gather.15.cloned.1.call-done = bf16[2048,1536]{1,0:T(8,128)(2,1)} async-done(((bf16[256,1536]{1,0:T(8,128)(2,1)}), bf16[2048,1536]{1,0:T(8,128)(2,1)}) %all-gather.15.cloned.1.call-update) | async-done | bytes 6291472 | tf_op jit(solution)/shard_map/all_gather | solution.py:166
  542.1 11.9 fusion.124
  554.0 35.4 %all-gather.17.cloned.1.call-done = bf16[2048,1536]{1,0:T(8,128)(2,1)} async-done(((bf16[256,1536]{1,0:T(8,128)(2,1)}), bf16[2048,1536]{1,0:T(8,128)(2,1)}) %all-gather.17.cloned.1.call-update) | async-done | bytes 6291472 | tf_op jit(solution)/shard_map/all_gather | solution.py:167
  589.4 11.7 fusion.125
  601.1 36.8 %all-gather.19.cloned.1.call-done = bf16[1536,2048]{1,0:T(8,128)(2,1)} async-done(((bf16[1536,256]{1,0:T(8,128)(2,1)}), bf16[1536,2048]{1,0:T(8,128)(2,1)}) %all-gather.19.cloned.1.call-update) | async-done | bytes 6291472 | tf_op jit(solution)/shard_map/all_gather | solution.py:168
  638.0 19.7 multiply_convert_fusion.3
  667.7 10.5 convolution_add_fusion.1
  678.3 12.2 fusion.126
  690.5 278.8 %all-reduce.115.cloned.1.call-done = f32[1024,2048]{1,0:T(8,128)} async-done(((f32[1024,2048]{1,0:T(8,128)}), f32[1024,2048]{1,0:T(8,128)}) %all-reduce.115.cloned.1.call-update) | async-done | bytes 8388624 | tf_op jit(solution)/shard_map/psum | solution.py:98
  984.4 12.4 multiply_bitcast_fusion
  1220.3 12.6 fusion.132
  1233.1 12.6 fusion.133
  1245.8 13.4 fusion.116
  1279.9 518.0 %all-reduce.119.cloned.1.call-done = (f32[1024,2048]{1,0:T(8,128)}, f32[1024,2048]{1,0:T(8,128)}) async-done(((f32[1024,2048]{1,0:T(8,128)}, f32[1024,2048]{1,0:T(8,128)}), (f32[1024,2048]{1,0:T(8,128)}, f32[1024,2048]{1,0:T(8,128)})) %all-reduce.119.cloned.1.call-update) | async-done | bytes 16777232 | tf_op jit(solution)/shard_map/psum | solution.py:98
  1804.9 25.6 %all-reduce.105 = (f32[2048]{0:T(1024)}, f32[4,640]{1,0:T(4,128)}, f32[640]{0:T(1024)}, f32[640]{0:T(1024)}, f32[640]{0:T(1024)}, /*index=5*/f32[640]{0:T(1024)}, f32[2048]{0:T(1024)}) all-reduce(f32[2048]{0:T(1024)S(1)} %get-tuple-element.97, f32[4,640]{1,0:T(4,128)S(1)} %pad_add_fusion.11, ...), channel_id=1, replica_groups=mesh['dp'=8,'tensor'=4] {'dp'}, use_global_device_ids=true, to_apply=%region_11.12 | all-reduce | flops 9216 | bytes 73728 | tf_op jit(solution)/shard_map/psum | solution.py:249
  1830.4 12.1 add_bitcast_fusion
  1842.5 13.2 fusion.2
  1857.4 60.8 %reduce-scatter.11.cloned.1.call-done = f32[640,256]{1,0:T(8,128)} async-done(((f32[640,2048]{1,0:T(8,128)}), f32[640,256]{1,0:T(8,128)}) %reduce-scatter.11.cloned.1.call-update) | async-done | bytes 655376 | tf_op jit(solution)/shard_map/reduce_scatter | solution.py:241
  1918.2 60.5 %reduce-scatter.7.cloned.1.call-done = f32[256,640]{1,0:T(8,128)} async-done(((f32[2048,640]{1,0:T(8,128)}), f32[256,640]{1,0:T(8,128)}) %reduce-scatter.7.cloned.1.call-update) | async-done | bytes 655376 | tf_op jit(solution)/shard_map/reduce_scatter | solution.py:237
  1978.7 96.8 %reduce-scatter.13.cloned.1.call-done = f32[256,1536]{1,0:T(8,128)} async-done(((f32[2048,1536]{1,0:T(8,128)}), f32[256,1536]{1,0:T(8,128)}) %reduce-scatter.13.cloned.1.call-update) | async-done | bytes 1572880 | tf_op jit(solution)/shard_map/reduce_scatter | solution.py:204
  2075.5 96.7 %reduce-scatter.15.cloned.1.call-done = f32[256,1536]{1,0:T(8,128)} async-done(((f32[2048,1536]{1,0:T(8,128)}), f32[256,1536]{1,0:T(8,128)}) %reduce-scatter.15.cloned.1.call-update) | async-done | bytes 1572880 | tf_op jit(solution)/shard_map/reduce_scatter | solution.py:205
  2172.3 96.8 %reduce-scatter.17.cloned.1.call-done = f32[1536,256]{1,0:T(8,128)} async-done(((f32[1536,2048]{1,0:T(8,128)}), f32[1536,256]{1,0:T(8,128)}) %reduce-scatter.17.cloned.1.call-update) | async-done | bytes 1572880 | tf_op jit(solution)/shard_map/reduce_scatter | solution.py:206
  (750 shorter events, 478.1 us)
Async XLA Ops:
  7.2 37.0 %all-gather.9.cloned.1.call-start = ((), (), s32[]{:S(2)}) async-start(), calls=%async_computation.6 | async-start | bytes 2949120 | tf_op jit(solution)/shard_map/all_gather | solution.py:128
  7.9 177.2 %all-gather.11.cloned.1.call-start = ((), (), s32[]{:S(2)}) async-start(), calls=%async_computation.7 | async-start | bytes 2949120 | tf_op jit(solution)/shard_map/all_gather | solution.py:127
  8.7 186.8 %all-gather.13.cloned.1.call-start = ((), (), s32[]{:S(2)}) async-start(), calls=%async_computation.8 | async-start | bytes 2949120 | tf_op jit(solution)/shard_map/all_gather | solution.py:131
  9.4 486.4 %all-reduce.113.cloned.1.call-start = ((), (), s32[]{:S(2)}) async-start(), calls=%async_computation.9 | async-start | bytes 16777216 | tf_op jit(solution)/shard_map/psum | solution.py:98
  11.0 56.3 %copy-start.169 = (pred[1024]{0:T(1024)(128)(4,1)}, pred[1024]{0:T(1024)(128)(4,1)S(1)}, u32[]{:S(2)}) copy-start(pred[1024]{0:T(1024)(128)(4,1)S(1)} %compare_reduce_fusion) | copy-start | bytes 3076
  11.0 56.2 %copy-start.191 = (pred[1024]{0:T(1024)(128)(4,1)}, pred[1024]{0:T(1024)(128)(4,1)S(1)}, u32[]{:S(2)}) copy-start(pred[1024]{0:T(1024)(128)(4,1)S(1)} %iota_compare_fusion) | copy-start | bytes 3076
  15.2 35.6 %copy-start.171 = (pred[1024]{0:T(1024)(128)(4,1)}, pred[1024]{0:T(1024)(128)(4,1)S(1)}, u32[]{:S(2)}) copy-start(pred[1024]{0:T(1024)(128)(4,1)S(1)} %get-tuple-element.240) | copy-start | bytes 3076
  15.2 35.6 %copy-start.173 = (pred[1024]{0:T(1024)(128)(4,1)}, pred[1024]{0:T(1024)(128)(4,1)S(1)}, u32[]{:S(2)}) copy-start(pred[1024]{0:T(1024)(128)(4,1)S(1)} %get-tuple-element.237) | copy-start | bytes 3076
  15.2 35.6 %copy-start.175 = (pred[1024]{0:T(1024)(128)(4,1)}, pred[1024]{0:T(1024)(128)(4,1)S(1)}, u32[]{:S(2)}) copy-start(pred[1024]{0:T(1024)(128)(4,1)S(1)} %get-tuple-element.238) | copy-start | bytes 3076
  15.2 35.6 %copy-start.177 = (pred[1024]{0:T(1024)(128)(4,1)}, pred[1024]{0:T(1024)(128)(4,1)S(1)}, u32[]{:S(2)}) copy-start(pred[1024]{0:T(1024)(128)(4,1)S(1)} %get-tuple-element.239) | copy-start | bytes 3076
  15.3 35.5 %copy-start.154 = (f32[640]{0:T(1024)}, f32[640]{0:T(1024)S(1)}, u32[]{:S(2)}) copy-start(f32[640]{0:T(1024)S(1)} %get-tuple-element.105) | copy-start | bytes 7684
  204.5 337.6 %all-gather.15.cloned.1.call-start = ((), (), s32[]{:S(2)}) async-start(), calls=%async_computation.10 | async-start | bytes 7077888 | tf_op jit(solution)/shard_map/all_gather | solution.py:166
  205.1 384.3 %all-gather.17.cloned.1.call-start = ((), (), s32[]{:S(2)}) async-start(), calls=%async_computation.11 | async-start | bytes 7077888 | tf_op jit(solution)/shard_map/all_gather | solution.py:167
  205.7 432.3 %all-gather.19.cloned.1.call-start = ((), (), s32[]{:S(2)}) async-start(), calls=%async_computation.12 | async-start | bytes 7077888 | tf_op jit(solution)/shard_map/all_gather | solution.py:168
  206.4 299.6 %copy-start.134 = (f32[2048]{0:T(1024)S(1)}, f32[2048]{0:T(1024)}, u32[]{:S(2)}) copy-start(f32[2048]{0:T(1024)} %param.32) | copy-start | bytes 24580
  206.4 762.8 %all-reduce.115.cloned.1.call-start = ((), (), s32[]{:S(2)}) async-start(), calls=%async_computation.13 | async-start | bytes 16777216 | tf_op jit(solution)/shard_map/psum | solution.py:98
  678.3 600.0 %all-reduce.117.cloned.1.call-start = ((), (), s32[]{:S(2)}) async-start(), calls=%async_computation.20 | async-start | bytes 1638400
  1177.2 620.7 %all-reduce.119.cloned.1.call-start = ((), (), s32[]{:S(2)}) async-start(), calls=%async_computation.21 | async-start | bytes 33554432 | tf_op jit(solution)/shard_map/psum | solution.py:98
  1191.8 665.6 %reduce-scatter.9.cloned.1.call-start = ((), (), s32[]{:S(2)}) async-start(), calls=%async_computation.15 | async-start | bytes 5898240 | tf_op jit(solution)/shard_map/reduce_scatter | solution.py:238
  1202.2 716.0 %reduce-scatter.11.cloned.1.call-start = ((), (), s32[]{:S(2)}) async-start(), calls=%async_computation.16 | async-start | bytes 5898240 | tf_op jit(solution)/shard_map/reduce_scatter | solution.py:241
  1211.8 767.0 %reduce-scatter.7.cloned.1.call-start = ((), (), s32[]{:S(2)}) async-start(), calls=%async_computation.14 | async-start | bytes 5898240 | tf_op jit(solution)/shard_map/reduce_scatter | solution.py:237
  1220.2 855.3 %reduce-scatter.13.cloned.1.call-start = ((), (), s32[]{:S(2)}) async-start(), calls=%async_computation.17 | async-start | bytes 14155776 | tf_op jit(solution)/shard_map/reduce_scatter | solution.py:204
  1232.9 939.4 %reduce-scatter.15.cloned.1.call-start = ((), (), s32[]{:S(2)}) async-start(), calls=%async_computation.18 | async-start | bytes 14155776 | tf_op jit(solution)/shard_map/reduce_scatter | solution.py:205
  1245.8 1023.2 %reduce-scatter.17.cloned.1.call-start = ((), (), s32[]{:S(2)}) async-start(), calls=%async_computation.19 | async-start | bytes 14155776 | tf_op jit(solution)/shard_map/reduce_scatter | solution.py:206
  (193 other events, 1545.4 us)
Sparse Core Ops, SparseCore 0:
  9.9 33.9 all-gather.8
  45.7 30.1 all-gather.10
  77.8 30.5 all-gather.12
  204.6 291.1 all-reduce.112
  497.5 44.5 all-gather.14
  543.9 45.5 all-gather.16
  591.3 46.6 all-gather.18
  678.4 290.8 all-reduce.114
  1177.3 54.7 all-reduce.116
  1235.2 562.5 all-reduce.118
  1801.8 55.5 reduce-scatter.8
  1861.6 56.5 reduce-scatter.10
  1922.2 56.5 reduce-scatter.6
  1983.1 92.3 reduce-scatter.12
  2079.8 92.3 reduce-scatter.14
  2176.6 92.3 reduce-scatter.16
where the time goes:
time: 2280 us
  waiting for transfers between devices  1610 us (71%)
  local copies, waits for them, and re-layouts  232 us (10%)
  matrix products  206 us (9%)
  other arithmetic  166 us (7%)
  blocking collectives  46.7 us (2%)
    psum x3, waiting for transfers between devices, tensor_reduce(): return lax.psum(partial_sum, 'tensor')  1090 us
    pad x79, local copies, waits for them, and re-layouts, recurrence(): _, states = lax.associative_scan(combine, (carries, drive), axis=0)  98.6 us
    reduce_scatter x1, waiting for transfers between devices, per_device(): lax.psum_scatter(gate_w_grad, 'dp', scatter_dimension=0, tiled=True)  96.8 us
    reduce_scatter x1, waiting for transfers between devices, per_device(): lax.psum_scatter(down_grad, 'dp', scatter_dimension=1, tiled=True)  96.8 us
    reduce_scatter x1, waiting for transfers between devices, per_device(): lax.psum_scatter(value_w_grad, 'dp', scatter_dimension=0, tiled=True)  96.7 us
    slice x78, local copies, waits for them, and re-layouts, recurrence(): _, states = lax.associative_scan(combine, (carries, drive), axis=0)  91.7 us
    dot_general x6, matrix products, contract_rows(): lax.dot_general(left, right, (((0,), (0,)), ((), ())), preferred_element_...  65.8 us
    dot_general x6, matrix products, contract_cols(): lax.dot_general(left, right, (((1,), (1,)), ((), ())), preferred_element_...  61.8 us
  transfers between devices with their start and end apart: 16, of which 12 were waited for; matrix products, arithmetic and copies ran while one was open for 15% of the time, Pallas kernels for 0%

commit v1 on v0

--- a/solution.py
+++ b/solution.py
@@ -1,6 +1,10 @@
+import functools
+
 import jax
 import jax.numpy as jnp
 from jax import lax
+from jax.experimental import pallas as pl
+from jax.experimental.pallas import tpu as pltpu
 from jax.sharding import PartitionSpec as P
 
 EPS = 1e-06
@@ -284,6 +288,1108 @@
     )
 
 
+BF = jnp.bfloat16
+F32 = jnp.float32
+HEAD = 160
+CHUNK = 256
+SMALL = 128
+FTILE = 512
+MIB = 1024 * 1024
+GELU_C = 0.7978845608028654
+GELU_K = 0.044715
+
+PART, INWARD, SUM, ACROSS, OWN, OUTWARD, GAIN = range(7)
+ACTS, NORMED, FIRST, INV, WEIGHTS, MID, BACK, OUTPUT, INPUT = range(7, 16)
+UNIT_GRAD, UNIT_RESULT, PRE_GRAD, GATES_GRAD, CHANNEL_SUMS, PACKED = range(16, 22)
+SMALL_SUMS, GAIN_SUMS, GAIN_ONE, FORWARD, CARRIED = range(22, 27)
+TO_NORM, TO_MIDDLE, TO_OUTPUT, TO_INPUT = range(4)
+
+
+def hbm(value):
+    return pltpu.with_memory_space_constraint(value, pltpu.HBM)
+
+
+def params(megabytes):
+    return pltpu.CompilerParams(vmem_limit_bytes=megabytes * MIB)
+
+
+def nt_dot(left, right):
+    return lax.dot_general(left, right, (((1,), (1,)), ((), ())), preferred_element_type=F32)
+
+
+def nn_dot(left, right):
+    return jnp.dot(left, right, preferred_element_type=F32)
+
+
+def gelu_parts(value):
+    square = value * value
+    tanh = jnp.tanh(GELU_C * value * (1.0 + GELU_K * square))
+    half = 0.5 * (1.0 + tanh)
+    slope = half + 0.5 * value * (1.0 - tanh * tanh) * GELU_C * (1.0 + 3.0 * GELU_K * square)
+    return value * half, slope
+
+
+def document_begin(place, starts_ref, segs):
+    begin = jnp.full(place.shape, -3, jnp.int32)
+    for seg in range(segs):
+        start = starts_ref[0, seg]
+        begin = jnp.where(start <= place, jnp.maximum(begin, start), begin)
+    return begin
+
+
+def at_reset(place, starts_ref, segs):
+    reset = place == starts_ref[0, 0]
+    for seg in range(1, segs):
+        reset = reset | (place == starts_ref[0, seg])
+    return reset
+
+
+def iota_rows(rows, offset):
+    return lax.broadcasted_iota(jnp.int32, (rows, 1), 0) + offset
+
+
+def forward_kernel(segs, first, assemble, starts_ref, *refs):
+    if assemble:
+        me_ref, pieces, refs = refs[0], refs[1:5], refs[5:]
+        normed_ref, heads_ref, vec_ref, before_ref = refs[:4]
+        outs, (ext, held, weight, in_sem, out_sem) = refs[-14:-5], refs[-5:]
+        weight_out, outs = outs[0], outs[1:]
+    else:
+        normed_ref, heads_ref, vec_ref, before_ref, weight = refs[:5]
+        outs, (ext, held) = refs[-10:-2], refs[-2:]
+    gate_ref, branch_ref, mixed_ref, states_ref, rate_ref, inlet_ref, product_ref, tail_ref = outs
+    block = pl.program_id(0) + first
+    rows, channels = gate_ref.shape
+
+    if assemble:
+        share = weight.shape[0] // 8
+        keep = pltpu.make_async_copy(weight, weight_out, out_sem)
+
+        @pl.when(pl.program_id(0) == 0)
+        def _():
+            copies = []
+            for which, piece in enumerate(pieces):
+                for index in range(4):
+                    owner = me_ref[0] ^ (2 * index + which // 2)
+                    copies.append(
+                        pltpu.make_async_copy(
+                            piece.at[index],
+                            weight.at[
+                                pl.ds(pl.multiple_of(owner * share, share), share),
+                                pl.ds((which % 2) * channels, channels),
+                            ],
+                            in_sem.at[which * 4 + index],
+                        )
+                    )
+            for copy in copies:
+                copy.start()
+            for copy in copies:
+                copy.wait()
+            keep.start()
+
+    @pl.when(pl.program_id(0) == 0)
+    def _():
+        ext[0:8] = before_ref[0:8]
+        held[...] = jnp.broadcast_to(before_ref[8:9], (8, channels))
+
+    pre = nn_dot(normed_ref[...], weight[...])
+    gate = pre[:, :channels]
+    gate_ref[...] = gate
+    branch = pre[:, channels:]
+    branch_ref[...] = branch
+    ext[8:] = branch
+    place = iota_rows(rows, block * rows)
+    begin = document_begin(place, starts_ref, segs)
+    reset = at_reset(place, starts_ref, segs)
+    total = jnp.broadcast_to(vec_ref[4:5], (rows, channels))
+    for lag in range(4):
+        usable = place - lag >= begin
+        total = total + vec_ref[lag : lag + 1] * jnp.where(usable, ext[8 - lag : 8 - lag + rows], 0.0)
+    mixed = total.astype(BF)
+    mixed_ref[...] = mixed
+    pres = nt_dot(mixed, heads_ref[...])
+    rate = jax.nn.sigmoid(pres[:, :channels] + vec_ref[5:6])
+    inlet = jax.nn.sigmoid(pres[:, channels:] + vec_ref[6:7])
+    rate_ref[...] = rate
+    inlet_ref[...] = inlet
+    factor = jnp.exp(-vec_ref[7:8] * rate)
+    scale = jnp.sqrt(jnp.maximum(1.0 - factor * factor, 0.001))
+    scale = jnp.where(reset, 1.0, scale)
+    carry = jnp.where(reset, 0.0, factor)
+    drive = scale * inlet * mixed.astype(F32)
+    row8 = lax.broadcasted_iota(jnp.int32, (8, 1), 0)
+    last = held[0:1]
+    for group in range(rows // 8):
+        span = slice(group * 8, group * 8 + 8)
+        coef, value = carry[span], drive[span]
+        for shift in (1, 2, 4):
+            inside = row8 >= shift
+            coef_prev = pltpu.roll(coef, shift, 0)
+            value_prev = pltpu.roll(value, shift, 0)
+            value = jnp.where(inside, coef * value_prev + value, value)
+            coef = jnp.where(inside, coef * coef_prev, coef)
+        state = coef * last + value
+        states_ref[span] = state
+        last = state[7:8]
+    held[...] = jnp.broadcast_to(last, (8, channels))
+    act, _ = gelu_parts(gate)
+    product_ref[...] = (states_ref[...] * act).astype(BF)
+    ext[0:8] = ext[rows : rows + 8]
+
+    @pl.when(pl.program_id(0) == pl.num_programs(0) - 1)
+    def _():
+        tail_ref[0:8] = ext[0:8]
+        tail_ref[8:16] = held[...]
+        if assemble:
+            keep.wait()
+
+
+def run_forward(starts, normed, heads, vec, before, weight, first, steps, kept=(), me=None):
+    tokens, width = normed.shape
+    channels = before.shape[1]
+    assemble = me is not None
+    by_rows = lambda i: (i + first, 0)
+    whole = lambda i: (0, 0)
+    anywhere = pl.BlockSpec(memory_space=pl.ANY)
+    smem = pl.BlockSpec(memory_space=pltpu.SMEM)
+    spec = pl.BlockSpec((SMALL, channels), by_rows)
+    full = lambda dtype: pltpu.HBM((tokens, channels), dtype)
+    main = [hbm(normed), hbm(heads), vec, before]
+    main_specs = [
+        pl.BlockSpec((SMALL, width), by_rows),
+        pl.BlockSpec(heads.shape, whole),
+        pl.BlockSpec(vec.shape, whole),
+        pl.BlockSpec(before.shape, whole),
+    ]
+    out_specs = [spec] * 7 + [pl.BlockSpec((16, channels), whole)]
+    out_shape = [full(F32), full(F32), full(BF), full(F32), full(F32), full(F32), full(BF)]
+    out_shape.append(jax.ShapeDtypeStruct((16, channels), F32))
+    scratch = [pltpu.VMEM((SMALL + 8, channels), F32), pltpu.VMEM((8, channels), F32)]
+    if assemble:
+        args = [starts, me, *weight, *main]
+        in_specs = [smem, smem] + [anywhere] * 4 + main_specs
+        out_specs = [anywhere] + out_specs
+        out_shape = [pltpu.HBM((width, 2 * channels), BF)] + out_shape
+        scratch += [
+            pltpu.VMEM((width, 2 * channels), BF),
+            pltpu.SemaphoreType.DMA((16,)),
+            pltpu.SemaphoreType.DMA,
+        ]
+    else:
+        args = [starts, *main, hbm(weight)]
+        in_specs = [smem] + main_specs + [pl.BlockSpec(weight.shape, whole)]
+    aliases = {}
+    for index, item in enumerate(kept):
+        aliases[len(args)] = index
+        in_specs.append(anywhere)
+        args.append(hbm(item))
+    return pl.pallas_call(
+        functools.partial(forward_kernel, starts.shape[1], first, assemble),
+        grid=(steps,),
+        in_specs=in_specs,
+        out_specs=out_specs,
+        out_shape=out_shape,
+        input_output_aliases=aliases,
+        scratch_shapes=scratch,
+        compiler_params=params(32),
+        cost_estimate=pl.CostEstimate(
+            flops=4 * steps * SMALL * channels * (width + channels),
+            bytes_accessed=30 * steps * SMALL * channels,
+            transcendentals=6 * steps * SMALL * channels,
+        ),
+        name="recurrent_forward",
+    )(*args)
+
+
+def backward_kernel(
+    segs,
+    first,
+    count,
+    starts_ref,
+    grad_ref,
+    outw_ref,
+    gate_ref,
+    branch_ref,
+    mixed_ref,
+    states_ref,
+    before_ref,
+    rate_ref,
+    inlet_ref,
+    heads_ref,
+    vec_ref,
+    hist_ref,
+    carried_ref,
+    *refs,
+):
+    pre_grad_ref, gates_grad_ref, carried_out = refs[-8:-5]
+    carry_ext, mixed_ext, state_ext, lam_rows, held = refs[-5:]
+    sums_ref = carried_out.at[24:32]
+    step = pl.program_id(0)
+    block = first + count - 1 - step
+    rows, channels = gate_ref.shape
+
+    @pl.when(step == 0)
+    def _():
+        held[...] = carried_ref[0:16]
+        mixed_ext[8 + rows :] = carried_ref[16:24]
+        sums_ref[...] = carried_ref[24:32]
+
+    place = iota_rows(rows, block * rows)
+    reset = at_reset(place, starts_ref, segs)
+    product_grad = nn_dot(grad_ref[...], outw_ref[...])
+    act, slope = gelu_parts(gate_ref[...])
+    states = states_ref[...]
+    pre_grad_ref[:, :channels] = (product_grad * states * slope).astype(BF)
+    state_grad = product_grad * act
+    rate, inlet = rate_ref[...], inlet_ref[...]
+    decay = vec_ref[7:8]
+    factor = jnp.exp(-decay * rate)
+    room = 1.0 - factor * factor
+    bare_scale = jnp.sqrt(jnp.maximum(room, 0.001))
+    scale = jnp.where(reset, 1.0, bare_scale)
+    carry = jnp.where(reset, 0.0, factor)
+    state_ext[8:] = states
+    state_ext[7:8] = jnp.where(block == 0, vec_ref[8:9], before_ref[7:8])
+    prev_states = state_ext[7 : 7 + rows]
+    carry_ext[0:rows] = carry
+    carry_ext[rows : rows + 1] = held[8:9]
+    later_carry = carry_ext[1 : rows + 1]
+    row8 = lax.broadcasted_iota(jnp.int32, (8, 1), 0)
+    after = held[0:1]
+    for group in reversed(range(rows // 8)):
+        span = slice(group * 8, group * 8 + 8)
+        coef, value = later_carry[span], state_grad[span]
+        for shift in (1, 2, 4):
+            inside = row8 < 8 - shift
+            coef_next = pltpu.roll(coef, 8 - shift, 0)
+            value_next = pltpu.roll(value, 8 - shift, 0)
+            value = jnp.where(inside, coef * value_next + value, value)
+            coef = jnp.where(inside, coef * coef_next, coef)
+        lam = coef * after + value
+        lam_rows[span] = lam
+        after = lam[0:1]
+    held[0:1] = after
+    held[8:9] = carry[0:1]
+    lam = lam_rows[...]
+    mixed = mixed_ref[...].astype(F32)
+    scale_grad = lam * inlet * mixed
+    scale_part = jnp.where(room > 0.001, scale_grad * factor * factor / bare_scale, 0.0)
+    log_grad = jnp.where(reset, 0.0, lam * prev_states * factor - scale_part)
+    inlet_pre_grad = lam * scale * mixed * inlet * (1.0 - inlet)
+    recur_pre_grad = -decay * log_grad * rate * (1.0 - rate)
+    gates_grad_ref[:, :channels] = recur_pre_grad.astype(BF)
+    gates_grad_ref[:, channels:] = inlet_pre_grad.astype(BF)
+    mixed_grad = lam * scale * inlet + nn_dot(gates_grad_ref[...], heads_ref[...])
+    mixed_ext[8 : 8 + rows] = mixed_grad
+    branch = branch_ref[...]
+    branch_grad = jnp.zeros((rows, channels), F32)
+    tap_sums = []
+    for lag in range(4):
+        live = place >= document_begin(place + lag, starts_ref, segs)
+        part = jnp.where(live, mixed_ext[8 + lag : 8 + lag + rows], 0.0)
+        branch_grad = branch_grad + vec_ref[lag : lag + 1] * part
+        tap_sums.append(jnp.sum(branch * part, axis=0, keepdims=True))
+    pre_grad_ref[:, channels:] = branch_grad.astype(BF)
+    others = [mixed_grad, recur_pre_grad, inlet_pre_grad, -rate * log_grad]
+    tap_sums += [jnp.sum(item, axis=0, keepdims=True) for item in others]
+    for index, item in enumerate(tap_sums):
+        sums_ref[index : index + 1] += item
+
+    @pl.when(block == 0)
+    def _():
+        mixed_ext[0:8] = jnp.zeros((8, channels), F32)
+        early = iota_rows(8, -8)
+        for lag in range(4):
+            live = early >= document_begin(early + lag, starts_ref, segs)
+            part = jnp.where(live, mixed_ext[lag : lag + 8], 0.0)
+            sums_ref[lag : lag + 1] += jnp.sum(hist_ref[...] * part, axis=0, keepdims=True)
+
+    mixed_ext[8 + rows :] = mixed_grad[0:8]
+
+    @pl.when(step == count - 1)
+    def _():
+        carried_out[0:16] = held[...]
+        carried_out[16:24] = mixed_grad[0:8]
+
+
+def run_backward(
+    starts, grad, outw, saved, heads, vec, hist, carried, first, count, kept=()
+):
+    tokens, width = grad.shape
+    channels = hist.shape[1]
+    by_rows = lambda i: (first + count - 1 - i, 0)
+    before = lambda i: (jnp.maximum((first + count - 1 - i) * (SMALL // 8) - 1, 0), 0)
+    whole = lambda i: (0, 0)
+    spec = pl.BlockSpec((SMALL, channels), by_rows)
+    wide = pl.BlockSpec((SMALL, 2 * channels), by_rows)
+    gate, branch, mixed, states, rate, inlet = [hbm(item) for item in saved]
+    args = [starts, hbm(grad), hbm(outw), gate, branch, mixed, states, states, rate, inlet]
+    args += [hbm(heads), vec, hist, carried]
+    in_specs = [
+        pl.BlockSpec(memory_space=pltpu.SMEM),
+        pl.BlockSpec((SMALL, width), by_rows),
+        pl.BlockSpec(outw.shape, whole),
+        spec,
+        spec,
+        spec,
+        spec,
+        pl.BlockSpec((8, channels), before),
+        spec,
+        spec,
+        pl.BlockSpec(heads.shape, whole),
+        pl.BlockSpec(vec.shape, whole),
+        pl.BlockSpec(hist.shape, whole),
+        pl.BlockSpec(carried.shape, whole),
+    ]
+    aliases = {}
+    for index, item in enumerate(kept):
+        aliases[len(args)] = index
+        in_specs.append(pl.BlockSpec(memory_space=pl.ANY))
+        args.append(hbm(item))
+    return pl.pallas_call(
+        functools.partial(backward_kernel, starts.shape[1], first, count),
+        grid=(count,),
+        in_specs=in_specs,
+        out_specs=[wide, wide, pl.BlockSpec(carried.shape, whole)],
+        out_shape=[
+            pltpu.HBM((tokens, 2 * channels), BF),
+            pltpu.HBM((tokens, 2 * channels), BF),
+            jax.ShapeDtypeStruct(carried.shape, F32),
+        ],
+        input_output_aliases=aliases,
+        scratch_shapes=[
+            pltpu.VMEM((SMALL + 8, channels), F32),
+            pltpu.VMEM((SMALL + 16, channels), F32),
+            pltpu.VMEM((SMALL + 8, channels), F32),
+            pltpu.VMEM((SMALL, channels), F32),
+            pltpu.VMEM((16, channels), F32),
+        ],
+        compiler_params=params(32),
+        cost_estimate=pl.CostEstimate(
+            flops=2 * count * SMALL * channels * (width + 2 * channels),
+            bytes_accessed=34 * count * SMALL * channels,
+            transcendentals=6 * count * SMALL * channels,
+        ),
+        name="recurrent_backward",
+    )(*args)
+
+
+def ffn_kernel(part, units, zed_ref, own, came, act_ref, gain_ref, cot_ref, weight_ref, *refs):
+    outs, (weight, normed, acts, in_sem, out_sem) = refs[-10:-5], refs[-5:]
+    acts_out, normed_out, first_out, inv_out, back_out = outs
+    rows, width = own.shape
+    tiles = units // FTILE
+    spans = [
+        [slice(k * units + t * FTILE, k * units + (t + 1) * FTILE) for k in range(3)]
+        for t in range(tiles)
+    ]
+    copies = [
+        [
+            pltpu.make_async_copy(
+                weight_ref.at[:, pl.ds(span.start, FTILE)],
+                weight.at[:, pl.ds(span.start, FTILE)],
+                in_sem.at[3 * t + k],
+            )
+            for k, span in enumerate(spans[t])
+        ]
+        for t in range(tiles)
+    ]
+    for copy in sum(copies, []):
+        copy.start()
+    first = pick(zed_ref, own, came)
+    first_out[...] = first.astype(BF)
+    middle = act_ref[...] + first
+    mean = jnp.sum(middle * middle, axis=1, keepdims=True) / width
+    inv = lax.rsqrt(mean + EPS)
+    inv_out[...] = jnp.broadcast_to(inv, inv_out.shape)
+    normed[...] = (middle * inv * gain_ref[1:2]).astype(BF)
+    out_rows = pl.ds(part * rows, rows)
+    keep = [
+        pltpu.make_async_copy(normed, normed_out.at[out_rows], out_sem.at[0]),
+        pltpu.make_async_copy(acts, acts_out.at[out_rows], out_sem.at[1]),
+    ]
+    keep[0].start()
+    for t in range(tiles):
+        for copy in copies[t]:
+            copy.wait()
+        one, two, three = spans[t]
+        gate = nn_dot(normed[...], weight[:, one])
+        value = nn_dot(normed[...], weight[:, two])
+        inner_grad = nn_dot(cot_ref[...], weight[:, three])
+        act, slope = gelu_parts(gate)
+        acts[:, one] = (inner_grad * value * slope).astype(BF)
+        acts[:, two] = (inner_grad * act).astype(BF)
+        acts[:, three] = (act * value).astype(BF)
+    keep[1].start()
+    for n in range(width // FTILE):
+        span = slice(n * FTILE, (n + 1) * FTILE)
+        back_out[:, span] = nt_dot(acts[:, : 2 * units], weight[span, : 2 * units]).astype(BF)
+    for copy in keep:
+        copy.wait()
+
+
+def run_ffn(part, zed, own, came, flat, gains, cot, weights, kept):
+    tokens, width = cot.shape
+    units = weights.shape[1] // 3
+    rows = own.shape[0]
+    tiles = units // FTILE
+    anywhere = pl.BlockSpec(memory_space=pl.ANY)
+    whole = lambda i: (0, 0)
+    held = lambda i: (part, 0)
+    in_specs = [
+        pl.BlockSpec(memory_space=pltpu.SMEM),
+        pl.BlockSpec(own.shape, whole),
+        pl.BlockSpec(own.shape, whole),
+        pl.BlockSpec((rows, width), held),
+        pl.BlockSpec(gains.shape, whole),
+        pl.BlockSpec((rows, width), held),
+        anywhere,
+    ]
+    args = [zed, own, came, hbm(flat), gains, hbm(cot), hbm(weights)]
+    aliases = {}
+    for index, item in enumerate(kept):
+        aliases[len(args)] = index
+        in_specs.append(anywhere)
+        args.append(hbm(item))
+    return pl.pallas_call(
+        functools.partial(ffn_kernel, part, units),
+        grid=(1,),
+        in_specs=in_specs,
+        out_specs=[
+            anywhere,
+            anywhere,
+            pl.BlockSpec((rows, width), held),
+            pl.BlockSpec((rows, 128), held),
+            pl.BlockSpec((rows, width), whole),
+        ],
+        out_shape=[
+            pltpu.HBM((tokens, 3 * units), BF),
+            pltpu.HBM((tokens, width), BF),
+            pltpu.HBM((tokens, width), BF),
+            pltpu.HBM((tokens, 128), F32),
+            jax.ShapeDtypeStruct((rows, width), BF),
+        ],
+        input_output_aliases=aliases,
+        scratch_shapes=[
+            pltpu.VMEM(weights.shape, BF),
+            pltpu.VMEM((rows, width), BF),
+            pltpu.VMEM((rows, 3 * units), BF),
+            pltpu.SemaphoreType.DMA((3 * tiles,)),
+            pltpu.SemaphoreType.DMA((2,)),
+        ],
+        compiler_params=params(46),
+        cost_estimate=pl.CostEstimate(
+            flops=10 * rows * width * units,
+            bytes_accessed=2 * weights.size,
+            transcendentals=rows * units,
+        ),
+        name="ffn_chunk",
+    )(*args)
+
+
+def nt_kernel(left, right, *outs):
+    total = nt_dot(left[...], right[...])
+    rows = outs[0].shape[0]
+    for index, out in enumerate(outs):
+        out[...] = total[index * rows : (index + 1) * rows].astype(out.dtype)
+
+
+def run_nt(left, first, pieces, left_col, right, right_col, depth):
+    width = right.shape[0]
+    rows = pieces * CHUNK
+    tile = 1024 if pieces == 1 else 512
+    return pl.pallas_call(
+        nt_kernel,
+        grid=(width // tile,),
+        in_specs=[
+            pl.BlockSpec((pl.Element(rows), pl.Element(depth)), lambda i: (first, left_col * depth)),
+            pl.BlockSpec((tile, depth), lambda i: (i, right_col)),
+        ],
+        out_specs=[pl.BlockSpec((CHUNK, tile), lambda i: (0, i))] * pieces,
+        out_shape=[jax.ShapeDtypeStruct((CHUNK, width), BF)] * pieces,
+        compiler_params=params(32),
+        cost_estimate=pl.CostEstimate(
+            flops=2 * rows * width * depth, bytes_accessed=4 * width * depth, transcendentals=0
+        ),
+        name="rows_by_rows",
+    )(hbm(left), hbm(right))
+
+
+def tn_kernel(left, right, *refs):
+    refs[-1][...] = contract_rows(left[...], right[...]).astype(BF)
+
+
+def run_weight_grad(left, right, column, tiles, kept, total):
+    tokens, width = left.shape
+    in_specs = [
+        pl.BlockSpec((tokens, width), lambda j: (0, 0)),
+        pl.BlockSpec((tokens, FTILE), lambda j: (0, column + j)),
+    ]
+    args = [hbm(left), hbm(right)]
+    if kept is not None:
+        in_specs.append(pl.BlockSpec(memory_space=pl.ANY))
+        args.append(hbm(kept))
+    return pl.pallas_call(
+        tn_kernel,
+        grid=(tiles,),
+        in_specs=in_specs,
+        out_specs=pl.BlockSpec((width, FTILE), lambda j: (0, column + j)),
+        out_shape=pltpu.HBM((width, total), BF),
+        input_output_aliases={} if kept is None else {2: 0},
+        compiler_params=params(36),
+        cost_estimate=pl.CostEstimate(
+            flops=2 * tokens * width * tiles * FTILE,
+            bytes_accessed=2 * tokens * (width + tiles * FTILE) + 2 * width * tiles * FTILE,
+            transcendentals=0,
+        ),
+        name="unit_weight_grad",
+    )(*args)
+
+
+def packed_kernel(left, right, *refs):
+    total = contract_rows(left[...], right[...]).astype(BF)
+    out = refs[-1]
+    rows, channels = total.shape[0], out.shape[2]
+    for index in range(right.shape[1] // channels):
+        span = slice(index * channels, (index + 1) * channels)
+        out[0, index * rows : (index + 1) * rows] = total[:, span]
+
+
+def run_packed_grad(left, right, place, kept, shape):
+    tokens, width = left.shape
+    share = width // 8
+    tall = share * (right.shape[1] // shape[2])
+    in_specs = [
+        pl.BlockSpec((tokens, share), lambda d: (0, d)),
+        pl.BlockSpec(right.shape, lambda d: (0, 0)),
+    ]
+    args = [hbm(left), hbm(right)]
+    if kept is not None:
+        in_specs.append(pl.BlockSpec(memory_space=pl.ANY))
+        args.append(hbm(kept))
+    return pl.pallas_call(
+        packed_kernel,
+        grid=(8,),
+        in_specs=in_specs,
+        out_specs=pl.BlockSpec((1, tall, shape[2]), lambda d: (d, place, 0)),
+        out_shape=pltpu.HBM(shape, BF),
+        input_output_aliases={} if kept is None else {2: 0},
+        compiler_params=params(32),
+        cost_estimate=pl.CostEstimate(
+            flops=2 * tokens * width * right.shape[1],
+            bytes_accessed=2 * (tokens + right.shape[1]) * width,
+            transcendentals=0,
+        ),
+        name="branch_weight_grad",
+    )(*args)
+
+
+def thin_kernel(grads, mixed, kept, out, total):
+    which = pl.program_id(0)
+    channels = mixed.shape[1]
+    product = contract_rows(grads[...], mixed[...])
+    owner = lax.broadcasted_iota(jnp.int32, (1, channels), 1) // HEAD
+    own = jnp.zeros((HEAD, channels), F32)
+    for head in range(channels // HEAD):
+        rows = product[head * HEAD : (head + 1) * HEAD]
+        own = jnp.where(owner == head, rows, own)
+    total[which] = own
+
+    @pl.when(which == 1)
+    def _():
+        slim = HEAD // 8
+        for share in range(8):
+            rows = slice(share * slim, (share + 1) * slim)
+            parts = [total[0, rows], total[1, rows], jnp.zeros((8, channels), F32)]
+            out[share] = jnp.concatenate(parts, 0).astype(BF)
+
+
+def run_thin_grad(grads, mixed, packed):
+    tokens, channels = mixed.shape
+    place = packed.shape[1] // 48 - 1
+    return pl.pallas_call(
+        thin_kernel,
+        grid=(2,),
+        in_specs=[
+            pl.BlockSpec((tokens, channels), lambda i: (0, i)),
+            pl.BlockSpec((tokens, channels), lambda i: (0, 0)),
+            pl.BlockSpec(memory_space=pl.ANY),
+        ],
+        out_specs=pl.BlockSpec((8, 48, channels), lambda i: (0, place, 0)),
+        out_shape=pltpu.HBM(packed.shape, BF),
+        scratch_shapes=[pltpu.VMEM((2, HEAD, channels), F32)],
+        input_output_aliases={2: 0},
+        compiler_params=params(32),
+        cost_estimate=pl.CostEstimate(
+            flops=4 * tokens * channels * channels,
+            bytes_accessed=8 * tokens * channels,
+            transcendentals=0,
+        ),
+        name="gate_weight_grad",
+    )(hbm(grads), hbm(mixed), hbm(packed))
+
+
+def pick(zed_ref, own, came):
+    inner = (zed_ref[0] == 1) | (zed_ref[0] == 2)
+    return jnp.where(inner, own[...].astype(F32), came[...].astype(F32))
+
+
+def norm_back(grad, normed, inv, gains, which):
+    dot = jnp.sum(normed * grad, axis=1, keepdims=True) / normed.shape[1]
+    return inv * (grad * gains[which : which + 1] - normed * gains[which + 2 : which + 3] * dot)
+
+
+def middle_kernel(zed_ref, own, came, normed_ref, inv, gains, cot, *refs):
+    grad_out, back_out, gain_out = refs[-3:]
+    total = pick(zed_ref, own, came)
+    normed = normed_ref[...].astype(F32)
+    back = norm_back(total, normed, inv[:, 0:1], gains, 1)
+    back_out[...] = back.astype(BF)
+    grad_out[...] = (cot[...] + back).astype(BF)
+
+    @pl.when(pl.program_id(0) == 0)
+    def _():
+        gain_out[...] = jnp.zeros(gain_out.shape, F32)
+
+    gain_out[0:1] += jnp.sum(total * normed, axis=0, keepdims=True)
+
+
+def output_kernel(zed_ref, own, came, first, act, *refs):
+    refs[-1][...] = act[...] + (first[...].astype(F32) + pick(zed_ref, own, came))
+
+
+def input_kernel(zed_ref, own, came, normed, inv, gains, back, cot, *refs):
+    total = pick(zed_ref, own, came)
+    through = norm_back(total, normed[...].astype(F32), inv[:, 0:1], gains, 0)
+    refs[-1][...] = cot[...] + (back[...].astype(F32) + through)
+
+
+def run_rows(body, name, zed, own, came, others, first, outs, kept):
+    rows, width = own.shape
+    step = 64
+    by_rows = lambda i: (i + first // step, 0)
+    whole = lambda i: (0, 0)
+
+    def spec(shape):
+        if shape[0] == 8:
+            return pl.BlockSpec(shape, whole)
+        return pl.BlockSpec((step, shape[1]), by_rows)
+
+    part = pl.BlockSpec((step, width), lambda i: (i, 0))
+    in_specs = [pl.BlockSpec(memory_space=pltpu.SMEM), part, part]
+    in_specs += [spec(item.shape) for item in others]
+    args = [zed, own, came]
+    args += [item if item.shape[0] == 8 else hbm(item) for item in others]
+    aliases = {}
+    for index, item in enumerate(kept):
+        aliases[len(args)] = index
+        in_specs.append(pl.BlockSpec(memory_space=pl.ANY))
+        args.append(hbm(item))
+    return pl.pallas_call(
+        body,
+        grid=(rows // step,),
+        in_specs=in_specs,
+        out_specs=[spec(item.shape) for item in outs],
+        out_shape=outs,
+        input_output_aliases=aliases,
+        compiler_params=params(24),
+        cost_estimate=pl.CostEstimate(
+            flops=20 * rows * width, bytes_accessed=20 * rows * width, transcendentals=0
+        ),
+        name=name,
+    )(*args)
+
+
+def swap_dp(value, bit):
+    return lax.ppermute(value, "dp", [(i, i ^ bit) for i in range(8)])
+
+
+def gather_pair(one, two):
+    one2, two4 = swap_dp(one, 2), swap_dp(two, 4)
+    one4, one6 = swap_dp(one, 4), swap_dp(one2, 4)
+    two2, two6 = swap_dp(two, 2), swap_dp(two4, 2)
+    return jnp.stack([one, one2, one4, one6]), jnp.stack([two, two2, two4, two6])
+
+
+def natural_kernel(me_ref, *refs):
+    pieces, (out_ref, sem) = refs[:4], refs[4:]
+    half = pieces[0].shape[1]
+    copies = []
+    for which, piece in enumerate(pieces):
+        for index in range(4):
+            owner = me_ref[0] ^ (2 * index + which // 2)
+            start = pl.multiple_of(owner * 2 * half + (which % 2) * half, half)
+            copies.append(
+                pltpu.make_async_copy(
+                    piece.at[index], out_ref.at[pl.ds(start, half)], sem.at[which * 4 + index]
+                )
+            )
+    for copy in copies:
+        copy.start()
+    for copy in copies:
+        copy.wait()
+
+
+def natural_order(pieces, me):
+    _, rows, columns = pieces[0].shape
+    anywhere = pl.BlockSpec(memory_space=pl.ANY)
+    return pl.pallas_call(
+        natural_kernel,
+        in_specs=[pl.BlockSpec(memory_space=pltpu.SMEM)] + [anywhere] * 4,
+        out_specs=pl.BlockSpec(memory_space=pltpu.VMEM),
+        out_shape=jax.ShapeDtypeStruct((16 * rows, columns), pieces[0].dtype),
+        scratch_shapes=[pltpu.SemaphoreType.DMA((16,))],
+        compiler_params=params(16),
+        cost_estimate=pl.CostEstimate(
+            flops=0, bytes_accessed=64 * rows * columns, transcendentals=0
+        ),
+        name="natural_order",
+    )(me, *pieces)
+
+
+def gather_small(value):
+    me = lax.axis_index("dp")
+    held = value[None]
+    for bit in (1, 2, 4):
+        other = swap_dp(held, bit)
+        high = (me & bit) != 0
+        first = jnp.where(high, other, held)
+        second = jnp.where(high, held, other)
+        held = jnp.concatenate([first, second], 0)
+    return held
+
+
+def inward(value):
+    return lax.ppermute(value, "tensor", [(0, 1), (3, 2)])
+
+
+def across(value):
+    return lax.ppermute(value, "tensor", [(1, 2), (2, 1)])
+
+
+def outward(value):
+    return lax.ppermute(value, "tensor", [(1, 0), (2, 3)])
+
+
+def add_low(one, two):
+    return (one.astype(F32) + two.astype(F32)).astype(BF)
+
+
+def line_device(
+    activations,
+    gain_one,
+    gelu_branch,
+    lru_branch,
+    conv_weight,
+    conv_bias,
+    recur_weight,
+    inlet_weight,
+    recur_bias,
+    inlet_bias,
+    decay_param,
+    out_weight,
+    gain_two,
+    ffn_gate,
+    ffn_value,
+    ffn_down,
+    doc_starts,
+    recur_state,
+    conv_state,
+    cotangent,
+):
+    _, length, width = activations.shape
+    channels = gelu_branch.shape[1]
+    units = ffn_gate.shape[1]
+    flat = activations.reshape(length, width)
+    incoming = cotangent.reshape(length, width)
+    me = lax.axis_index("dp").astype(jnp.int32)[None]
+    zed = lax.axis_index("tensor").astype(jnp.int32)[None]
+    count = channels // HEAD
+    chunks = length // CHUNK
+
+    near = gather_pair(gelu_branch, lru_branch)
+    thin = jnp.stack([recur_weight.T, inlet_weight.T])
+    thin_full = gather_small(thin).transpose(1, 0, 2, 3).reshape(2, HEAD, channels)
+    owner = jnp.arange(channels) // HEAD
+    same = owner[:, None] == owner[None, :]
+    heads = jnp.where(same[None], jnp.tile(thin_full, (1, count, 1)), 0).reshape(
+        2 * channels, channels
+    )
+    ffn_own = jnp.concatenate([ffn_gate, ffn_value, ffn_down.T], 1)
+    out_own = out_weight.T
+    inv_one = lax.rsqrt(jnp.mean(flat * flat, axis=-1, keepdims=True) + EPS)
+    normed = (flat * inv_one * gain_one).astype(BF)
+    gains = jnp.stack([gain_one, gain_two, 1.0 / gain_one, 1.0 / gain_two] + [gain_one] * 4)
+    decay = 8.0 * jax.nn.softplus(-decay_param)
+    vec = jnp.concatenate(
+        [
+            conv_weight,
+            conv_bias[None],
+            recur_bias[None],
+            inlet_bias[None],
+            decay[None],
+            recur_state,
+            jnp.zeros((7, channels), F32),
+        ],
+        0,
+    )
+    hist = jnp.concatenate([jnp.zeros((5, channels), F32), conv_state[0]], 0)
+    before = jnp.concatenate([hist, jnp.broadcast_to(recur_state, (8, channels))], 0)
+    near, heads, ffn_own, out_own, inv_one, normed, vec, before = lax.optimization_barrier(
+        (near, heads, ffn_own, out_own, inv_one, normed, vec, before)
+    )
+    far = tuple(swap_dp(item, 1) for item in near)
+    ffn_full = lax.all_gather(ffn_own, "dp", axis=0, tiled=True)
+    far, out_own = lax.optimization_barrier((far, out_own))
+    out_half = out_own.shape[0] // 2
+    out_near = gather_pair(out_own[:out_half], out_own[out_half:])
+    out_far = tuple(swap_dp(item, 1) for item in out_near)
+
+    blocks = CHUNK // SMALL
+    branch_full, *made = run_forward(
+        doc_starts, normed, heads, vec, before, near + far, 0, blocks, me=me
+    )
+    out_full = natural_order(out_near + out_far, me)
+    cot_low = incoming.astype(BF)
+    wide_inv = jnp.broadcast_to(inv_one, (length, 128))
+
+    jobs = [(kind, c) for kind in (TO_NORM, TO_MIDDLE, TO_OUTPUT) for c in range(chunks)]
+    jobs += [(TO_INPUT, c) for c in reversed(range(chunks))]
+    total_jobs = len(jobs)
+    live = {(FORWARD, index): item for index, item in enumerate(made)}
+    flying = {}
+    unit_result = rec_result = None
+
+    def part_one(c):
+        rows = live[FORWARD, 6][c * CHUNK : (c + 1) * CHUNK]
+        return nt_dot(rows, out_full).astype(BF)
+
+    def tie(arrived):
+        if arrived in flying:
+            live[arrived] = flying.pop(arrived)
+        names = sorted(live)
+        values = lax.optimization_barrier(tuple(live[name] for name in names))
+        live.update(zip(names, values))
+
+    def one(kind):
+        return live[kind, 0]
+
+    def kept(*names):
+        return tuple(live[name, 0] for name in names if (name, 0) in live)
+
+    def keep(names, values):
+        for name, value in zip(names, values):
+            live[name, 0] = value
+
+    def small_step(step):
+        if 0 <= step < 3:
+            live[SMALL_SUMS, 0] = one(SMALL_SUMS) + swap_dp(one(SMALL_SUMS), 1 << step)
+        if step == 3:
+            live[GAIN_SUMS, 0] = one(SMALL_SUMS)[8 * channels :]
+        if 3 <= step < 5:
+            pairs = [(i, i ^ (step - 2)) for i in range(4)]
+            live[GAIN_SUMS, 0] = one(GAIN_SUMS) + lax.ppermute(one(GAIN_SUMS), "tensor", pairs)
+
+    def send_in(job):
+        if (PART, job) in live and (INWARD, job) not in flying:
+            flying[INWARD, job] = inward(live[PART, job])
+
+    def backward(first, count):
+        return run_backward(
+            doc_starts,
+            one(MID),
+            out_full,
+            [live[FORWARD, index] for index in range(6)],
+            heads,
+            vec,
+            hist,
+            one(CARRIED),
+            first,
+            count,
+            kept(PRE_GRAD, GATES_GRAD),
+        )
+
+    live[PART, 0] = part_one(0)
+    live[CARRIED, 0] = jnp.zeros((32, channels), F32)
+    shape = (8, 3 * width // 8 + 48, channels)
+    tiles = units // FTILE
+    second, third, fourth = chunks, 2 * chunks, 3 * chunks
+    for slot in range(total_jobs + 4):
+        if slot == total_jobs:
+            live[UNIT_RESULT, 0] = unit_result
+        tie((INWARD, slot - 2))
+        small_step(3 * (slot - total_jobs))
+        job = slot - 2
+        if (INWARD, job) in live:
+            live[SUM, job] = add_low(live.pop((PART, job)), live.pop((INWARD, job)))
+            flying[ACROSS, job] = across(live[SUM, job])
+        if slot == third:
+            (live[PART, slot],) = run_nt(one(ACTS), 0, 1, 2, one(WEIGHTS), 2, units)
+        send_in(slot)
+
+        tie((ACROSS, slot - 3))
+        small_step(3 * (slot - total_jobs) + 1)
+        job = slot - 3
+        if (ACROSS, job) in live:
+            live[OWN, job] = add_low(live.pop((SUM, job)), live.pop((ACROSS, job)))
+            flying[OUTWARD, job] = outward(live[OWN, job])
+        if slot == second:
+            live[WEIGHTS, 0] = ffn_full
+
+        tie((OUTWARD, slot - 4))
+        small_step(3 * (slot - total_jobs) + 2)
+        job = slot - 4
+        if (OUTWARD, job) in live:
+            kind, c = jobs[job]
+            whole = (zed, live.pop((OWN, job)), live.pop((OUTWARD, job)))
+            first = c * CHUNK
+            if kind == TO_NORM:
+                names = (ACTS, NORMED, FIRST, INV)
+                *made, live[PART, slot] = run_ffn(
+                    c, *whole, flat, gains, cot_low, one(WEIGHTS), kept(*names)
+                )
+                keep(names, made)
+                send_in(slot)
+            elif kind == TO_MIDDLE:
+                low = pltpu.HBM((length, width), BF)
+                *made, live[GAIN, c] = run_rows(
+                    middle_kernel,
+                    "middle_grad",
+                    *whole,
+                    [one(NORMED), one(INV), gains, incoming],
+                    first,
+                    [low, low, jax.ShapeDtypeStruct((8, width), F32)],
+                    kept(MID, BACK),
+                )
+                keep((MID, BACK), made)
+            else:
+                if kind == TO_OUTPUT:
+                    name, body, label = OUTPUT, output_kernel, "output"
+                    others = [one(FIRST), flat]
+                else:
+                    name, body, label = INPUT, input_kernel, "input_grad"
+                    others = [normed, wide_inv, gains, one(BACK), incoming]
+                wide = [pltpu.HBM((length, width), F32)]
+                keep((name,), run_rows(body, label, *whole, others, first, wide, kept(name)))
+
+        if slot < 2:
+            start = blocks if slot == 0 else 2 * blocks
+            steps = blocks if slot == 0 else length // SMALL - 2 * blocks
+            made = run_forward(
+                doc_starts,
+                normed,
+                heads,
+                vec,
+                live[FORWARD, 7],
+                branch_full,
+                start,
+                steps,
+                [live[FORWARD, index] for index in range(7)],
+            )
+            for index, item in enumerate(made):
+                live[FORWARD, index] = item
+            for c in range(1, 2) if slot == 0 else range(2, chunks):
+                live[PART, c] = part_one(c)
+        if slot == third:
+            made = run_nt(one(ACTS), CHUNK, chunks - 1, 2, live.pop((WEIGHTS, 0)), 2, units)
+            for c in range(1, chunks):
+                live[PART, third + c] = made[c - 1]
+        if third <= slot < third + 3:
+            which = slot - third
+            live[UNIT_GRAD, 0] = run_weight_grad(
+                one(NORMED) if which < 2 else cot_low,
+                one(ACTS),
+                which * tiles,
+                tiles,
+                live.get((UNIT_GRAD, 0)),
+                3 * units,
+            )
+        if slot == third + 3:
+            unit_result = lax.psum_scatter(
+                live.pop((UNIT_GRAD, 0)), "dp", scatter_dimension=0, tiled=True
+            )
+            live.pop((ACTS, 0))
+            live.pop((NORMED, 0))
+            half = length // SMALL // 2
+            names = (PRE_GRAD, GATES_GRAD, CARRIED)
+            keep(names, backward(half, half))
+            pieces = chunks // 2
+            made = run_nt(one(PRE_GRAD), length // 2, pieces, 0, branch_full, 0, 2 * channels)
+            for c in range(pieces):
+                live[PART, fourth + c] = made[pieces - 1 - c]
+            send_in(fourth)
+            keep(names, backward(0, half))
+            made = run_nt(one(PRE_GRAD), 0, pieces, 0, branch_full, 0, 2 * channels)
+            for c in range(pieces):
+                live[PART, fourth + pieces + c] = made[pieces - 1 - c]
+        if slot == fourth:
+            live[PACKED, 0] = run_packed_grad(normed, one(PRE_GRAD), 0, None, shape)
+        if slot == fourth + 1:
+            live[PACKED, 0] = run_packed_grad(
+                one(MID), live[FORWARD, 6], 2, one(PACKED), shape
+            )
+        if slot == fourth + 2:
+            live[PACKED, 0] = run_thin_grad(one(GATES_GRAD), live[FORWARD, 2], one(PACKED))
+        if fourth <= slot < total_jobs:
+            c = jobs[slot][1]
+            rows = slice(c * CHUNK, (c + 1) * CHUNK)
+            part = live[PART, slot].astype(F32) * flat[rows] * inv_one[rows]
+            live[GAIN_ONE, 0] = live.get((GAIN_ONE, 0), 0.0) + jnp.sum(part, axis=0)
+        if slot == total_jobs - 1:
+            gain_sum = sum(live.pop((GAIN, c))[0] for c in range(chunks))
+            live[SMALL_SUMS, 0] = jnp.concatenate(
+                [
+                    live.pop((CARRIED, 0))[24:].reshape(-1),
+                    live.pop((GAIN_ONE, 0)),
+                    jnp.where(zed == 1, gain_sum / gain_two, 0.0),
+                ]
+            )
+            live.pop((GATES_GRAD, 0))
+        if slot == total_jobs:
+            rec_result = lax.psum_scatter(
+                live.pop((PACKED, 0)), "dp", scatter_dimension=0, tiled=True
+            )[0]
+
+    branch, states = live[FORWARD, 1], live[FORWARD, 3]
+    sums_all = one(SMALL_SUMS)[: 8 * channels].reshape(8, channels)
+    last_begin = jnp.max(
+        jnp.where(doc_starts <= length - 1, doc_starts, -3), axis=1, keepdims=True
+    )
+    places = length - 3 + jnp.arange(3, dtype=jnp.int32)
+    conv_keep = (places[None, :] >= last_begin)[:, :, None]
+    conv_final = jnp.where(conv_keep, branch[None, length - 3 :], 0.0)
+    decay_grad = sums_all[7] * (-8.0 * jax.nn.sigmoid(-decay_param))
+    ffn_w = one(UNIT_RESULT).astype(F32)
+    rec_w = rec_result.astype(F32)
+    own = out_weight.shape[1]
+    slim = recur_weight.shape[1]
+    return (
+        one(OUTPUT)[None],
+        states[length - 1 :],
+        conv_final,
+        one(INPUT)[None],
+        one(GAIN_SUMS)[:width],
+        rec_w[:own],
+        rec_w[own : 2 * own],
+        sums_all[0:4],
+        sums_all[4],
+        rec_w[3 * own : 3 * own + slim].T,
+        rec_w[3 * own + slim : 3 * own + 2 * slim].T,
+        sums_all[5],
+        sums_all[6],
+        decay_grad,
+        rec_w[2 * own : 3 * own].T,
+        one(GAIN_SUMS)[width:],
+        ffn_w[:, :units],
+        ffn_w[:, units : 2 * units],
+        ffn_w[:, 2 * units :].T,
+    )
+
+
+def fits_line(mesh):
+    return mesh.shape["dp"] == 8 and mesh.shape["tensor"] == 4
+
+
 def solution(mesh):
     in_specs = (
         P("dp", None, None),
@@ -328,6 +1434,7 @@
         P("dp", "tensor"),
         P("tensor", "dp"),
     )
+    body = line_device if fits_line(mesh) else per_device
     return jax.shard_map(
-        per_device, mesh=mesh, in_specs=in_specs, out_specs=out_specs, check_vma=False
-    )
+        body, mesh=mesh, in_specs=in_specs, out_specs=out_specs, check_vma=False
+    )

time: 2280 us -> 647 us (0.28)
  waiting for transfers between devices: 1610 us -> 116 us
  Pallas kernels: 0 us -> 268 us
  local copies, waits for them, and re-layouts: 232 us -> 23.5 us
  matrix products: 206 us -> 9.17 us
  starting transfers between devices: 1.22 us -> 137 us
  other arithmetic: 166 us -> 66.9 us
  blocking collectives: 46.7 us -> 0 us
    psum x3 -> x0, waiting for transfers between devices: 1090 us -> none  [tensor_reduce(): return lax.psum(partial_sum, 'tensor')]
    reduce_scatter x6 -> x2, waiting for transfers between devices: 413 us -> 0.02 us  [the longest x1 0.02 us: line_device(): lax.psum_scatter(live.pop((UNIT_GRAD, 0)), 'dp', scatter_dimension=0, til...]
    pallas_call x0 -> x32, Pallas kernels: none -> 268 us  [the longest x4 62.8 us: run_ffn(): pl.pallas_call(functools.partial(ffn_kernel, part, units), grid=(1,), in_...]
    dot_general x24 -> x4, matrix products: 206 us -> 9.17 us  [nt_dot(): lax.dot_general(left, right, (((1,), (1,)), ((), ())), preferred_element_...]
    ppermute x0 -> x72, starting transfers between devices: none -> 136 us  [the longest x16 70.8 us: inward(): return lax.ppermute(value, 'tensor', [(0, 1), (3, 2)])]
    ppermute x0 -> x72, waiting for transfers between devices: none -> 116 us  [the longest x16 36.4 us: outward(): return lax.ppermute(value, 'tensor', [(1, 0), (2, 3)])]
    all_gather x6 -> x1, waiting for transfers between devices: 102 us -> 0.01 us  [line_device(): ffn_full = lax.all_gather(ffn_own, 'dp', axis=0, tiled=True)]
    pad x79 -> x0, local copies, waits for them, and re-layouts: 98.6 us -> none  [recurrence(): _, states = lax.associative_scan(combine, (carries, drive), axis=0)]
  transfers between devices with their start and end apart: 16 -> 75, of which waited for: 12 -> 24; matrix products, arithmetic and copies ran while one was open for 15% -> 14% of each run, Pallas kernels for 0% -> 42%
where the time goes in v1:
time: 647 us; the launch traced here: 636 us
  Pallas kernels  268 us (41%)
  starting transfers between devices  137 us (21%)
  waiting for transfers between devices  116 us (18%)
  other arithmetic  66.9 us (10%)
  local copies, waits for them, and re-layouts  23.5 us (4%)
  between operations  15.8 us (2%)
  matrix products  9.17 us (1%)
    ppermute x16, starting transfers between devices, inward(): return lax.ppermute(value, 'tensor', [(0, 1), (3, 2)])  70.8 us
    pallas_call x4, Pallas kernels, run_ffn(): pl.pallas_call(functools.partial(ffn_kernel, part, units), grid=(1,), in_...  62.8 us
    pallas_call x12, Pallas kernels, run_rows(): pl.pallas_call(body, grid=(rows // step,), in_specs=in_specs, out_specs=[...  57 us
    ppermute x16, waiting for transfers between devices, outward(): return lax.ppermute(value, 'tensor', [(1, 0), (2, 3)])  36.4 us
    convert_element_type x32, other arithmetic, add_low(): return (one.astype(F32) + two.astype(F32)).astype(BF)  34.5 us
    ppermute x22, waiting for transfers between devices, swap_dp(): return lax.ppermute(value, 'dp', [(i, i ^ bit) for i in range(8)])  33.8 us
    pallas_call x3, Pallas kernels, run_weight_grad(): pl.pallas_call(tn_kernel, grid=(tiles,), in_specs=in_specs, out_specs=pl....  33.4 us
    pallas_call x3, Pallas kernels, run_forward(): pl.pallas_call(functools.partial(forward_kernel, starts.shape[1], first,...  30.3 us
  transfers between devices with their start and end apart: 75, of which 24 were waited for; matrix products, arithmetic and copies ran while one was open for 14% of the time, Pallas kernels for 42%

profile of v1, /device:TPU:0, one launch (start us, length us, event | category | flops | bytes accessed | tf_op | source)
XLA Modules:
  0.0 636.2 jit_solution(11839937687804110739)
XLA Ops:
  83.0 7.4 %recurrent_forward.3 = (bf16[2048,1280]{1,0:T(8,128)(2,1)}, f32[1024,640]{1,0:T(8,128)}, f32[1024,640]{1,0:T(8,128)}, bf16[1024,640]{1,0:T(8,128)(2,1)}, f32[102...) custom-call(s32[1,3]{1,0:T(1,128)S(1)} %copy-done.5, ...), custom_call_target="tpu_custom_call" | custom-call | flops 1761607680 | bytes 4915200 | tf_op jit(solution)/shard_map/recurrent_forward/pallas_call | solution.py:486
  99.0 10.0 %recurrent_forward.4 = (f32[1024,640]{1,0:T(8,128)}, f32[1024,640]{1,0:T(8,128)}, bf16[1024,640]{1,0:T(8,128)(2,1)}, f32[1024,640]{1,0:T(8,128)}, f32[1024,640]{...) custom-call(s32[1,3]{1,0:T(1,128)S(1)} %copy-done.5, ...), custom_call_target="tpu_custom_call", output_to_operand_aliasing={{0}: (6, {}), {1}: (7, {}), {2}: (8, {}), {3}: (9, {}), {4}... | custom-call | flops 1761607680 | bytes 4915200 | tf_op jit(solution)/shard_map/recurrent_forward/pallas_call | solution.py:486
  112.7 12.9 %recurrent_forward.5 = (f32[1024,640]{1,0:T(8,128)}, f32[1024,640]{1,0:T(8,128)}, bf16[1024,640]{1,0:T(8,128)(2,1)}, f32[1024,640]{1,0:T(8,128)}, f32[1024,640]{...) custom-call(s32[1,3]{1,0:T(1,128)S(1)} %copy-done.5, ...), custom_call_target="tpu_custom_call", output_to_operand_aliasing={{0}: (6, {}), {1}: (7, {}), {2}: (8, {}), {3}: (9, {}), {4}... | custom-call | flops 3523215360 | bytes 9830400 | tf_op jit(solution)/shard_map/recurrent_forward/pallas_call | solution.py:486
  136.7 7.9 %collective-permute-done.20 = bf16[256,2048]{1,0:T(8,128)(2,1)S(1)} collective-permute-done((bf16[256,2048]{1,0:T(8,128)(2,1)S(1)}, bf16[256,2048]{1,0:T(8,128)(2,1)S(1)}, u32[]{:S(2)}, u32[]{:S(2)}) %collective-permute-start.20) | collective-permute-done | bytes 1048608 | tf_op jit(solution)/shard_map/ppermute | solution.py:1063
  145.8 8.1 %collective-permute-start.25 = (bf16[256,2048]{1,0:T(8,128)(2,1)}, bf16[256,2048]{1,0:T(8,128)(2,1)}, u32[]{:S(2)}, u32[]{:S(2)}) collective-permute-start(bf16[256,2048]{1,0:T(8,128)(2,1)} %convolution_convert_fusion), channel_id=1, source_target_pairs={{0,1},{3,2},{4,5},{7,6},{8,9},{11,10},{12,13},{15,14},{16,17},{19,... | collective-permute-start | bytes 3145736 | tf_op jit(solution)/shard_map/ppermute | solution.py:1063
  155.7 11.4 %collective-permute-done.22 = bf16[256,2048]{1,0:T(8,128)(2,1)S(1)} collective-permute-done((bf16[256,2048]{1,0:T(8,128)(2,1)S(1)}, bf16[256,2048]{1,0:T(8,128)(2,1)S(1)}, u32[]{:S(2)}, u32[]{:S(2)}) %collective-permute-start.22) | collective-permute-done | bytes 1048608 | tf_op jit(solution)/shard_map/ppermute | solution.py:1063
  172.3 8.4 %collective-permute-done.24.came = bf16[256,2048]{1,0:T(8,128)(2,1)S(1)} collective-permute-done((bf16[256,2048]{1,0:T(8,128)(2,1)S(1)}, bf16[256,2048]{1,0:T(8,128)(2,1)S(1)}, u32[]{:S(2)}, u32[]{:S(2)}) %collective-permute-start.24) | collective-permute-done | bytes 1048608 | tf_op jit(solution)/shard_map/ppermute | solution.py:1071
  180.7 15.6 %ffn_chunk.4 = (bf16[1024,4608]{1,0:T(8,128)(2,1)}, bf16[1024,2048]{1,0:T(8,128)(2,1)}, bf16[1024,2048]{1,0:T(8,128)(2,1)}, f32[1024,128]{1,0:T(8,128)}, bf16[256,2048]{1,0:T(8,128)(2,1)S(1)}) custom-call(s32[1]{0:T(128)} %bitcast.30.zed_ref, bf16[256,2048]{1,0:T(8,128)(2,1)S(1)} %add_convert_fusion.29.own, ...), custom_call_target="tpu_custom_call" | custom-call | flops 8053063680 | bytes 18874368 | tf_op jit(solution)/shard_map/ffn_chunk/pallas_call | solution.py:754
  205.9 15.9 %ffn_chunk.5 = (bf16[1024,4608]{1,0:T(8,128)(2,1)}, bf16[1024,2048]{1,0:T(8,128)(2,1)}, bf16[1024,2048]{1,0:T(8,128)(2,1)}, f32[1024,128]{1,0:T(8,128)}, bf16[256,2048]{1,0:T(8,128)(2,1)S(1)}) custom-call(s32[1]{0:T(128)} %bitcast.30.zed_ref, ...), custom_call_target="tpu_custom_call", output_to_operand_aliasing={{0}: (7, {}), {1}: (8, {}), {2}: (9, {}), {3}: (10, {})} | custom-call | flops 8053063680 | bytes 18874368 | tf_op jit(solution)/shard_map/ffn_chunk/pallas_call | solution.py:754
  230.4 15.6 %ffn_chunk.6 = (bf16[1024,4608]{1,0:T(8,128)(2,1)}, bf16[1024,2048]{1,0:T(8,128)(2,1)}, bf16[1024,2048]{1,0:T(8,128)(2,1)}, f32[1024,128]{1,0:T(8,128)}, bf16[256,2048]{1,0:T(8,128)(2,1)S(1)}) custom-call(s32[1]{0:T(128)} %bitcast.30.zed_ref, ...), custom_call_target="tpu_custom_call", output_to_operand_aliasing={{0}: (7, {}), {1}: (8, {}), {2}: (9, {}), {3}: (10, {})} | custom-call | flops 8053063680 | bytes 18874368 | tf_op jit(solution)/shard_map/ffn_chunk/pallas_call | solution.py:754
  253.5 15.6 %ffn_chunk.7 = (bf16[1024,4608]{1,0:T(8,128)(2,1)}, bf16[1024,2048]{1,0:T(8,128)(2,1)}, bf16[1024,2048]{1,0:T(8,128)(2,1)}, f32[1024,128]{1,0:T(8,128)}, bf16[256,2048]{1,0:T(8,128)(2,1)S(1)}) custom-call(s32[1]{0:T(128)} %bitcast.30.zed_ref, ...), custom_call_target="tpu_custom_call", output_to_operand_aliasing={{0}: (7, {}), {1}: (8, {}), {2}: (9, {}), {3}: (10, {})} | custom-call | flops 8053063680 | bytes 18874368 | tf_op jit(solution)/shard_map/ffn_chunk/pallas_call | solution.py:754
  285.1 11.1 %unit_weight_grad.3.refs_0_ = bf16[2048,4608]{1,0:T(8,128)(2,1)} custom-call(bf16[1024,2048]{1,0:T(8,128)(2,1)} %get-tuple-element.1759.normed_ref.left, bf16[1024,4608]{1,0:T(8,128)(2,1)} %get-tuple-element.1693.left.right), custom_call_target="tpu_custom_call" | custom-call | flops 6442450944 | bytes 13631488 | tf_op jit(solution)/shard_map/unit_weight_grad/pallas_call | solution.py:832
  300.7 8.9 %rows_by_rows.5 = (bf16[256,2048]{1,0:T(8,128)(2,1)S(1)}, bf16[256,2048]{1,0:T(8,128)(2,1)}, bf16[256,2048]{1,0:T(8,128)(2,1)}) custom-call(bf16[1024,4608]{1,0:T(8,128)(2,1)} %get-tuple-element.1693.left.right, bf16[2048,4608]{1,0:T(8,128)(2,1)} %all-gather.2.cloned.1.call-done.weight_ref.right), custom_call_target="tpu_custom_call" | custom-call | flops 4831838208 | bytes 12582912 | tf_op jit(solution)/shard_map/rows_by_rows/pallas_call | solution.py:801
  310.7 7.4 %collective-permute-start.43 = (bf16[256,2048]{1,0:T(8,128)(2,1)S(1)}, bf16[256,2048]{1,0:T(8,128)(2,1)}, u32[]{:S(2)}, u32[]{:S(2)}) collective-permute-start(bf16[256,2048]{1,0:T(8,128)(2,1)S(1)} %get-tuple-element.1710), channel_id=1, source_target_pairs={{0,1},{3,2},{4,5},{7,6},{8,9},{11,10},{12,13},{15,14},{16,17},{19,... | collective-permute-start | bytes 3145736 | tf_op jit(solution)/shard_map/ppermute | solution.py:1063
  324.4 11.2 %unit_weight_grad.4.refs_0_ = bf16[2048,4608]{1,0:T(8,128)(2,1)} custom-call(bf16[1024,2048]{1,0:T(8,128)(2,1)} %get-tuple-element.1759.normed_ref.left, bf16[1024,4608]{1,0:T(8,128)(2,1)} %get-tuple-element.1693.left.right, bf16[2048,4608]{1,0:T(8,128)(2,1)} %unit_weight_grad.3.refs_0_), custom_call_target="tpu_custom_call", output_to_operand_aliasing={{}: (2, {})} | custom-call | flops 6442450944 | bytes 13631488 | tf_op jit(solution)/shard_map/unit_weight_grad/pallas_call | solution.py:832
  346.8 11.1 %unit_weight_grad.5 = bf16[2048,4608]{1,0:T(8,128)(2,1)} custom-call(bf16[1024,2048]{1,0:T(8,128)(2,1)} %bitcast_convert_fusion.cot_ref.left, bf16[1024,4608]{1,0:T(8,128)(2,1)} %get-tuple-element.1693.left.right, bf16[2048,4608]{1,0:T(8,128)(2,1)} %unit_weight_grad.4.refs_0_), custom_call_target="tpu_custom_call", output_to_operand_aliasing={{}: (2, {})} | custom-call | flops 6442450944 | bytes 13631488 | tf_op jit(solution)/shard_map/unit_weight_grad/pallas_call | solution.py:832
  381.5 15.3 %recurrent_backward.2 = (bf16[1024,1280]{1,0:T(8,128)(2,1)}, bf16[1024,1280]{1,0:T(8,128)(2,1)}, f32[32,640]{1,0:T(8,128)S(1)}) custom-call(s32[1,3]{1,0:T(1,128)S(1)} %copy-done.5, bf16[1024,2048]{1,0:T(8,128)(2,1)} %get-tuple-element.1948.grad_ref.left, bf16[2048,640]{1,0:T(8,128)(2,1)} %copy-done, f32[1024,640]{1,0:T(8,128)} %get-tuple-element.1764.gate_ref, ...), custom_call_target="tpu_custom_call" | custom-call | flops 2181038080 | bytes 11141120 | tf_op jit(solution)/shard_map/recurrent_backward/pallas_call | solution.py:649
  405.0 14.1 %recurrent_backward.3 = (bf16[1024,1280]{1,0:T(8,128)(2,1)}, bf16[1024,1280]{1,0:T(8,128)(2,1)}, f32[32,640]{1,0:T(8,128)S(1)}) custom-call(s32[1,3]{1,0:T(1,128)S(1)} %copy-done.5, bf16[1024,2048]{1,0:T(8,128)(2,1)} %get-tuple-element.1948.grad_ref.left, bf16[2048,640]{1,0:T(8,128)(2,1)} %copy-done, ...), custom_call_target="tpu_custom_call", output_to_operand_aliasing={{0}: (14, {}), {1}: (15, {})} | custom-call | flops 2181038080 | bytes 11141120 | tf_op jit(solution)/shard_map/recurrent_backward/pallas_call | solution.py:649
  438.0 11.5 %branch_weight_grad.2.refs_0_ = bf16[8,816,640]{2,1,0:T(8,128)(2,1)} custom-call(bf16[1024,2048]{1,0:T(8,128)(2,1)} %multiply_convert_fusion.refs_5_.refs_0_.left.normed, bf16[1024,1280]{1,0:T(8,128)(2,1)} %get-tuple-element.1864.left.right), custom_call_target="tpu_custom_call" | custom-call | flops 5368709120 | bytes 9437184 | tf_op jit(solution)/shard_map/branch_weight_grad/pallas_call | solution.py:870
  466.8 9.3 %branch_weight_grad.3.kept = bf16[8,816,640]{2,1,0:T(8,128)(2,1)} custom-call(bf16[1024,2048]{1,0:T(8,128)(2,1)} %get-tuple-element.1948.grad_ref.left, bf16[1024,640]{1,0:T(8,128)(2,1)} %get-tuple-element.1955.right, bf16[8,816,640]{2,1,0:T(8,128)(2,1)} %branch_weight_grad.2.refs_0_), custom_call_target="tpu_custom_call", output_to_operand_aliasing={{}: (2, {})} | custom-call | flops 2684354560 | bytes 6815744 | tf_op jit(solution)/shard_map/branch_weight_grad/pallas_call | solution.py:870
  479.1 7.6 %collective-permute-start.58 = (bf16[256,2048]{1,0:T(8,128)(2,1)}, bf16[256,2048]{1,0:T(8,128)(2,1)}, u32[]{:S(2)}, u32[]{:S(2)}) collective-permute-start(bf16[256,2048]{1,0:T(8,128)(2,1)} %get-tuple-element.2102), channel_id=1, source_target_pairs={{0,1},{3,2},{4,5},{7,6},{8,9},{11,10},{12,13},{15,14},{16,17},{19,... | collective-permute-start | bytes 3145736 | tf_op jit(solution)/shard_map/ppermute | solution.py:1063
  542.0 9.1 %collective-permute-done.63 = bf16[256,2048]{1,0:T(8,128)(2,1)S(1)} collective-permute-done((bf16[256,2048]{1,0:T(8,128)(2,1)S(1)}, bf16[256,2048]{1,0:T(8,128)(2,1)S(1)}, u32[]{:S(2)}, u32[]{:S(2)}) %collective-permute-start.63) | collective-permute-done | bytes 1048608 | tf_op jit(solution)/shard_map/ppermute | solution.py:1063
  562.9 15.5 %collective-permute-done.68 = f32[4096]{0:T(1024)S(1)} collective-permute-done((f32[4096]{0:T(1024)S(1)}, f32[4096]{0:T(1024)S(1)}, u32[]{:S(2)}, u32[]{:S(2)}) %collective-permute-start.68) | collective-permute-done | bytes 16416 | tf_op jit(solution)/shard_map/ppermute | solution.py:1191
  591.3 15.5 %collective-permute-done.71.came = bf16[256,2048]{1,0:T(8,128)(2,1)S(1)} collective-permute-done((bf16[256,2048]{1,0:T(8,128)(2,1)S(1)}, bf16[256,2048]{1,0:T(8,128)(2,1)S(1)}, u32[]{:S(2)}, u32[]{:S(2)}) %collective-permute-start.71) | collective-permute-done | bytes 1048608 | tf_op jit(solution)/shard_map/ppermute | solution.py:1071
  (355 shorter events, 343.8 us)
Async XLA Ops:
  7.2 173.5 %all-gather.2.cloned.1.call-start = ((), (), s32[]{:S(2)}) async-start(), calls=%async_computation.2 | async-start | bytes 21233664 | tf_op jit(solution)/shard_map/all_gather | solution.py:1142
  12.3 34.1 %collective-permute-start.3 = (bf16[256,640]{1,0:T(8,128)(2,1)}, bf16[256,640]{1,0:T(8,128)(2,1)S(1)}, u32[]{:S(2)}, u32[]{:S(2)}) collective-permute-start(bf16[256,640]{1,0:T(8,128)(2,1)} %param.23), channel_id=1, source_target_pairs={{0,8},{4,12},{8,0},{12,4},{16,24},{20,28},{24,16},{28,20},{1,9},{5... | collective-permute-start | bytes 983048 | tf_op jit(solution)/shard_map/ppermute | solution.py:1004
  48.3 468.1 %reduce-scatter.3.cloned.1.call-start = ((), (), s32[]{:S(2)}) async-start(), calls=%async_computation.3 | async-start | bytes 21233664 | tf_op jit(solution)/shard_map/reduce_scatter | solution.py:1308
  95.3 35.4 %collective-permute-start.19 = (bf16[256,2048]{1,0:T(8,128)(2,1)S(1)}, bf16[256,2048]{1,0:T(8,128)(2,1)S(1)}, u32[]{:S(2)}, u32[]{:S(2)}) collective-permute-start(bf16[256,2048]{1,0:T(8,128)(2,1)S(1)} %convolution_convert_fusion.3), channel_id=1, source_target_pairs={{0,1},{3,2},{4,5},{7,6},{8,9},{11,10},{12,13},{15,14},{16,17},{19,... | collective-permute-start | bytes 3145736 | tf_op jit(solution)/shard_map/ppermute | solution.py:1063
  111.1 33.6 %collective-permute-start.20 = (bf16[256,2048]{1,0:T(8,128)(2,1)S(1)}, bf16[256,2048]{1,0:T(8,128)(2,1)S(1)}, u32[]{:S(2)}, u32[]{:S(2)}) collective-permute-start(bf16[256,2048]{1,0:T(8,128)(2,1)S(1)} %convolution_convert_fusion.2), channel_id=1, source_target_pairs={{0,1},{3,2},{4,5},{7,6},{8,9},{11,10},{12,13},{15,14},{16,17},{19,... | collective-permute-start | bytes 3145736 | tf_op jit(solution)/shard_map/ppermute | solution.py:1063
  145.8 53.9 %collective-permute-start.25 = (bf16[256,2048]{1,0:T(8,128)(2,1)}, bf16[256,2048]{1,0:T(8,128)(2,1)}, u32[]{:S(2)}, u32[]{:S(2)}) collective-permute-start(bf16[256,2048]{1,0:T(8,128)(2,1)} %convolution_convert_fusion), channel_id=1, source_target_pairs={{0,1},{3,2},{4,5},{7,6},{8,9},{11,10},{12,13},{15,14},{16,17},{19,... | collective-permute-start | bytes 3145736 | tf_op jit(solution)/shard_map/ppermute | solution.py:1063
  168.5 33.9 %collective-permute-start.26 = (bf16[256,2048]{1,0:T(8,128)(2,1)}, bf16[256,2048]{1,0:T(8,128)(2,1)}, u32[]{:S(2)}, u32[]{:S(2)}) collective-permute-start(bf16[256,2048]{1,0:T(8,128)(2,1)} %add_convert_fusion.28), channel_id=1, source_target_pairs={{1,2},{2,1},{5,6},{6,5},{9,10},{10,9},{13,14},{14,13},{17,18},{18,... | collective-permute-start | bytes 3145736 | tf_op jit(solution)/shard_map/ppermute | solution.py:1067
  170.6 35.3 %collective-permute-start.27 = (bf16[256,2048]{1,0:T(8,128)(2,1)S(1)}, bf16[256,2048]{1,0:T(8,128)(2,1)}, u32[]{:S(2)}, u32[]{:S(2)}) collective-permute-start(bf16[256,2048]{1,0:T(8,128)(2,1)S(1)} %add_convert_fusion.27.own), channel_id=1, source_target_pairs={{1,0},{2,3},{5,4},{6,7},{9,8},{10,11},{13,12},{14,15},{17,16},{18,... | collective-permute-start | bytes 3145736 | tf_op jit(solution)/shard_map/ppermute | solution.py:1071
  251.5 33.6 %collective-permute-start.36 = (bf16[256,2048]{1,0:T(8,128)(2,1)S(1)}, bf16[256,2048]{1,0:T(8,128)(2,1)S(1)}, u32[]{:S(2)}, u32[]{:S(2)}) collective-permute-start(bf16[256,2048]{1,0:T(8,128)(2,1)S(1)} %add_convert_fusion.21.own), channel_id=1, source_target_pairs={{1,0},{2,3},{5,4},{6,7},{9,8},{10,11},{13,12},{14,15},{17,16},{18,... | collective-permute-start | bytes 3145736 | tf_op jit(solution)/shard_map/ppermute | solution.py:1071
  269.2 40.4 %collective-permute-start.37 = (bf16[256,2048]{1,0:T(8,128)(2,1)S(1)}, bf16[256,2048]{1,0:T(8,128)(2,1)S(1)}, u32[]{:S(2)}, u32[]{:S(2)}) collective-permute-start(bf16[256,2048]{1,0:T(8,128)(2,1)S(1)} %get-tuple-element.1556), channel_id=1, source_target_pairs={{0,1},{3,2},{4,5},{7,6},{8,9},{11,10},{12,13},{15,14},{16,17},{19,... | collective-permute-start | bytes 3145736 | tf_op jit(solution)/shard_map/ppermute | solution.py:1063
  274.4 43.7 %collective-permute-start.38 = (bf16[256,2048]{1,0:T(8,128)(2,1)S(1)}, bf16[256,2048]{1,0:T(8,128)(2,1)S(1)}, u32[]{:S(2)}, u32[]{:S(2)}) collective-permute-start(bf16[256,2048]{1,0:T(8,128)(2,1)S(1)} %add_convert_fusion.20), channel_id=1, source_target_pairs={{1,2},{2,1},{5,6},{6,5},{9,10},{10,9},{13,14},{14,13},{17,18},{18,... | collective-permute-start | bytes 3145736 | tf_op jit(solution)/shard_map/ppermute | solution.py:1067
  279.3 56.3 %collective-permute-start.40 = (bf16[256,2048]{1,0:T(8,128)(2,1)S(1)}, bf16[256,2048]{1,0:T(8,128)(2,1)S(1)}, u32[]{:S(2)}, u32[]{:S(2)}) collective-permute-start(bf16[256,2048]{1,0:T(8,128)(2,1)S(1)} %rows_by_rows.4), channel_id=1, source_target_pairs={{0,1},{3,2},{4,5},{7,6},{8,9},{11,10},{12,13},{15,14},{16,17},{19,... | collective-permute-start | bytes 3145736 | tf_op jit(solution)/shard_map/ppermute | solution.py:1063
  283.6 36.2 %collective-permute-start.39 = (bf16[256,2048]{1,0:T(8,128)(2,1)S(1)}, bf16[256,2048]{1,0:T(8,128)(2,1)S(1)}, u32[]{:S(2)}, u32[]{:S(2)}) collective-permute-start(bf16[256,2048]{1,0:T(8,128)(2,1)S(1)} %add_convert_fusion.19.own), channel_id=1, source_target_pairs={{1,0},{2,3},{5,4},{6,7},{9,8},{10,11},{13,12},{14,15},{17,16},{18,... | collective-permute-start | bytes 3145736 | tf_op jit(solution)/shard_map/ppermute | solution.py:1071
  310.7 47.2 %collective-permute-start.43 = (bf16[256,2048]{1,0:T(8,128)(2,1)S(1)}, bf16[256,2048]{1,0:T(8,128)(2,1)}, u32[]{:S(2)}, u32[]{:S(2)}) collective-permute-start(bf16[256,2048]{1,0:T(8,128)(2,1)S(1)} %get-tuple-element.1710), channel_id=1, source_target_pairs={{0,1},{3,2},{4,5},{7,6},{8,9},{11,10},{12,13},{15,14},{16,17},{19,... | collective-permute-start | bytes 3145736 | tf_op jit(solution)/shard_map/ppermute | solution.py:1063
  364.2 260.7 %reduce-scatter.5.cloned.1.call-start = ((), (), s32[]{:S(2)}) async-start(), calls=%async_computation.4 | async-start | bytes 9400320 | tf_op jit(solution)/shard_map/reduce_scatter | solution.py:1349
  364.3 61.9 %collective-permute-start.46 = (bf16[256,2048]{1,0:T(8,128)(2,1)}, bf16[256,2048]{1,0:T(8,128)(2,1)S(1)}, u32[]{:S(2)}, u32[]{:S(2)}) collective-permute-start(bf16[256,2048]{1,0:T(8,128)(2,1)} %get-tuple-element.1797), channel_id=1, source_target_pairs={{0,1},{3,2},{4,5},{7,6},{8,9},{11,10},{12,13},{15,14},{16,17},{19,... | collective-permute-start | bytes 3145736 | tf_op jit(solution)/shard_map/ppermute | solution.py:1063
  368.5 60.2 %collective-permute-start.47 = (bf16[256,2048]{1,0:T(8,128)(2,1)}, bf16[256,2048]{1,0:T(8,128)(2,1)S(1)}, u32[]{:S(2)}, u32[]{:S(2)}) collective-permute-start(bf16[256,2048]{1,0:T(8,128)(2,1)} %add_convert_fusion.14), channel_id=1, source_target_pairs={{1,2},{2,1},{5,6},{6,5},{9,10},{10,9},{13,14},{14,13},{17,18},{18,... | collective-permute-start | bytes 3145736 | tf_op jit(solution)/shard_map/ppermute | solution.py:1067
  369.3 62.4 %collective-permute-start.48 = (bf16[256,2048]{1,0:T(8,128)(2,1)S(1)}, bf16[256,2048]{1,0:T(8,128)(2,1)S(1)}, u32[]{:S(2)}, u32[]{:S(2)}) collective-permute-start(bf16[256,2048]{1,0:T(8,128)(2,1)S(1)} %add_convert_fusion.13.own), channel_id=1, source_target_pairs={{1,0},{2,3},{5,4},{6,7},{9,8},{10,11},{13,12},{14,15},{17,16},{18,... | collective-permute-start | bytes 3145736 | tf_op jit(solution)/shard_map/ppermute | solution.py:1071
  370.8 78.7 %collective-permute-start.49 = (bf16[256,2048]{1,0:T(8,128)(2,1)}, bf16[256,2048]{1,0:T(8,128)(2,1)S(1)}, u32[]{:S(2)}, u32[]{:S(2)}) collective-permute-start(bf16[256,2048]{1,0:T(8,128)(2,1)} %get-tuple-element.1881), channel_id=1, source_target_pairs={{0,1},{3,2},{4,5},{7,6},{8,9},{11,10},{12,13},{15,14},{16,17},{19,... | collective-permute-start | bytes 3145736 | tf_op jit(solution)/shard_map/ppermute | solution.py:1063
  403.7 72.4 %collective-permute-start.52 = (bf16[256,2048]{1,0:T(8,128)(2,1)S(1)}, bf16[256,2048]{1,0:T(8,128)(2,1)S(1)}, u32[]{:S(2)}, u32[]{:S(2)}) collective-permute-start(bf16[256,2048]{1,0:T(8,128)(2,1)S(1)} %get-tuple-element.1970), channel_id=1, source_target_pairs={{0,1},{3,2},{4,5},{7,6},{8,9},{11,10},{12,13},{15,14},{16,17},{19,... | collective-permute-start | bytes 3145736 | tf_op jit(solution)/shard_map/ppermute | solution.py:1063
  451.1 35.6 %collective-permute-start.53 = (bf16[256,2048]{1,0:T(8,128)(2,1)S(1)}, bf16[256,2048]{1,0:T(8,128)(2,1)S(1)}, u32[]{:S(2)}, u32[]{:S(2)}) collective-permute-start(bf16[256,2048]{1,0:T(8,128)(2,1)S(1)} %add_convert_fusion.10), channel_id=1, source_target_pairs={{1,2},{2,1},{5,6},{6,5},{9,10},{10,9},{13,14},{14,13},{17,18},{18,... | collective-permute-start | bytes 3145736 | tf_op jit(solution)/shard_map/ppermute | solution.py:1067
  451.8 48.1 %collective-permute-start.55 = (bf16[256,2048]{1,0:T(8,128)(2,1)}, bf16[256,2048]{1,0:T(8,128)(2,1)}, u32[]{:S(2)}, u32[]{:S(2)}) collective-permute-start(bf16[256,2048]{1,0:T(8,128)(2,1)} %get-tuple-element.2048), channel_id=1, source_target_pairs={{0,1},{3,2},{4,5},{7,6},{8,9},{11,10},{12,13},{15,14},{16,17},{19,... | collective-permute-start | bytes 3145736 | tf_op jit(solution)/shard_map/ppermute | solution.py:1063
  479.1 37.3 %collective-permute-start.58 = (bf16[256,2048]{1,0:T(8,128)(2,1)}, bf16[256,2048]{1,0:T(8,128)(2,1)}, u32[]{:S(2)}, u32[]{:S(2)}) collective-permute-start(bf16[256,2048]{1,0:T(8,128)(2,1)} %get-tuple-element.2102), channel_id=1, source_target_pairs={{0,1},{3,2},{4,5},{7,6},{8,9},{11,10},{12,13},{15,14},{16,17},{19,... | collective-permute-start | bytes 3145736 | tf_op jit(solution)/shard_map/ppermute | solution.py:1063
  533.6 44.9 %collective-permute-start.67 = (bf16[256,2048]{1,0:T(8,128)(2,1)S(1)}, bf16[256,2048]{1,0:T(8,128)(2,1)S(1)}, u32[]{:S(2)}, u32[]{:S(2)}) collective-permute-start(bf16[256,2048]{1,0:T(8,128)(2,1)S(1)} %add_convert_fusion.3.own), channel_id=1, source_target_pairs={{1,0},{2,3},{5,4},{6,7},{9,8},{10,11},{13,12},{14,15},{17,16},{18,... | collective-permute-start | bytes 3145736 | tf_op jit(solution)/shard_map/ppermute | solution.py:1071
  (90 other events, 1324.0 us)
Sparse Core Ops, SparseCore 0:
  48.4 107.1 all-gather.1
  364.4 124.9 reduce-scatter.2
  529.9 69.9 reduce-scatter.4

commit v2 on v1

--- a/solution.py
+++ b/solution.py
@@ -295,13 +295,14 @@
 SMALL = 128
 FTILE = 512
 MIB = 1024 * 1024
+COST = pl.CostEstimate(flops=1, bytes_accessed=1, transcendentals=0)
 GELU_C = 0.7978845608028654
 GELU_K = 0.044715
 
 PART, INWARD, SUM, ACROSS, OWN, OUTWARD, GAIN = range(7)
 ACTS, NORMED, FIRST, INV, WEIGHTS, MID, BACK, OUTPUT, INPUT = range(7, 16)
 UNIT_GRAD, UNIT_RESULT, PRE_GRAD, GATES_GRAD, CHANNEL_SUMS, PACKED = range(16, 22)
-SMALL_SUMS, GAIN_SUMS, GAIN_ONE, FORWARD, CARRIED = range(22, 27)
+SMALL_SUMS, GAIN_ONE, FORWARD, CARRIED = range(22, 26)
 TO_NORM, TO_MIDDLE, TO_OUTPUT, TO_INPUT = range(4)
 
 
@@ -311,6 +312,23 @@
 
 def params(megabytes):
     return pltpu.CompilerParams(vmem_limit_bytes=megabytes * MIB)
+
+
+def ordered(chain, body, args, in_specs, out_specs, out_shape, aliases, **options):
+    anywhere = pl.BlockSpec(memory_space=pl.ANY)
+    token = chain[0]
+    aliases = {source: target + 1 for source, target in aliases.items()}
+    aliases[len(args)] = 0
+    chain[0], *made = pl.pallas_call(
+        body,
+        in_specs=[*in_specs, anywhere],
+        out_specs=[anywhere, *out_specs],
+        out_shape=[pltpu.HBM(token.shape, token.dtype), *out_shape],
+        input_output_aliases=aliases,
+        cost_estimate=COST,
+        **options,
+    )(*args, hbm(token))
+    return made
 
 
 def nt_dot(left, right):
@@ -355,8 +373,8 @@
         outs, (ext, held, weight, in_sem, out_sem) = refs[-14:-5], refs[-5:]
         weight_out, outs = outs[0], outs[1:]
     else:
-        normed_ref, heads_ref, vec_ref, before_ref, weight = refs[:5]
-        outs, (ext, held) = refs[-10:-2], refs[-2:]
+        normed_ref, heads_ref, vec_ref, before_ref, weight, project_ref = refs[:6]
+        part_ref, outs, (ext, held) = refs[-11], refs[-10:-2], refs[-2:]
     gate_ref, branch_ref, mixed_ref, states_ref, rate_ref, inlet_ref, product_ref, tail_ref = outs
     block = pl.program_id(0) + first
     rows, channels = gate_ref.shape
@@ -433,7 +451,10 @@
         last = state[7:8]
     held[...] = jnp.broadcast_to(last, (8, channels))
     act, _ = gelu_parts(gate)
-    product_ref[...] = (states_ref[...] * act).astype(BF)
+    product = (states_ref[...] * act).astype(BF)
+    product_ref[...] = product
+    if not assemble:
+        part_ref[...] = nt_dot(product, project_ref[...]).astype(BF)
     ext[0:8] = ext[rows : rows + 8]
 
     @pl.when(pl.program_id(0) == pl.num_programs(0) - 1)
@@ -444,7 +465,9 @@
             keep.wait()
 
 
-def run_forward(starts, normed, heads, vec, before, weight, first, steps, kept=(), me=None):
+def run_forward(
+    chain, starts, normed, heads, vec, before, weight, first, steps, kept=(), me=None, project=None
+):
     tokens, width = normed.shape
     channels = before.shape[1]
     assemble = me is not None
@@ -476,29 +499,29 @@
             pltpu.SemaphoreType.DMA,
         ]
     else:
-        args = [starts, *main, hbm(weight)]
+        args = [starts, *main, hbm(weight), hbm(project)]
         in_specs = [smem] + main_specs + [pl.BlockSpec(weight.shape, whole)]
+        in_specs.append(pl.BlockSpec(project.shape, whole))
+        out_specs = [pl.BlockSpec((SMALL, width), lambda i: (i, 0))] + out_specs
+        out_shape = [jax.ShapeDtypeStruct((steps * SMALL, width), BF)] + out_shape
     aliases = {}
     for index, item in enumerate(kept):
-        aliases[len(args)] = index
+        aliases[len(args)] = index + 1
         in_specs.append(anywhere)
         args.append(hbm(item))
-    return pl.pallas_call(
+    return ordered(
+        chain,
         functools.partial(forward_kernel, starts.shape[1], first, assemble),
+        args,
+        in_specs,
+        out_specs,
+        out_shape,
+        aliases,
         grid=(steps,),
-        in_specs=in_specs,
-        out_specs=out_specs,
-        out_shape=out_shape,
-        input_output_aliases=aliases,
         scratch_shapes=scratch,
-        compiler_params=params(32),
-        cost_estimate=pl.CostEstimate(
-            flops=4 * steps * SMALL * channels * (width + channels),
-            bytes_accessed=30 * steps * SMALL * channels,
-            transcendentals=6 * steps * SMALL * channels,
-        ),
+        compiler_params=params(34),
         name="recurrent_forward",
-    )(*args)
+    )
 
 
 def backward_kernel(
@@ -613,7 +636,7 @@
 
 
 def run_backward(
-    starts, grad, outw, saved, heads, vec, hist, carried, first, count, kept=()
+    chain, starts, grad, outw, saved, heads, vec, hist, carried, first, count, kept=()
 ):
     tokens, width = grad.shape
     channels = hist.shape[1]
@@ -646,17 +669,19 @@
         aliases[len(args)] = index
         in_specs.append(pl.BlockSpec(memory_space=pl.ANY))
         args.append(hbm(item))
-    return pl.pallas_call(
+    return ordered(
+        chain,
         functools.partial(backward_kernel, starts.shape[1], first, count),
-        grid=(count,),
-        in_specs=in_specs,
-        out_specs=[wide, wide, pl.BlockSpec(carried.shape, whole)],
-        out_shape=[
+        args,
+        in_specs,
+        [wide, wide, pl.BlockSpec(carried.shape, whole)],
+        [
             pltpu.HBM((tokens, 2 * channels), BF),
             pltpu.HBM((tokens, 2 * channels), BF),
             jax.ShapeDtypeStruct(carried.shape, F32),
         ],
-        input_output_aliases=aliases,
+        aliases,
+        grid=(count,),
         scratch_shapes=[
             pltpu.VMEM((SMALL + 8, channels), F32),
             pltpu.VMEM((SMALL + 16, channels), F32),
@@ -664,20 +689,17 @@
             pltpu.VMEM((SMALL, channels), F32),
             pltpu.VMEM((16, channels), F32),
         ],
-        compiler_params=params(32),
-        cost_estimate=pl.CostEstimate(
-            flops=2 * count * SMALL * channels * (width + 2 * channels),
-            bytes_accessed=34 * count * SMALL * channels,
-            transcendentals=6 * count * SMALL * channels,
-        ),
+        compiler_params=params(28),
         name="recurrent_backward",
-    )(*args)
-
-
-def ffn_kernel(part, units, zed_ref, own, came, act_ref, gain_ref, cot_ref, weight_ref, *refs):
+    )
+
+
+def ffn_kernel(part, units, pieces, zed_ref, *refs):
+    owns, cames, refs = refs[:pieces], refs[pieces : 2 * pieces], refs[2 * pieces :]
+    act_ref, gain_ref, cot_ref, weight_ref = refs[:4]
     outs, (weight, normed, acts, in_sem, out_sem) = refs[-10:-5], refs[-5:]
     acts_out, normed_out, first_out, inv_out, back_out = outs
-    rows, width = own.shape
+    rows, width = act_ref.shape
     tiles = units // FTILE
     spans = [
         [slice(k * units + t * FTILE, k * units + (t + 1) * FTILE) for k in range(3)]
@@ -696,13 +718,16 @@
     ]
     for copy in sum(copies, []):
         copy.start()
-    first = pick(zed_ref, own, came)
-    first_out[...] = first.astype(BF)
-    middle = act_ref[...] + first
-    mean = jnp.sum(middle * middle, axis=1, keepdims=True) / width
-    inv = lax.rsqrt(mean + EPS)
-    inv_out[...] = jnp.broadcast_to(inv, inv_out.shape)
-    normed[...] = (middle * inv * gain_ref[1:2]).astype(BF)
+    tall = rows // pieces
+    for index in range(pieces):
+        span = slice(index * tall, (index + 1) * tall)
+        first = pick(zed_ref, owns[index], cames[index])
+        first_out[span] = first.astype(BF)
+        middle = act_ref[span] + first
+        mean = jnp.sum(middle * middle, axis=1, keepdims=True) / width
+        inv = lax.rsqrt(mean + EPS)
+        inv_out[span] = jnp.broadcast_to(inv, (tall, inv_out.shape[1]))
+        normed[span] = (middle * inv * gain_ref[1:2]).astype(BF)
     out_rows = pl.ds(part * rows, rows)
     keep = [
         pltpu.make_async_copy(normed, normed_out.at[out_rows], out_sem.at[0]),
@@ -728,48 +753,50 @@
         copy.wait()
 
 
-def run_ffn(part, zed, own, came, flat, gains, cot, weights, kept):
+def run_ffn(chain, part, zed, owns, cames, flat, gains, cot, weights, kept):
     tokens, width = cot.shape
     units = weights.shape[1] // 3
-    rows = own.shape[0]
+    pieces = len(owns)
+    rows = pieces * owns[0].shape[0]
     tiles = units // FTILE
     anywhere = pl.BlockSpec(memory_space=pl.ANY)
     whole = lambda i: (0, 0)
     held = lambda i: (part, 0)
     in_specs = [
         pl.BlockSpec(memory_space=pltpu.SMEM),
-        pl.BlockSpec(own.shape, whole),
-        pl.BlockSpec(own.shape, whole),
+        *[pl.BlockSpec(owns[0].shape, whole)] * (2 * pieces),
         pl.BlockSpec((rows, width), held),
         pl.BlockSpec(gains.shape, whole),
         pl.BlockSpec((rows, width), held),
         anywhere,
     ]
-    args = [zed, own, came, hbm(flat), gains, hbm(cot), hbm(weights)]
+    args = [zed, *map(hbm, owns), *map(hbm, cames), hbm(flat), gains, hbm(cot), hbm(weights)]
     aliases = {}
     for index, item in enumerate(kept):
         aliases[len(args)] = index
         in_specs.append(anywhere)
         args.append(hbm(item))
-    return pl.pallas_call(
-        functools.partial(ffn_kernel, part, units),
-        grid=(1,),
-        in_specs=in_specs,
-        out_specs=[
+    return ordered(
+        chain,
+        functools.partial(ffn_kernel, part, units, pieces),
+        args,
+        in_specs,
+        [
             anywhere,
             anywhere,
             pl.BlockSpec((rows, width), held),
             pl.BlockSpec((rows, 128), held),
             pl.BlockSpec((rows, width), whole),
         ],
-        out_shape=[
+        [
             pltpu.HBM((tokens, 3 * units), BF),
             pltpu.HBM((tokens, width), BF),
             pltpu.HBM((tokens, width), BF),
             pltpu.HBM((tokens, 128), F32),
             jax.ShapeDtypeStruct((rows, width), BF),
         ],
-        input_output_aliases=aliases,
+        aliases,
+        grid=(1,),
         scratch_shapes=[
             pltpu.VMEM(weights.shape, BF),
             pltpu.VMEM((rows, width), BF),
@@ -777,49 +804,59 @@
             pltpu.SemaphoreType.DMA((3 * tiles,)),
             pltpu.SemaphoreType.DMA((2,)),
         ],
-        compiler_params=params(46),
-        cost_estimate=pl.CostEstimate(
-            flops=10 * rows * width * units,
-            bytes_accessed=2 * weights.size,
-            transcendentals=rows * units,
-        ),
+        compiler_params=params(42),
         name="ffn_chunk",
-    )(*args)
-
-
-def nt_kernel(left, right, *outs):
+    )
+
+
+def nt_kernel(pieces, weighed, left, right, *refs):
     total = nt_dot(left[...], right[...])
-    rows = outs[0].shape[0]
-    for index, out in enumerate(outs):
-        out[...] = total[index * rows : (index + 1) * rows].astype(out.dtype)
-
-
-def run_nt(left, first, pieces, left_col, right, right_col, depth):
+    outs = refs[-pieces:]
+    if weighed:
+        outs, sums = refs[-pieces - 1 : -1], refs[-1]
+        sums[...] = jnp.zeros(sums.shape, F32)
+        sums[0:1] = jnp.sum(total * refs[0][...].astype(F32), axis=0, keepdims=True)
+    row = 0
+    for out in outs:
+        out[...] = total[row : row + out.shape[0]].astype(out.dtype)
+        row += out.shape[0]
+
+
+def run_nt(chain, left, first, sizes, left_col, right, right_col, depth, weigh=None):
     width = right.shape[0]
-    rows = pieces * CHUNK
-    tile = 1024 if pieces == 1 else 512
-    return pl.pallas_call(
-        nt_kernel,
+    rows = sum(sizes)
+    tile = 1024 if rows <= CHUNK else 512
+    args = [hbm(left), hbm(right)]
+    in_specs = [
+        pl.BlockSpec((pl.Element(rows), pl.Element(depth)), lambda i: (first, left_col * depth)),
+        pl.BlockSpec((tile, depth), lambda i: (i, right_col)),
+    ]
+    out_specs = [pl.BlockSpec((size, tile), lambda i: (0, i)) for size in sizes]
+    out_shape = [jax.ShapeDtypeStruct((size, width), BF) for size in sizes]
+    if weigh is not None:
+        args.append(hbm(weigh))
+        in_specs.append(pl.BlockSpec((rows, tile), lambda i: (first // rows, i)))
+        out_specs.append(pl.BlockSpec((8, tile), lambda i: (0, i)))
+        out_shape.append(jax.ShapeDtypeStruct((8, width), F32))
+    return ordered(
+        chain,
+        functools.partial(nt_kernel, len(sizes), weigh is not None),
+        args,
+        in_specs,
+        out_specs,
+        out_shape,
+        {},
         grid=(width // tile,),
-        in_specs=[
-            pl.BlockSpec((pl.Element(rows), pl.Element(depth)), lambda i: (first, left_col * depth)),
-            pl.BlockSpec((tile, depth), lambda i: (i, right_col)),
-        ],
-        out_specs=[pl.BlockSpec((CHUNK, tile), lambda i: (0, i))] * pieces,
-        out_shape=[jax.ShapeDtypeStruct((CHUNK, width), BF)] * pieces,
-        compiler_params=params(32),
-        cost_estimate=pl.CostEstimate(
-            flops=2 * rows * width * depth, bytes_accessed=4 * width * depth, transcendentals=0
-        ),
+        compiler_params=params(24),
         name="rows_by_rows",
-    )(hbm(left), hbm(right))
+    )
 
 
 def tn_kernel(left, right, *refs):
     refs[-1][...] = contract_rows(left[...], right[...]).astype(BF)
 
 
-def run_weight_grad(left, right, column, tiles, kept, total):
+def run_weight_grad(chain, left, right, column, tiles, kept, total):
     tokens, width = left.shape
     in_specs = [
         pl.BlockSpec((tokens, width), lambda j: (0, 0)),
@@ -829,21 +866,18 @@
     if kept is not None:
         in_specs.append(pl.BlockSpec(memory_space=pl.ANY))
         args.append(hbm(kept))
-    return pl.pallas_call(
+    return ordered(
+        chain,
         tn_kernel,
+        args,
+        in_specs,
+        [pl.BlockSpec((width, FTILE), lambda j: (0, column + j))],
+        [pltpu.HBM((width, total), BF)],
+        {} if kept is None else {2: 0},
         grid=(tiles,),
-        in_specs=in_specs,
-        out_specs=pl.BlockSpec((width, FTILE), lambda j: (0, column + j)),
-        out_shape=pltpu.HBM((width, total), BF),
-        input_output_aliases={} if kept is None else {2: 0},
-        compiler_params=params(36),
-        cost_estimate=pl.CostEstimate(
-            flops=2 * tokens * width * tiles * FTILE,
-            bytes_accessed=2 * tokens * (width + tiles * FTILE) + 2 * width * tiles * FTILE,
-            transcendentals=0,
-        ),
+        compiler_params=params(26),
         name="unit_weight_grad",
-    )(*args)
+    )
 
 
 def packed_kernel(left, right, *refs):
@@ -855,7 +889,7 @@
         out[0, index * rows : (index + 1) * rows] = total[:, span]
 
 
-def run_packed_grad(left, right, place, kept, shape):
+def run_packed_grad(chain, left, right, place, kept, shape):
     tokens, width = left.shape
     share = width // 8
     tall = share * (right.shape[1] // shape[2])
@@ -867,24 +901,22 @@
     if kept is not None:
         in_specs.append(pl.BlockSpec(memory_space=pl.ANY))
         args.append(hbm(kept))
-    return pl.pallas_call(
+    return ordered(
+        chain,
         packed_kernel,
+        args,
+        in_specs,
+        [pl.BlockSpec((1, tall, shape[2]), lambda d: (d, place, 0))],
+        [pltpu.HBM(shape, BF)],
+        {} if kept is None else {2: 0},
         grid=(8,),
-        in_specs=in_specs,
-        out_specs=pl.BlockSpec((1, tall, shape[2]), lambda d: (d, place, 0)),
-        out_shape=pltpu.HBM(shape, BF),
-        input_output_aliases={} if kept is None else {2: 0},
-        compiler_params=params(32),
-        cost_estimate=pl.CostEstimate(
-            flops=2 * tokens * width * right.shape[1],
-            bytes_accessed=2 * (tokens + right.shape[1]) * width,
-            transcendentals=0,
-        ),
+        compiler_params=params(18),
         name="branch_weight_grad",
-    )(*args)
-
-
-def thin_kernel(grads, mixed, kept, out, total):
+    )
+
+
+def thin_kernel(grads, mixed, *refs):
+    out, total = refs[-2:]
     which = pl.program_id(0)
     channels = mixed.shape[1]
     product = contract_rows(grads[...], mixed[...])
@@ -904,29 +936,26 @@
             out[share] = jnp.concatenate(parts, 0).astype(BF)
 
 
-def run_thin_grad(grads, mixed, packed):
+def run_thin_grad(chain, grads, mixed, packed):
     tokens, channels = mixed.shape
-    place = packed.shape[1] // 48 - 1
-    return pl.pallas_call(
+    place = (packed.shape[1] - 64) // 48
+    return ordered(
+        chain,
         thin_kernel,
-        grid=(2,),
-        in_specs=[
+        [hbm(grads), hbm(mixed), hbm(packed)],
+        [
             pl.BlockSpec((tokens, channels), lambda i: (0, i)),
             pl.BlockSpec((tokens, channels), lambda i: (0, 0)),
             pl.BlockSpec(memory_space=pl.ANY),
         ],
-        out_specs=pl.BlockSpec((8, 48, channels), lambda i: (0, place, 0)),
-        out_shape=pltpu.HBM(packed.shape, BF),
+        [pl.BlockSpec((8, 48, channels), lambda i: (0, place, 0))],
+        [pltpu.HBM(packed.shape, BF)],
+        {2: 0},
+        grid=(2,),
         scratch_shapes=[pltpu.VMEM((2, HEAD, channels), F32)],
-        input_output_aliases={2: 0},
-        compiler_params=params(32),
-        cost_estimate=pl.CostEstimate(
-            flops=4 * tokens * channels * channels,
-            bytes_accessed=8 * tokens * channels,
-            transcendentals=0,
-        ),
+        compiler_params=params(18),
         name="gate_weight_grad",
-    )(hbm(grads), hbm(mixed), hbm(packed))
+    )
 
 
 def pick(zed_ref, own, came):
@@ -964,7 +993,7 @@
     refs[-1][...] = cot[...] + (back[...].astype(F32) + through)
 
 
-def run_rows(body, name, zed, own, came, others, first, outs, kept):
+def run_rows(chain, body, name, zed, own, came, others, first, outs, kept):
     rows, width = own.shape
     step = 64
     by_rows = lambda i: (i + first // step, 0)
@@ -985,30 +1014,122 @@
         aliases[len(args)] = index
         in_specs.append(pl.BlockSpec(memory_space=pl.ANY))
         args.append(hbm(item))
-    return pl.pallas_call(
+    return ordered(
+        chain,
         body,
+        args,
+        in_specs,
+        [spec(item.shape) for item in outs],
+        outs,
+        aliases,
         grid=(rows // step,),
-        in_specs=in_specs,
-        out_specs=[spec(item.shape) for item in outs],
-        out_shape=outs,
-        input_output_aliases=aliases,
+        compiler_params=params(16),
+        name=name,
+    )
+
+
+def small_kernel(zed_ref, own, came, gains, *refs):
+    carried, out = refs[-4], refs[-1]
+    channels = carried.shape[1]
+    out[...] = jnp.zeros(out.shape, F32)
+    out[0:1] = pick(zed_ref, own, came)[0:1] * gains[2:3]
+    total = refs[0][0:1]
+    for item in refs[1:-4]:
+        total = total + item[0:1]
+    out[1:2] = total * gains[3:4]
+    out[8:16, :channels] = carried[24:32]
+
+
+def run_small(chain, zed, own, came, gains, parts, carried):
+    rows, width = own.shape
+    whole = lambda i: (0, 0)
+    last = pl.BlockSpec((16, width), lambda i: (rows // 16 - 1, 0))
+    others = [gains, *parts, carried]
+    return ordered(
+        chain,
+        small_kernel,
+        [zed, own, came, *others],
+        [pl.BlockSpec(memory_space=pltpu.SMEM), last, last]
+        + [pl.BlockSpec(item.shape, whole) for item in others],
+        [pl.BlockSpec((16, width), whole)],
+        [jax.ShapeDtypeStruct((16, width), F32)],
+        {},
+        grid=(1,),
+        compiler_params=params(16),
+        name="small_sums",
+    )
+
+
+def append_kernel(value, extra, *refs):
+    out = refs[-1]
+    rows = value.shape[0]
+    out[:rows] = value[...]
+    low = jnp.zeros((16, value.shape[1]), F32)
+    first = lax.broadcasted_iota(jnp.int32, (16, 1), 0) == 0
+    out[rows:] = jnp.where(first, extra[0:1], low).astype(BF)
+
+
+def run_append(chain, value, extra):
+    rows, width = value.shape
+    whole = lambda i: (0, 0)
+    (made,) = ordered(
+        chain,
+        append_kernel,
+        [value, extra],
+        [pl.BlockSpec(value.shape, whole), pl.BlockSpec(extra.shape, whole)],
+        [pl.BlockSpec((rows + 16, width), whole)],
+        [jax.ShapeDtypeStruct((rows + 16, width), BF)],
+        {},
+        grid=(1,),
         compiler_params=params(24),
-        cost_estimate=pl.CostEstimate(
-            flops=20 * rows * width, bytes_accessed=20 * rows * width, transcendentals=0
-        ),
-        name=name,
-    )(*args)
+        name="append",
+    )
+    return made
+
+
+def widen_kernel(value, *refs):
+    one, two, three = refs[-3:]
+    units = one.shape[1]
+    one[...] = value[:, :units].astype(F32)
+    two[...] = value[:, units : 2 * units].astype(F32)
+    three[...] = value[:, 2 * units :].astype(F32).T
+
+
+def run_widen(chain, value):
+    rows, units = value.shape[0], value.shape[1] // 3
+    shapes = [(rows, units), (rows, units), (units, rows)]
+    whole = lambda i: (0, 0)
+    return ordered(
+        chain,
+        widen_kernel,
+        [hbm(value)],
+        [pl.BlockSpec(value.shape, whole)],
+        [pl.BlockSpec(shape, whole) for shape in shapes],
+        [pltpu.HBM(shape, F32) for shape in shapes],
+        {},
+        grid=(1,),
+        compiler_params=params(32),
+        name="widen",
+    )
 
 
 def swap_dp(value, bit):
     return lax.ppermute(value, "dp", [(i, i ^ bit) for i in range(8)])
 
 
-def gather_pair(one, two):
-    one2, two4 = swap_dp(one, 2), swap_dp(two, 4)
-    one4, one6 = swap_dp(one, 4), swap_dp(one2, 4)
-    two2, two6 = swap_dp(two, 2), swap_dp(two4, 2)
-    return jnp.stack([one, one2, one4, one6]), jnp.stack([two, two2, two4, two6])
+def swap_own(own):
+    first = swap_dp(own[0], 2), swap_dp(own[1], 4)
+    return first, (swap_dp(own[0], 4), swap_dp(own[1], 2))
+
+
+def swap_got(got):
+    return swap_dp(got[0], 4), swap_dp(got[1], 2)
+
+
+def stack_pair(own, got, far):
+    first, second = got
+    one = jnp.stack([own[0], first[0], second[0], far[0]])
+    return one, jnp.stack([own[1], second[1], first[1], far[1]])
 
 
 def natural_kernel(me_ref, *refs):
@@ -1040,23 +1161,15 @@
         out_shape=jax.ShapeDtypeStruct((16 * rows, columns), pieces[0].dtype),
         scratch_shapes=[pltpu.SemaphoreType.DMA((16,))],
         compiler_params=params(16),
-        cost_estimate=pl.CostEstimate(
-            flops=0, bytes_accessed=64 * rows * columns, transcendentals=0
-        ),
+        cost_estimate=COST,
         name="natural_order",
     )(me, *pieces)
 
 
-def gather_small(value):
-    me = lax.axis_index("dp")
-    held = value[None]
-    for bit in (1, 2, 4):
-        other = swap_dp(held, bit)
-        high = (me & bit) != 0
-        first = jnp.where(high, other, held)
-        second = jnp.where(high, held, other)
-        held = jnp.concatenate([first, second], 0)
-    return held
+def widen(held, bit):
+    other = swap_dp(held, bit)
+    high = (lax.axis_index("dp") & bit) != 0
+    return jnp.stack([jnp.where(high, other, held), jnp.where(high, held, other)])
 
 
 def inward(value):
@@ -1071,8 +1184,28 @@
     return lax.ppermute(value, "tensor", [(1, 0), (2, 3)])
 
 
-def add_low(one, two):
-    return (one.astype(F32) + two.astype(F32)).astype(BF)
+def add_kernel(one, two, *refs):
+    out = refs[-1]
+    out[...] = (one[...].astype(F32) + two[...].astype(F32)).astype(out.dtype)
+
+
+def run_add(chain, one, two):
+    rows, width = one.shape
+    step = rows if rows % 64 else 64
+    spec = pl.BlockSpec((step, width), lambda i: (i, 0))
+    (made,) = ordered(
+        chain,
+        add_kernel,
+        [one, two],
+        [spec, spec],
+        [spec],
+        [jax.ShapeDtypeStruct(one.shape, one.dtype)],
+        {},
+        grid=(rows // step,),
+        compiler_params=params(16),
+        name="add",
+    )
+    return made
 
 
 def line_device(
@@ -1107,18 +1240,14 @@
     count = channels // HEAD
     chunks = length // CHUNK
 
-    near = gather_pair(gelu_branch, lru_branch)
+    ffn_own = jnp.concatenate([ffn_gate, ffn_value, ffn_down.T], 1)
+    out_own = out_weight.T
+    out_half = out_own.shape[0] // 2
+    out_own = (out_own[:out_half], out_own[out_half:])
     thin = jnp.stack([recur_weight.T, inlet_weight.T])
-    thin_full = gather_small(thin).transpose(1, 0, 2, 3).reshape(2, HEAD, channels)
     owner = jnp.arange(channels) // HEAD
     same = owner[:, None] == owner[None, :]
-    heads = jnp.where(same[None], jnp.tile(thin_full, (1, count, 1)), 0).reshape(
-        2 * channels, channels
-    )
-    ffn_own = jnp.concatenate([ffn_gate, ffn_value, ffn_down.T], 1)
-    out_own = out_weight.T
     inv_one = lax.rsqrt(jnp.mean(flat * flat, axis=-1, keepdims=True) + EPS)
-    normed = (flat * inv_one * gain_one).astype(BF)
     gains = jnp.stack([gain_one, gain_two, 1.0 / gain_one, 1.0 / gain_two] + [gain_one] * 4)
     decay = 8.0 * jax.nn.softplus(-decay_param)
     vec = jnp.concatenate(
@@ -1135,41 +1264,61 @@
     )
     hist = jnp.concatenate([jnp.zeros((5, channels), F32), conv_state[0]], 0)
     before = jnp.concatenate([hist, jnp.broadcast_to(recur_state, (8, channels))], 0)
-    near, heads, ffn_own, out_own, inv_one, normed, vec, before = lax.optimization_barrier(
-        (near, heads, ffn_own, out_own, inv_one, normed, vec, before)
-    )
+    own = (gelu_branch, lru_branch)
+    own, got, thin, inv_one, vec, before = lax.optimization_barrier(
+        (own, swap_own(own), widen(thin, 4), inv_one, vec, before)
+    )
+    normed = (flat * inv_one * gain_one).astype(BF)
+    corner = swap_got(got[0])
+    out_got = swap_own(out_own)
+    corner, out_got, thin, normed, ffn_own = lax.optimization_barrier(
+        (corner, out_got, widen(thin, 2), normed, ffn_own)
+    )
+    ffn_full = lax.all_gather(ffn_own, "dp", axis=0, tiled=True)
+    near = stack_pair(own, got, corner)
     far = tuple(swap_dp(item, 1) for item in near)
-    ffn_full = lax.all_gather(ffn_own, "dp", axis=0, tiled=True)
-    far, out_own = lax.optimization_barrier((far, out_own))
-    out_half = out_own.shape[0] // 2
-    out_near = gather_pair(out_own[:out_half], out_own[out_half:])
+    out_near = stack_pair(out_own, out_got, swap_got(out_got[0]))
+    near, far, out_near, thin = lax.optimization_barrier((near, far, out_near, widen(thin, 1)))
+    thin_full = thin.transpose(2, 1, 0, 3, 4, 5).reshape(8, 2, HEAD // 8, channels)
+    thin_full = thin_full.transpose(1, 0, 2, 3).reshape(2, HEAD, channels)
+    heads = jnp.where(same[None], jnp.tile(thin_full, (1, count, 1)), 0).reshape(
+        2 * channels, channels
+    )
+
+    blocks = CHUNK // SMALL
+    chain = [jnp.zeros((8, 128), F32)]
+    branch_full, *made = run_forward(
+        chain, doc_starts, normed, heads, vec, before, near + far, 0, blocks, me=me
+    )
     out_far = tuple(swap_dp(item, 1) for item in out_near)
-
-    blocks = CHUNK // SMALL
-    branch_full, *made = run_forward(
-        doc_starts, normed, heads, vec, before, near + far, 0, blocks, me=me
-    )
     out_full = natural_order(out_near + out_far, me)
-    cot_low = incoming.astype(BF)
     wide_inv = jnp.broadcast_to(inv_one, (length, 128))
 
-    jobs = [(kind, c) for kind in (TO_NORM, TO_MIDDLE, TO_OUTPUT) for c in range(chunks)]
-    jobs += [(TO_INPUT, c) for c in reversed(range(chunks))]
-    total_jobs = len(jobs)
+    half = CHUNK // 2
+    ahead = [(c * CHUNK, CHUNK) for c in range(chunks)]
+    cut = [(0, half), (half, half)]
+    jobs = [(TO_NORM, *rows) for rows in cut + ahead[1:]]
+    second = len(jobs)
+    jobs += [(TO_MIDDLE, *rows) for rows in ahead]
+    third = len(jobs)
+    jobs += [(TO_OUTPUT, *rows) for rows in ahead]
+    fourth = len(jobs)
+    halves = [(row, half) for row in range(0, 2 * CHUNK, half)]
+    jobs += [(TO_INPUT, *rows) for rows in ahead[:1:-1] + halves[::-1]]
     live = {(FORWARD, index): item for index, item in enumerate(made)}
-    flying = {}
-    unit_result = rec_result = None
-
-    def part_one(c):
-        rows = live[FORWARD, 6][c * CHUNK : (c + 1) * CHUNK]
-        return nt_dot(rows, out_full).astype(BF)
-
-    def tie(arrived):
-        if arrived in flying:
-            live[arrived] = flying.pop(arrived)
-        names = sorted(live)
-        values = lax.optimization_barrier(tuple(live[name] for name in names))
-        live.update(zip(names, values))
+
+    def send(job):
+        part, chain[0] = lax.optimization_barrier((live[PART, job], chain[0]))
+        live[PART, job] = part
+        live[INWARD, job] = inward(part)
+
+    def summed(job):
+        live[SUM, job] = run_add(chain, live.pop((PART, job)), live.pop((INWARD, job)))
+        live[ACROSS, job] = across(live[SUM, job])
+
+    def total(job):
+        live[OWN, job] = run_add(chain, live.pop((SUM, job)), live.pop((ACROSS, job)))
+        live[OUTWARD, job] = outward(live[OWN, job])
 
     def one(kind):
         return live[kind, 0]
@@ -1181,21 +1330,73 @@
         for name, value in zip(names, values):
             live[name, 0] = value
 
-    def small_step(step):
-        if 0 <= step < 3:
-            live[SMALL_SUMS, 0] = one(SMALL_SUMS) + swap_dp(one(SMALL_SUMS), 1 << step)
-        if step == 3:
-            live[GAIN_SUMS, 0] = one(SMALL_SUMS)[8 * channels :]
-        if 3 <= step < 5:
-            pairs = [(i, i ^ (step - 2)) for i in range(4)]
-            live[GAIN_SUMS, 0] = one(GAIN_SUMS) + lax.ppermute(one(GAIN_SUMS), "tensor", pairs)
-
-    def send_in(job):
-        if (PART, job) in live and (INWARD, job) not in flying:
-            flying[INWARD, job] = inward(live[PART, job])
-
-    def backward(first, count):
-        return run_backward(
+    def forward(c):
+        live[PART, c + 1], *made = run_forward(
+            chain,
+            doc_starts,
+            normed,
+            heads,
+            vec,
+            live[FORWARD, 7],
+            branch_full,
+            c * blocks,
+            blocks,
+            [live[FORWARD, index] for index in range(7)],
+            project=out_full,
+        )
+        for index, item in enumerate(made):
+            live[FORWARD, index] = item
+
+    def ffn(c, *from_jobs):
+        names = (ACTS, NORMED, FIRST, INV)
+        *made, live[PART, second + c] = run_ffn(
+            chain,
+            c,
+            zed,
+            [live.pop((OWN, job)) for job in from_jobs],
+            [live.pop((OUTWARD, job)) for job in from_jobs],
+            flat,
+            gains,
+            cot_low,
+            one(WEIGHTS),
+            kept(*names),
+        )
+        keep(names, made)
+        send(second + c)
+
+    def middle(c):
+        job = second + c
+        low = pltpu.HBM((length, width), BF)
+        *made, live[GAIN, c] = run_rows(
+            chain,
+            middle_kernel,
+            "middle_grad",
+            zed,
+            live.pop((OWN, job)),
+            live.pop((OUTWARD, job)),
+            [one(NORMED), one(INV), gains, incoming],
+            c * CHUNK,
+            [low, low, jax.ShapeDtypeStruct((8, width), F32)],
+            kept(MID, BACK),
+        )
+        keep((MID, BACK), made)
+
+    def rows_out(job):
+        if jobs[job][0] == TO_OUTPUT:
+            name, body, label = OUTPUT, output_kernel, "output"
+            others = [one(FIRST), flat]
+        else:
+            name, body, label = INPUT, input_kernel, "input_grad"
+            others = [normed, wide_inv, gains, one(BACK), incoming]
+        wide = [pltpu.HBM((length, width), F32)]
+        whole = (zed, live.pop((OWN, job)), live.pop((OUTWARD, job)))
+        made = run_rows(chain, body, label, *whole, others, jobs[job][1], wide, kept(name))
+        keep((name,), made)
+
+    def backward(c):
+        names = (PRE_GRAD, GATES_GRAD, CARRIED)
+        made = run_backward(
+            chain,
             doc_starts,
             one(MID),
             out_full,
@@ -1204,154 +1405,192 @@
             vec,
             hist,
             one(CARRIED),
-            first,
-            count,
-            kept(PRE_GRAD, GATES_GRAD),
+            c * blocks,
+            2 * blocks,
+            kept(*names[:2]),
         )
-
-    live[PART, 0] = part_one(0)
+        keep(names, made)
+        sizes = [CHUNK, CHUNK] if c else [half] * 4
+        *parts, live[GAIN_ONE, c] = run_nt(
+            chain, one(PRE_GRAD), c * CHUNK, sizes, 0, branch_full, 0, 2 * channels, normed
+        )
+        for index, part in enumerate(reversed(parts)):
+            live[PART, fourth + chunks - 2 - c + index] = part
+
+    def ahead_parts(first, sizes):
+        made = run_nt(chain, one(ACTS), first, sizes, 2, one(WEIGHTS), 2, units)
+        for index, part in enumerate(made):
+            live[PART, third + first // CHUNK + index] = part
+
+    def unit_grad(which):
+        (live[UNIT_GRAD, 0],) = run_weight_grad(
+            chain,
+            one(NORMED) if which < 2 else cot_low,
+            one(ACTS),
+            which * tiles,
+            tiles,
+            live.get((UNIT_GRAD, 0)),
+            3 * units,
+        )
+
+    def scatter(kind):
+        live[kind, 0], chain[0] = lax.optimization_barrier((live[kind, 0], chain[0]))
+        return lax.psum_scatter(live.pop((kind, 0)), "dp", scatter_dimension=0, tiled=True)
+
+    def pack(*args):
+        (live[PACKED, 0],) = run_packed_grad(chain, *args, live.get((PACKED, 0)), shape)
+
+    def small_pack(job):
+        (live[SMALL_SUMS, 0],) = run_small(
+            chain,
+            zed,
+            live[OWN, job],
+            live[OUTWARD, job],
+            gains,
+            [live.pop((GAIN, c)) for c in range(chunks)],
+            live.pop((CARRIED, 0)),
+        )
+
+    def small_start(step):
+        live[SMALL_SUMS, 1] = swap_dp(one(SMALL_SUMS), 1 << step)
+
+    def small_end():
+        live[SMALL_SUMS, 0] = run_add(chain, one(SMALL_SUMS), live.pop((SMALL_SUMS, 1)))
+
+    def arrived(job, kind=OUTWARD):
+        value, chain[0] = lax.optimization_barrier((live[kind, job], chain[0]))
+        live[kind, job] = value
+
+    def drain():
+        names = [name for name in live if name[0] in (INWARD, ACROSS, OUTWARD)]
+        values, chain[0] = lax.optimization_barrier((tuple(live[n] for n in names), chain[0]))
+        live.update(zip(names, values))
+
+    tiles = units // FTILE
+    shape = (8, 3 * width // 8 + 64, channels)
+    live[WEIGHTS, 0] = ffn_full
     live[CARRIED, 0] = jnp.zeros((32, channels), F32)
-    shape = (8, 3 * width // 8 + 48, channels)
-    tiles = units // FTILE
-    second, third, fourth = chunks, 2 * chunks, 3 * chunks
-    for slot in range(total_jobs + 4):
-        if slot == total_jobs:
-            live[UNIT_RESULT, 0] = unit_result
-        tie((INWARD, slot - 2))
-        small_step(3 * (slot - total_jobs))
-        job = slot - 2
-        if (INWARD, job) in live:
-            live[SUM, job] = add_low(live.pop((PART, job)), live.pop((INWARD, job)))
-            flying[ACROSS, job] = across(live[SUM, job])
-        if slot == third:
-            (live[PART, slot],) = run_nt(one(ACTS), 0, 1, 2, one(WEIGHTS), 2, units)
-        send_in(slot)
-
-        tie((ACROSS, slot - 3))
-        small_step(3 * (slot - total_jobs) + 1)
-        job = slot - 3
-        if (ACROSS, job) in live:
-            live[OWN, job] = add_low(live.pop((SUM, job)), live.pop((ACROSS, job)))
-            flying[OUTWARD, job] = outward(live[OWN, job])
-        if slot == second:
-            live[WEIGHTS, 0] = ffn_full
-
-        tie((OUTWARD, slot - 4))
-        small_step(3 * (slot - total_jobs) + 2)
-        job = slot - 4
-        if (OUTWARD, job) in live:
-            kind, c = jobs[job]
-            whole = (zed, live.pop((OWN, job)), live.pop((OUTWARD, job)))
-            first = c * CHUNK
-            if kind == TO_NORM:
-                names = (ACTS, NORMED, FIRST, INV)
-                *made, live[PART, slot] = run_ffn(
-                    c, *whole, flat, gains, cot_low, one(WEIGHTS), kept(*names)
-                )
-                keep(names, made)
-                send_in(slot)
-            elif kind == TO_MIDDLE:
-                low = pltpu.HBM((length, width), BF)
-                *made, live[GAIN, c] = run_rows(
-                    middle_kernel,
-                    "middle_grad",
-                    *whole,
-                    [one(NORMED), one(INV), gains, incoming],
-                    first,
-                    [low, low, jax.ShapeDtypeStruct((8, width), F32)],
-                    kept(MID, BACK),
-                )
-                keep((MID, BACK), made)
-            else:
-                if kind == TO_OUTPUT:
-                    name, body, label = OUTPUT, output_kernel, "output"
-                    others = [one(FIRST), flat]
-                else:
-                    name, body, label = INPUT, input_kernel, "input_grad"
-                    others = [normed, wide_inv, gains, one(BACK), incoming]
-                wide = [pltpu.HBM((length, width), F32)]
-                keep((name,), run_rows(body, label, *whole, others, first, wide, kept(name)))
-
-        if slot < 2:
-            start = blocks if slot == 0 else 2 * blocks
-            steps = blocks if slot == 0 else length // SMALL - 2 * blocks
-            made = run_forward(
-                doc_starts,
-                normed,
-                heads,
-                vec,
-                live[FORWARD, 7],
-                branch_full,
-                start,
-                steps,
-                [live[FORWARD, index] for index in range(7)],
-            )
-            for index, item in enumerate(made):
-                live[FORWARD, index] = item
-            for c in range(1, 2) if slot == 0 else range(2, chunks):
-                live[PART, c] = part_one(c)
-        if slot == third:
-            made = run_nt(one(ACTS), CHUNK, chunks - 1, 2, live.pop((WEIGHTS, 0)), 2, units)
-            for c in range(1, chunks):
-                live[PART, third + c] = made[c - 1]
-        if third <= slot < third + 3:
-            which = slot - third
-            live[UNIT_GRAD, 0] = run_weight_grad(
-                one(NORMED) if which < 2 else cot_low,
-                one(ACTS),
-                which * tiles,
-                tiles,
-                live.get((UNIT_GRAD, 0)),
-                3 * units,
-            )
-        if slot == third + 3:
-            unit_result = lax.psum_scatter(
-                live.pop((UNIT_GRAD, 0)), "dp", scatter_dimension=0, tiled=True
-            )
-            live.pop((ACTS, 0))
-            live.pop((NORMED, 0))
-            half = length // SMALL // 2
-            names = (PRE_GRAD, GATES_GRAD, CARRIED)
-            keep(names, backward(half, half))
-            pieces = chunks // 2
-            made = run_nt(one(PRE_GRAD), length // 2, pieces, 0, branch_full, 0, 2 * channels)
-            for c in range(pieces):
-                live[PART, fourth + c] = made[pieces - 1 - c]
-            send_in(fourth)
-            keep(names, backward(0, half))
-            made = run_nt(one(PRE_GRAD), 0, pieces, 0, branch_full, 0, 2 * channels)
-            for c in range(pieces):
-                live[PART, fourth + pieces + c] = made[pieces - 1 - c]
-        if slot == fourth:
-            live[PACKED, 0] = run_packed_grad(normed, one(PRE_GRAD), 0, None, shape)
-        if slot == fourth + 1:
-            live[PACKED, 0] = run_packed_grad(
-                one(MID), live[FORWARD, 6], 2, one(PACKED), shape
-            )
-        if slot == fourth + 2:
-            live[PACKED, 0] = run_thin_grad(one(GATES_GRAD), live[FORWARD, 2], one(PACKED))
-        if fourth <= slot < total_jobs:
-            c = jobs[slot][1]
-            rows = slice(c * CHUNK, (c + 1) * CHUNK)
-            part = live[PART, slot].astype(F32) * flat[rows] * inv_one[rows]
-            live[GAIN_ONE, 0] = live.get((GAIN_ONE, 0), 0.0) + jnp.sum(part, axis=0)
-        if slot == total_jobs - 1:
-            gain_sum = sum(live.pop((GAIN, c))[0] for c in range(chunks))
-            live[SMALL_SUMS, 0] = jnp.concatenate(
-                [
-                    live.pop((CARRIED, 0))[24:].reshape(-1),
-                    live.pop((GAIN_ONE, 0)),
-                    jnp.where(zed == 1, gain_sum / gain_two, 0.0),
-                ]
-            )
-            live.pop((GATES_GRAD, 0))
-        if slot == total_jobs:
-            rec_result = lax.psum_scatter(
-                live.pop((PACKED, 0)), "dp", scatter_dimension=0, tiled=True
-            )[0]
+    for job, (_, first, rows) in enumerate(jobs[:2]):
+        live[PART, job] = nt_dot(live[FORWARD, 6][first : first + rows], out_full).astype(BF)
+
+    send(0)
+    send(1)
+    forward(1)
+    send(2)
+    summed(0)
+    forward(2)
+    summed(1)
+    send(3)
+    total(0)
+    total(1)
+    summed(2)
+    forward(3)
+    drain()
+    cot_low, chain[0] = lax.optimization_barrier((incoming.astype(BF), chain[0]))
+    summed(3)
+    total(2)
+    live[WEIGHTS, 0], chain[0] = lax.optimization_barrier((live[WEIGHTS, 0], chain[0]))
+    send(4)
+    ffn(0, 0, 1)
+    total(3)
+    summed(4)
+    ffn(1, 2)
+    total(4)
+    summed(5)
+    ffn(2, 3)
+    summed(6)
+    total(5)
+    ffn(3, 4)
+    summed(7)
+    total(6)
+    arrived(5)
+    ahead_parts(0, [CHUNK])
+    send(9)
+    unit_grad(0)
+    summed(8)
+    total(7)
+    arrived(6)
+    unit_grad(1)
+    unit_grad(2)
+    ahead_parts(CHUNK, [CHUNK])
+    drain()
+    summed(9)
+    total(8)
+    unit_result = scatter(UNIT_GRAD)
+    send(10)
+    middle(0)
+    middle(1)
+    middle(2)
+    ahead_parts(2 * CHUNK, [CHUNK, CHUNK])
+    live.pop((WEIGHTS, 0))
+    send(11)
+    summed(10)
+    total(9)
+    middle(3)
+    backward(2)
+    send(12)
+    summed(11)
+    total(10)
+    arrived(9)
+    backward(0)
+    gain_part = live.pop((GAIN_ONE, 0)) + live.pop((GAIN_ONE, 2))
+    live[PART, 15] = run_append(chain, live[PART, 15], gain_part)
+    send(13)
+    summed(12)
+    total(11)
+    arrived(10)
+    pack(normed, one(PRE_GRAD), 0)
+    pack(one(MID), live[FORWARD, 6], 2)
+    send(14)
+    summed(13)
+    total(12)
+    arrived(11)
+    (live[PACKED, 0],) = run_thin_grad(
+        chain, one(GATES_GRAD), live[FORWARD, 2], one(PACKED)
+    )
+    rows_out(9)
+    rows_out(10)
+    summed(14)
+    total(13)
+    arrived(12)
+    unit_result, live[PACKED, 0], chain[0] = lax.optimization_barrier(
+        (unit_result, live[PACKED, 0], chain[0])
+    )
+    rec_result = scatter(PACKED)[0]
+    send(15)
+    rows_out(11)
+    send(16)
+    summed(15)
+    rows_out(12)
+    total(14)
+    send(17)
+    arrived(13)
+    summed(16)
+    rows_out(13)
+    send(18)
+    total(15)
+    summed(17)
+    rows_out(14)
+    total(16)
+    summed(18)
+    arrived(15)
+    small_pack(15)
+    small_start(0)
+    rows_out(15)
+    total(17)
+    small_end()
+    small_start(1)
+    rows_out(16)
+    total(18)
+    small_end()
+    small_start(2)
+    rows_out(17)
+    unit_grads = run_widen(chain, unit_result)
+    small_end()
+    rows_out(18)
 
     branch, states = live[FORWARD, 1], live[FORWARD, 3]
-    sums_all = one(SMALL_SUMS)[: 8 * channels].reshape(8, channels)
+    sums_all = one(SMALL_SUMS)[8:, :channels]
     last_begin = jnp.max(
         jnp.where(doc_starts <= length - 1, doc_starts, -3), axis=1, keepdims=True
     )
@@ -1359,7 +1598,6 @@
     conv_keep = (places[None, :] >= last_begin)[:, :, None]
     conv_final = jnp.where(conv_keep, branch[None, length - 3 :], 0.0)
     decay_grad = sums_all[7] * (-8.0 * jax.nn.sigmoid(-decay_param))
-    ffn_w = one(UNIT_RESULT).astype(F32)
     rec_w = rec_result.astype(F32)
     own = out_weight.shape[1]
     slim = recur_weight.shape[1]
@@ -1368,7 +1606,7 @@
         states[length - 1 :],
         conv_final,
         one(INPUT)[None],
-        one(GAIN_SUMS)[:width],
+        one(SMALL_SUMS)[0],
         rec_w[:own],
         rec_w[own : 2 * own],
         sums_all[0:4],
@@ -1379,10 +1617,8 @@
         sums_all[6],
         decay_grad,
         rec_w[2 * own : 3 * own].T,
-        one(GAIN_SUMS)[width:],
-        ffn_w[:, :units],
-        ffn_w[:, units : 2 * units],
-        ffn_w[:, 2 * units :].T,
+        one(SMALL_SUMS)[1],
+        *unit_grads,
     )
 
 

time: 647 us -> 587 us (0.907)
  waiting for transfers between devices: 116 us -> 57.3 us
  other arithmetic: 66.9 us -> 28.4 us
  Pallas kernels: 268 us -> 304 us
  starting transfers between devices: 137 us -> 147 us
    convert_element_type x34 -> x1, other arithmetic: 39.3 us -> 2.66 us  [line_device(): incoming.astype(BF)]
    pallas_call x31 -> x79, Pallas kernels: 266 us -> 300 us  [ordered(): pl.pallas_call(body, in_specs=[*in_specs, anywhere], out_specs=[anywhere,...]
    ppermute x22, waiting for transfers between devices: 33.8 us -> 14.3 us  [swap_dp(): return lax.ppermute(value, 'dp', [(i, i ^ bit) for i in range(8)])]
    ppermute x2 -> x0, waiting for transfers between devices: 17.2 us -> none  [small_step(): lax.ppermute(one(GAIN_SUMS), 'tensor', pairs)]
    ppermute x16 -> x19, waiting for transfers between devices: 28.5 us -> 13.1 us  [inward(): return lax.ppermute(value, 'tensor', [(0, 1), (3, 2)])]
    ppermute x16 -> x19, starting transfers between devices: 70.8 us -> 85.7 us  [inward(): return lax.ppermute(value, 'tensor', [(0, 1), (3, 2)])]
    reduce_sum x4 -> x0, other arithmetic: 8.69 us -> none  [line_device(): live[GAIN_ONE, 0] = live.get((GAIN_ONE, 0), 0.0) + jnp.sum(part, axis=0)]
    ppermute x2 -> x0, starting transfers between devices: 7.27 us -> none  [small_step(): lax.ppermute(one(GAIN_SUMS), 'tensor', pairs)]
  transfers between devices with their start and end apart: 75 -> 82, of which waited for: 24 -> 13; matrix products, arithmetic and copies ran while one was open for 14% -> 7% of each run, Pallas kernels for 42% -> 53%
where the time goes in v2:
time: 587 us; the launch traced here: 576 us
  Pallas kernels  304 us (52%)
  starting transfers between devices  147 us (25%)
  waiting for transfers between devices  57.3 us (10%)
  other arithmetic  28.4 us (5%)
  local copies, waits for them, and re-layouts  19.7 us (3%)
  between operations  16.3 us (3%)
    pallas_call x79, Pallas kernels, ordered(): pl.pallas_call(body, in_specs=[*in_specs, anywhere], out_specs=[anywhere,...  300 us
    ppermute x19, starting transfers between devices, inward(): return lax.ppermute(value, 'tensor', [(0, 1), (3, 2)])  85.7 us
    ppermute x19, waiting for transfers between devices, outward(): return lax.ppermute(value, 'tensor', [(1, 0), (2, 3)])  29.8 us
    ppermute x19, starting transfers between devices, outward(): return lax.ppermute(value, 'tensor', [(1, 0), (2, 3)])  26.2 us
    ppermute x22, starting transfers between devices, swap_dp(): return lax.ppermute(value, 'dp', [(i, i ^ bit) for i in range(8)])  20.1 us
    ppermute x19, starting transfers between devices, across(): return lax.ppermute(value, 'tensor', [(1, 2), (2, 1)])  14.9 us
    ppermute x22, waiting for transfers between devices, swap_dp(): return lax.ppermute(value, 'dp', [(i, i ^ bit) for i in range(8)])  14.3 us
    ppermute x19, waiting for transfers between devices, inward(): return lax.ppermute(value, 'tensor', [(0, 1), (3, 2)])  13.1 us
  transfers between devices with their start and end apart: 82, of which 13 were waited for; matrix products, arithmetic and copies ran while one was open for 7% of the time, Pallas kernels for 53%

profile of v2, /device:TPU:0, one launch (start us, length us, event | category | flops | bytes accessed | tf_op | source)
XLA Modules:
  0.0 576.3 jit_solution(16159161134032745347)
XLA Ops:
  64.9 8.8 %recurrent_forward.4 = (f32[8,128]{1,0:T(8,128)}, bf16[2048,1280]{1,0:T(8,128)(2,1)}, f32[1024,640]{1,0:T(8,128)}, f32[1024,640]{1,0:T(8,128)}, bf16[1024,640]{1...) custom-call(s32[1,3]{1,0:T(1,128)S(1)} %copy-done.34, ...), custom_call_target="tpu_custom_call", output_to_operand_aliasing={{0}: (10, {})} | custom-call | flops 1 | bytes 1 | tf_op jit(solution)/shard_map/recurrent_forward/pallas_call | solution.py:322
  86.4 10.9 %recurrent_forward.5 = (f32[8,128]{1,0:T(8,128)}, bf16[256,2048]{1,0:T(8,128)(2,1)S(1)}, f32[1024,640]{1,0:T(8,128)}, f32[1024,640]{1,0:T(8,128)}, bf16[1024,640...) custom-call(s32[1,3]{1,0:T(1,128)S(1)} %copy-done.34, ...), custom_call_target="tpu_custom_call", output_to_operand_aliasing={{2}: (7, {}), {3}: (8, {}), {4}: (9, {}), {5}: (10, {}), {6... | custom-call | flops 1 | bytes 1 | tf_op jit(solution)/shard_map/recurrent_forward/pallas_call | solution.py:322
  99.5 11.0 %recurrent_forward.6 = (f32[8,128]{1,0:T(8,128)}, bf16[256,2048]{1,0:T(8,128)(2,1)S(1)}, f32[1024,640]{1,0:T(8,128)}, f32[1024,640]{1,0:T(8,128)}, bf16[1024,640...) custom-call(s32[1,3]{1,0:T(1,128)S(1)} %copy-done.34, ...), custom_call_target="tpu_custom_call", output_to_operand_aliasing={{2}: (7, {}), {3}: (8, {}), {4}: (9, {}), {5}: (10, {}), {6... | custom-call | flops 1 | bytes 1 | tf_op jit(solution)/shard_map/recurrent_forward/pallas_call | solution.py:322
  117.6 11.3 %collective-permute-done.20.two = bf16[256,2048]{1,0:T(8,128)(2,1)S(1)} collective-permute-done((bf16[256,2048]{1,0:T(8,128)(2,1)S(1)}, bf16[256,2048]{1,0:T(8,128)(2,1)S(1)}, u32[]{:S(2)}, u32[]{:S(2)}) %collective-permute-start.20) | collective-permute-done | bytes 1048608 | tf_op jit(solution)/shard_map/ppermute | solution.py:1176
  135.3 10.8 %recurrent_forward.7 = (f32[8,128]{1,0:T(8,128)}, bf16[256,2048]{1,0:T(8,128)(2,1)S(1)}, f32[1024,640]{1,0:T(8,128)}, f32[1024,640]{1,0:T(8,128)}, bf16[1024,640...) custom-call(s32[1,3]{1,0:T(1,128)S(1)} %copy-done.34, ...), custom_call_target="tpu_custom_call", output_to_operand_aliasing={{2}: (7, {}), {3}: (8, {}), {4}: (9, {}), {5}: (10, {}), {6... | custom-call | flops 1 | bytes 1 | tf_op jit(solution)/shard_map/recurrent_forward/pallas_call | solution.py:322
  149.3 8.7 %collective-permute-done.25.refs_2_ = bf16[128,2048]{1,0:T(8,128)(2,1)S(1)} collective-permute-done((bf16[128,2048]{1,0:T(8,128)(2,1)S(1)}, bf16[128,2048]{1,0:T(8,128)(2,1)S(1)}, u32[]{:S(2)}, u32[]{:S(2)}) %collective-permute-start.25) | collective-permute-done | bytes 524320 | tf_op jit(solution)/shard_map/ppermute | solution.py:1184
  166.0 15.9 %ffn_chunk.4 = (f32[8,128]{1,0:T(8,128)}, bf16[1024,4608]{1,0:T(8,128)(2,1)}, bf16[1024,2048]{1,0:T(8,128)(2,1)}, bf16[1024,2048]{1,0:T(8,128)(2,1)}, f32[1024,1...) custom-call(s32[1]{0:T(128)} %bitcast.zed_ref, bf16[128,2048]{1,0:T(8,128)(2,1)} %copy-done.24, ...), custom_call_target="tpu_custom_call", output_to_operand_aliasing={{0}: (9, {})} | custom-call | flops 1 | bytes 1 | tf_op jit(solution)/shard_map/ffn_chunk/pallas_call | solution.py:322
  187.5 6.7 %collective-permute-start.34 = (bf16[256,2048]{1,0:T(8,128)(2,1)S(1)}, bf16[256,2048]{1,0:T(8,128)(2,1)S(1)}, u32[]{:S(2)}, u32[]{:S(2)}) collective-permute-start(bf16[256,2048]{1,0:T(8,128)(2,1)S(1)} %get-tuple-element.456.one), channel_id=1, source_target_pairs={{0,1},{3,2},{4,5},{7,6},{8,9},{11,10},{12,13},{15,14},{16,17},{19,... | collective-permute-start | bytes 3145736 | tf_op jit(solution)/shard_map/ppermute | solution.py:1176
  196.7 15.9 %ffn_chunk.5 = (f32[8,128]{1,0:T(8,128)}, bf16[1024,4608]{1,0:T(8,128)(2,1)}, bf16[1024,2048]{1,0:T(8,128)(2,1)}, bf16[1024,2048]{1,0:T(8,128)(2,1)}, f32[1024,1...) custom-call(s32[1]{0:T(128)} %bitcast.zed_ref, ...), custom_call_target="tpu_custom_call", output_to_operand_aliasing={{1}: (7, {}), {2}: (8, {}), {3}: (9, {}), {4}: (10, {}), {0... | custom-call | flops 1 | bytes 1 | tf_op jit(solution)/shard_map/ffn_chunk/pallas_call | solution.py:322
  221.2 15.8 %ffn_chunk.6 = (f32[8,128]{1,0:T(8,128)}, bf16[1024,4608]{1,0:T(8,128)(2,1)}, bf16[1024,2048]{1,0:T(8,128)(2,1)}, bf16[1024,2048]{1,0:T(8,128)(2,1)}, f32[1024,1...) custom-call(s32[1]{0:T(128)} %bitcast.zed_ref, ...), custom_call_target="tpu_custom_call", output_to_operand_aliasing={{1}: (7, {}), {2}: (8, {}), {3}: (9, {}), {4}: (10, {}), {0... | custom-call | flops 1 | bytes 1 | tf_op jit(solution)/shard_map/ffn_chunk/pallas_call | solution.py:322
  245.9 15.8 %ffn_chunk.7 = (f32[8,128]{1,0:T(8,128)}, bf16[1024,4608]{1,0:T(8,128)(2,1)}, bf16[1024,2048]{1,0:T(8,128)(2,1)}, bf16[1024,2048]{1,0:T(8,128)(2,1)}, f32[1024,1...) custom-call(s32[1]{0:T(128)} %bitcast.zed_ref, ...), custom_call_target="tpu_custom_call", output_to_operand_aliasing={{1}: (7, {}), {2}: (8, {}), {3}: (9, {}), {4}: (10, {}), {0... | custom-call | flops 1 | bytes 1 | tf_op jit(solution)/shard_map/ffn_chunk/pallas_call | solution.py:322
  273.3 11.1 %unit_weight_grad.3 = (f32[8,128]{1,0:T(8,128)}, bf16[2048,4608]{1,0:T(8,128)(2,1)}) custom-call(bf16[1024,2048]{1,0:T(8,128)(2,1)} %get-tuple-element.477.left.normed_ref, bf16[1024,4608]{1,0:T(8,128)(2,1)} %get-tuple-element.470.left.right, f32[8,128]{1,0:T(8,128)} %get-tuple-element.485.refs_0_), custom_call_target="tpu_custom_call", output_to_operand_aliasing={{0}: (2, {})} | custom-call | flops 1 | bytes 1 | tf_op jit(solution)/shard_map/unit_weight_grad/pallas_call | solution.py:322
  287.3 7.3 %collective-permute-start.43 = (bf16[256,2048]{1,0:T(8,128)(2,1)S(1)}, bf16[256,2048]{1,0:T(8,128)(2,1)S(1)}, u32[]{:S(2)}, u32[]{:S(2)}) collective-permute-start(bf16[256,2048]{1,0:T(8,128)(2,1)S(1)} %get-tuple-element.493.one), channel_id=1, source_target_pairs={{0,1},{3,2},{4,5},{7,6},{8,9},{11,10},{12,13},{15,14},{16,17},{19,... | collective-permute-start | bytes 3145736 | tf_op jit(solution)/shard_map/ppermute | solution.py:1176
  294.6 11.5 %unit_weight_grad.4 = (f32[8,128]{1,0:T(8,128)}, bf16[2048,4608]{1,0:T(8,128)(2,1)}) custom-call(bf16[1024,2048]{1,0:T(8,128)(2,1)} %get-tuple-element.477.left.normed_ref, bf16[1024,4608]{1,0:T(8,128)(2,1)} %get-tuple-element.470.left.right, bf16[2048,4608]{1,0:T(8,128)(2,1)} %get-tuple-element.495.refs_0_, ...), custom_call_target="tpu_custom_call", output_to_operand_aliasing={{1}: (2, {}), {0}: (3, {})} | custom-call | flops 1 | bytes 1 | tf_op jit(solution)/shard_map/unit_weight_grad/pallas_call | solution.py:322
  306.2 11.2 %unit_weight_grad.5 = (f32[8,128]{1,0:T(8,128)}, bf16[2048,4608]{1,0:T(8,128)(2,1)}) custom-call(bf16[1024,2048]{1,0:T(8,128)(2,1)} %bitcast_convert_fusion.refs_6_.refs_4_.left, bf16[1024,4608]{1,0:T(8,128)(2,1)} %get-tuple-element.470.left.right, bf16[2048,4608]{1,0:T(8,128)(2,1)} %get-tuple-element.497.refs_0_, ...), custom_call_target="tpu_custom_call", output_to_operand_aliasing={{1}: (2, {}), {0}: (3, {})} | custom-call | flops 1 | bytes 1 | tf_op jit(solution)/shard_map/unit_weight_grad/pallas_call | solution.py:322
  342.5 7.5 %rows_by_rows.7 = (f32[8,128]{1,0:T(8,128)}, bf16[256,2048]{1,0:T(8,128)(2,1)S(1)}, bf16[256,2048]{1,0:T(8,128)(2,1)S(1)}) custom-call(bf16[1024,4608]{1,0:T(8,128)(2,1)} %get-tuple-element.470.left.right, bf16[2048,4608]{1,0:T(8,128)(2,1)} %all-gather.2.cloned.1.call-done.refs_7_.refs_5_.right, ...), custom_call_target="tpu_custom_call", output_to_operand_aliasing={{0}: (2, {})} | custom-call | flops 1 | bytes 1 | tf_op jit(solution)/shard_map/rows_by_rows/pallas_call | solution.py:322
  363.1 13.9 %recurrent_backward.2 = (f32[8,128]{1,0:T(8,128)}, bf16[1024,1280]{1,0:T(8,128)(2,1)}, bf16[1024,1280]{1,0:T(8,128)(2,1)}, f32[32,640]{1,0:T(8,128)S(1)}) custom-call(s32[1,3]{1,0:T(1,128)S(1)} %copy-done.34, bf16[1024,2048]{1,0:T(8,128)(2,1)} %get-tuple-element.532.grad_ref.left, bf16[2048,640]{1,0:T(8,128)(2,1)} %copy-done, ...), custom_call_target="tpu_custom_call", output_to_operand_aliasing={{0}: (14, {})} | custom-call | flops 1 | bytes 1 | tf_op jit(solution)/shard_map/recurrent_backward/pallas_call | solution.py:322
  390.6 14.2 %recurrent_backward.3 = (f32[8,128]{1,0:T(8,128)}, bf16[1024,1280]{1,0:T(8,128)(2,1)}, bf16[1024,1280]{1,0:T(8,128)(2,1)}, f32[32,640]{1,0:T(8,128)S(1)}) custom-call(s32[1,3]{1,0:T(1,128)S(1)} %copy-done.34, bf16[1024,2048]{1,0:T(8,128)(2,1)} %get-tuple-element.532.grad_ref.left, ...), custom_call_target="tpu_custom_call", output_to_operand_aliasing={{1}: (14, {}), {2}: (15, {}), {0}: (16, {})} | custom-call | flops 1 | bytes 1 | tf_op jit(solution)/shard_map/recurrent_backward/pallas_call | solution.py:322
  404.9 6.7 %rows_by_rows.9 = (f32[8,128]{1,0:T(8,128)}, bf16[128,2048]{1,0:T(8,128)(2,1)S(1)}, bf16[128,2048]{1,0:T(8,128)(2,1)S(1)}, bf16[128,2048]{1,0:T(8,128)(2,1)S(1)}...) custom-call(bf16[1024,1280]{1,0:T(8,128)(2,1)} %get-tuple-element.554.left.right, ...), custom_call_target="tpu_custom_call", output_to_operand_aliasing={{0}: (3, {})} | custom-call | flops 1 | bytes 1 | tf_op jit(solution)/shard_map/rows_by_rows/pallas_call | solution.py:322
  421.4 11.3 %branch_weight_grad.2 = (f32[8,128]{1,0:T(8,128)}, bf16[8,832,640]{2,1,0:T(8,128)(2,1)}) custom-call(bf16[1024,2048]{1,0:T(8,128)(2,1)} %multiply_convert_fusion.refs_5_.refs_0_.left.normed, bf16[1024,1280]{1,0:T(8,128)(2,1)} %get-tuple-element.554.left.right, f32[8,128]{1,0:T(8,128)} %get-tuple-element.570.refs_0_), custom_call_target="tpu_custom_call", output_to_operand_aliasing={{0}: (2, {})} | custom-call | flops 1 | bytes 1 | tf_op jit(solution)/shard_map/branch_weight_grad/pallas_call | solution.py:322
  432.7 9.2 %branch_weight_grad.3 = (f32[8,128]{1,0:T(8,128)}, bf16[8,832,640]{2,1,0:T(8,128)(2,1)}) custom-call(bf16[1024,2048]{1,0:T(8,128)(2,1)} %get-tuple-element.532.grad_ref.left, bf16[1024,640]{1,0:T(8,128)(2,1)} %get-tuple-element.565.right, bf16[8,832,640]{2,1,0:T(8,128)(2,1)} %get-tuple-element.571.refs_0_, ...), custom_call_target="tpu_custom_call", output_to_operand_aliasing={{1}: (2, {}), {0}: (3, {})} | custom-call | flops 1 | bytes 1 | tf_op jit(solution)/shard_map/branch_weight_grad/pallas_call | solution.py:322
  466.7 6.8 %collective-permute-start.61 = (bf16[144,2048]{1,0:T(8,128)(2,1)}, bf16[144,2048]{1,0:T(8,128)(2,1)S(1)}, u32[]{:S(2)}, u32[]{:S(2)}) collective-permute-start(bf16[144,2048]{1,0:T(8,128)(2,1)} %copy-done.22), channel_id=1, source_target_pairs={{0,1},{3,2},{4,5},{7,6},{8,9},{11,10},{12,13},{15,14},{16,17},{19,... | collective-permute-start | bytes 1769480 | tf_op jit(solution)/shard_map/ppermute | solution.py:1176
  493.0 6.9 %collective-permute-start.68 = (bf16[128,2048]{1,0:T(8,128)(2,1)S(1)}, bf16[128,2048]{1,0:T(8,128)(2,1)S(1)}, u32[]{:S(2)}, u32[]{:S(2)}) collective-permute-start(bf16[128,2048]{1,0:T(8,128)(2,1)S(1)} %copy-done.29), channel_id=1, source_target_pairs={{0,1},{3,2},{4,5},{7,6},{8,9},{11,10},{12,13},{15,14},{16,17},{19,... | collective-permute-start | bytes 1572872 | tf_op jit(solution)/shard_map/ppermute | solution.py:1176
  512.8 8.0 %collective-permute-done.67.came = bf16[256,2048]{1,0:T(8,128)(2,1)S(1)} collective-permute-done((bf16[256,2048]{1,0:T(8,128)(2,1)S(1)}, bf16[256,2048]{1,0:T(8,128)(2,1)S(1)}, u32[]{:S(2)}, u32[]{:S(2)}) %collective-permute-start.67) | collective-permute-done | bytes 1048608 | tf_op jit(solution)/shard_map/ppermute | solution.py:1184
  (414 shorter events, 302.7 us)
Async XLA Ops:
  7.2 153.1 %all-gather.2.cloned.1.call-start = ((), (), s32[]{:S(2)}) async-start(), calls=%async_computation.2 | async-start | bytes 21233664 | tf_op jit(solution)/shard_map/all_gather | solution.py:1277
  48.8 417.0 %reduce-scatter.3.cloned.1.call-start = ((), (), s32[]{:S(2)}) async-start(), calls=%async_computation.3 | async-start | bytes 21233664 | tf_op jit(solution)/shard_map/reduce_scatter | solution.py:1438
  97.3 31.7 %collective-permute-start.20 = (bf16[256,2048]{1,0:T(8,128)(2,1)S(1)}, bf16[256,2048]{1,0:T(8,128)(2,1)S(1)}, u32[]{:S(2)}, u32[]{:S(2)}) collective-permute-start(bf16[256,2048]{1,0:T(8,128)(2,1)S(1)} %get-tuple-element.404.one), channel_id=1, source_target_pairs={{0,1},{3,2},{4,5},{7,6},{8,9},{11,10},{12,13},{15,14},{16,17},{19,... | collective-permute-start | bytes 3145736 | tf_op jit(solution)/shard_map/ppermute | solution.py:1176
  111.5 46.5 %collective-permute-start.24 = (bf16[256,2048]{1,0:T(8,128)(2,1)S(1)}, bf16[256,2048]{1,0:T(8,128)(2,1)S(1)}, u32[]{:S(2)}, u32[]{:S(2)}) collective-permute-start(bf16[256,2048]{1,0:T(8,128)(2,1)S(1)} %get-tuple-element.418.one), channel_id=1, source_target_pairs={{0,1},{3,2},{4,5},{7,6},{8,9},{11,10},{12,13},{15,14},{16,17},{19,... | collective-permute-start | bytes 3145736 | tf_op jit(solution)/shard_map/ppermute | solution.py:1176
  164.3 31.4 %collective-permute-start.31 = (bf16[256,2048]{1,0:T(8,128)(2,1)S(1)}, bf16[256,2048]{1,0:T(8,128)(2,1)S(1)}, u32[]{:S(2)}, u32[]{:S(2)}) collective-permute-start(bf16[256,2048]{1,0:T(8,128)(2,1)S(1)} %get-tuple-element.441.refs_0_), channel_id=1, source_target_pairs={{1,0},{2,3},{5,4},{6,7},{9,8},{10,11},{13,12},{14,15},{17,16},{18,... | collective-permute-start | bytes 3145736 | tf_op jit(solution)/shard_map/ppermute | solution.py:1184
  186.7 30.5 %collective-permute-start.30 = (bf16[256,2048]{1,0:T(8,128)(2,1)S(1)}, bf16[256,2048]{1,0:T(8,128)(2,1)S(1)}, u32[]{:S(2)}, u32[]{:S(2)}) collective-permute-start(bf16[256,2048]{1,0:T(8,128)(2,1)S(1)} %get-tuple-element.440.one), channel_id=1, source_target_pairs={{1,2},{2,1},{5,6},{6,5},{9,10},{10,9},{13,14},{14,13},{17,18},{18,... | collective-permute-start | bytes 3145736 | tf_op jit(solution)/shard_map/ppermute | solution.py:1180
  187.5 30.1 %collective-permute-start.34 = (bf16[256,2048]{1,0:T(8,128)(2,1)S(1)}, bf16[256,2048]{1,0:T(8,128)(2,1)S(1)}, u32[]{:S(2)}, u32[]{:S(2)}) collective-permute-start(bf16[256,2048]{1,0:T(8,128)(2,1)S(1)} %get-tuple-element.456.one), channel_id=1, source_target_pairs={{0,1},{3,2},{4,5},{7,6},{8,9},{11,10},{12,13},{15,14},{16,17},{19,... | collective-permute-start | bytes 3145736 | tf_op jit(solution)/shard_map/ppermute | solution.py:1176
  212.6 29.2 %collective-permute-start.36 = (bf16[256,2048]{1,0:T(8,128)(2,1)S(1)}, bf16[256,2048]{1,0:T(8,128)(2,1)S(1)}, u32[]{:S(2)}, u32[]{:S(2)}) collective-permute-start(bf16[256,2048]{1,0:T(8,128)(2,1)S(1)} %get-tuple-element.464.one), channel_id=1, source_target_pairs={{0,1},{3,2},{4,5},{7,6},{8,9},{11,10},{12,13},{15,14},{16,17},{19,... | collective-permute-start | bytes 3145736 | tf_op jit(solution)/shard_map/ppermute | solution.py:1176
  237.0 29.4 %collective-permute-start.37 = (bf16[256,2048]{1,0:T(8,128)(2,1)S(1)}, bf16[256,2048]{1,0:T(8,128)(2,1)S(1)}, u32[]{:S(2)}, u32[]{:S(2)}) collective-permute-start(bf16[256,2048]{1,0:T(8,128)(2,1)S(1)} %get-tuple-element.471.one), channel_id=1, source_target_pairs={{0,1},{3,2},{4,5},{7,6},{8,9},{11,10},{12,13},{15,14},{16,17},{19,... | collective-permute-start | bytes 3145736 | tf_op jit(solution)/shard_map/ppermute | solution.py:1176
  285.1 36.4 %collective-permute-start.45 = (bf16[256,2048]{1,0:T(8,128)(2,1)S(1)}, bf16[256,2048]{1,0:T(8,128)(2,1)S(1)}, u32[]{:S(2)}, u32[]{:S(2)}) collective-permute-start(bf16[256,2048]{1,0:T(8,128)(2,1)S(1)} %get-tuple-element.488.own), channel_id=1, source_target_pairs={{1,0},{2,3},{5,4},{6,7},{9,8},{10,11},{13,12},{14,15},{17,16},{18,... | collective-permute-start | bytes 3145736 | tf_op jit(solution)/shard_map/ppermute | solution.py:1184
  286.4 35.1 %collective-permute-start.44 = (bf16[256,2048]{1,0:T(8,128)(2,1)S(1)}, bf16[256,2048]{1,0:T(8,128)(2,1)S(1)}, u32[]{:S(2)}, u32[]{:S(2)}) collective-permute-start(bf16[256,2048]{1,0:T(8,128)(2,1)S(1)} %get-tuple-element.494.one), channel_id=1, source_target_pairs={{1,2},{2,1},{5,6},{6,5},{9,10},{10,9},{13,14},{14,13},{17,18},{18,... | collective-permute-start | bytes 3145736 | tf_op jit(solution)/shard_map/ppermute | solution.py:1180
  287.3 34.2 %collective-permute-start.43 = (bf16[256,2048]{1,0:T(8,128)(2,1)S(1)}, bf16[256,2048]{1,0:T(8,128)(2,1)S(1)}, u32[]{:S(2)}, u32[]{:S(2)}) collective-permute-start(bf16[256,2048]{1,0:T(8,128)(2,1)S(1)} %get-tuple-element.493.one), channel_id=1, source_target_pairs={{0,1},{3,2},{4,5},{7,6},{8,9},{11,10},{12,13},{15,14},{16,17},{19,... | collective-permute-start | bytes 3145736 | tf_op jit(solution)/shard_map/ppermute | solution.py:1176
  323.9 241.2 %reduce-scatter.5.cloned.1.call-start = ((), (), s32[]{:S(2)}) async-start(), calls=%async_computation.4 | async-start | bytes 9584640 | tf_op jit(solution)/shard_map/reduce_scatter | solution.py:1438
  323.9 30.8 %collective-permute-start.48 = (bf16[256,2048]{1,0:T(8,128)(2,1)}, bf16[256,2048]{1,0:T(8,128)(2,1)S(1)}, u32[]{:S(2)}, u32[]{:S(2)}) collective-permute-start(bf16[256,2048]{1,0:T(8,128)(2,1)} %copy-done.18), channel_id=1, source_target_pairs={{0,1},{3,2},{4,5},{7,6},{8,9},{11,10},{12,13},{15,14},{16,17},{19,... | collective-permute-start | bytes 3145736 | tf_op jit(solution)/shard_map/ppermute | solution.py:1176
  325.3 30.5 %collective-permute-start.47 = (bf16[256,2048]{1,0:T(8,128)(2,1)}, bf16[256,2048]{1,0:T(8,128)(2,1)S(1)}, u32[]{:S(2)}, u32[]{:S(2)}) collective-permute-start(bf16[256,2048]{1,0:T(8,128)(2,1)} %copy-done.16), channel_id=1, source_target_pairs={{1,2},{2,1},{5,6},{6,5},{9,10},{10,9},{13,14},{14,13},{17,18},{18,... | collective-permute-start | bytes 3145736 | tf_op jit(solution)/shard_map/ppermute | solution.py:1180
  326.0 31.6 %collective-permute-start.46 = (bf16[256,2048]{1,0:T(8,128)(2,1)S(1)}, bf16[256,2048]{1,0:T(8,128)(2,1)S(1)}, u32[]{:S(2)}, u32[]{:S(2)}) collective-permute-start(bf16[256,2048]{1,0:T(8,128)(2,1)S(1)} %get-tuple-element.522.own), channel_id=1, source_target_pairs={{1,0},{2,3},{5,4},{6,7},{9,8},{10,11},{13,12},{14,15},{17,16},{18,... | collective-permute-start | bytes 3145736 | tf_op jit(solution)/shard_map/ppermute | solution.py:1184
  350.0 37.9 %collective-permute-start.52 = (bf16[256,2048]{1,0:T(8,128)(2,1)S(1)}, bf16[256,2048]{1,0:T(8,128)(2,1)S(1)}, u32[]{:S(2)}, u32[]{:S(2)}) collective-permute-start(bf16[256,2048]{1,0:T(8,128)(2,1)S(1)} %get-tuple-element.549.one), channel_id=1, source_target_pairs={{0,1},{3,2},{4,5},{7,6},{8,9},{11,10},{12,13},{15,14},{16,17},{19,... | collective-permute-start | bytes 3145736 | tf_op jit(solution)/shard_map/ppermute | solution.py:1176
  355.0 34.0 %collective-permute-start.51 = (bf16[256,2048]{1,0:T(8,128)(2,1)S(1)}, bf16[256,2048]{1,0:T(8,128)(2,1)S(1)}, u32[]{:S(2)}, u32[]{:S(2)}) collective-permute-start(bf16[256,2048]{1,0:T(8,128)(2,1)S(1)} %get-tuple-element.548.one), channel_id=1, source_target_pairs={{1,2},{2,1},{5,6},{6,5},{9,10},{10,9},{13,14},{14,13},{17,18},{18,... | collective-permute-start | bytes 3145736 | tf_op jit(solution)/shard_map/ppermute | solution.py:1180
  356.1 33.2 %collective-permute-start.50 = (bf16[256,2048]{1,0:T(8,128)(2,1)S(1)}, bf16[256,2048]{1,0:T(8,128)(2,1)S(1)}, u32[]{:S(2)}, u32[]{:S(2)}) collective-permute-start(bf16[256,2048]{1,0:T(8,128)(2,1)S(1)} %get-tuple-element.547.own), channel_id=1, source_target_pairs={{1,0},{2,3},{5,4},{6,7},{9,8},{10,11},{13,12},{14,15},{17,16},{18,... | collective-permute-start | bytes 3145736 | tf_op jit(solution)/shard_map/ppermute | solution.py:1184
  383.3 35.4 %collective-permute-start.49 = (bf16[256,2048]{1,0:T(8,128)(2,1)S(1)}, bf16[256,2048]{1,0:T(8,128)(2,1)S(1)}, u32[]{:S(2)}, u32[]{:S(2)}) collective-permute-start(bf16[256,2048]{1,0:T(8,128)(2,1)S(1)} %get-tuple-element.543.one), channel_id=1, source_target_pairs={{0,1},{3,2},{4,5},{7,6},{8,9},{11,10},{12,13},{15,14},{16,17},{19,... | collective-permute-start | bytes 3145736 | tf_op jit(solution)/shard_map/ppermute | solution.py:1176
  388.2 31.5 %collective-permute-start.56 = (bf16[256,2048]{1,0:T(8,128)(2,1)S(1)}, bf16[256,2048]{1,0:T(8,128)(2,1)S(1)}, u32[]{:S(2)}, u32[]{:S(2)}) collective-permute-start(bf16[256,2048]{1,0:T(8,128)(2,1)S(1)} %get-tuple-element.567.one), channel_id=1, source_target_pairs={{1,2},{2,1},{5,6},{6,5},{9,10},{10,9},{13,14},{14,13},{17,18},{18,... | collective-permute-start | bytes 3145736 | tf_op jit(solution)/shard_map/ppermute | solution.py:1180
  389.3 32.0 %collective-permute-start.55 = (bf16[256,2048]{1,0:T(8,128)(2,1)S(1)}, bf16[256,2048]{1,0:T(8,128)(2,1)S(1)}, u32[]{:S(2)}, u32[]{:S(2)}) collective-permute-start(bf16[256,2048]{1,0:T(8,128)(2,1)S(1)} %get-tuple-element.566.own), channel_id=1, source_target_pairs={{1,0},{2,3},{5,4},{6,7},{9,8},{10,11},{13,12},{14,15},{17,16},{18,... | collective-permute-start | bytes 3145736 | tf_op jit(solution)/shard_map/ppermute | solution.py:1184
  414.0 32.3 %collective-permute-start.54 = (bf16[256,2048]{1,0:T(8,128)(2,1)S(1)}, bf16[256,2048]{1,0:T(8,128)(2,1)S(1)}, u32[]{:S(2)}, u32[]{:S(2)}) collective-permute-start(bf16[256,2048]{1,0:T(8,128)(2,1)S(1)} %get-tuple-element.563.one), channel_id=1, source_target_pairs={{0,1},{3,2},{4,5},{7,6},{8,9},{11,10},{12,13},{15,14},{16,17},{19,... | collective-permute-start | bytes 3145736 | tf_op jit(solution)/shard_map/ppermute | solution.py:1176
  491.0 29.8 %collective-permute-start.67 = (bf16[256,2048]{1,0:T(8,128)(2,1)S(1)}, bf16[256,2048]{1,0:T(8,128)(2,1)S(1)}, u32[]{:S(2)}, u32[]{:S(2)}) collective-permute-start(bf16[256,2048]{1,0:T(8,128)(2,1)S(1)} %get-tuple-element.626.own), channel_id=1, source_target_pairs={{1,0},{2,3},{5,4},{6,7},{9,8},{10,11},{13,12},{14,15},{17,16},{18,... | collective-permute-start | bytes 3145736 | tf_op jit(solution)/shard_map/ppermute | solution.py:1184
  (123 other events, 1568.5 us)
Sparse Core Ops, SparseCore 0:
  48.9 99.0 all-gather.1
  324.0 124.5 reduce-scatter.2
  466.0 71.9 reduce-scatter.4

commit v3 on v2

--- a/solution.py
+++ b/solution.py
@@ -825,7 +825,7 @@
 def run_nt(chain, left, first, sizes, left_col, right, right_col, depth, weigh=None):
     width = right.shape[0]
     rows = sum(sizes)
-    tile = 1024 if rows <= CHUNK else 512
+    tile = 1024 if rows <= 2 * CHUNK else 512
     args = [hbm(left), hbm(right)]
     in_specs = [
         pl.BlockSpec((pl.Element(rows), pl.Element(depth)), lambda i: (first, left_col * depth)),
@@ -1132,8 +1132,8 @@
     return one, jnp.stack([own[1], second[1], first[1], far[1]])
 
 
-def natural_kernel(me_ref, *refs):
-    pieces, (out_ref, sem) = refs[:4], refs[4:]
+def project_kernel(me_ref, *refs):
+    pieces, product, (out_ref, *parts, sem) = refs[:4], refs[4], refs[5:]
     half = pieces[0].shape[1]
     copies = []
     for which, piece in enumerate(pieces):
@@ -1149,21 +1149,33 @@
         copy.start()
     for copy in copies:
         copy.wait()
-
-
-def natural_order(pieces, me):
-    _, rows, columns = pieces[0].shape
+    total = nt_dot(product[...], out_ref[...]).astype(BF)
+    row = 0
+    for part in parts:
+        part[...] = total[row : row + part.shape[0]]
+        row += part.shape[0]
+
+
+def run_project(pieces, me, product, sizes):
+    _, rows, channels = pieces[0].shape
+    width = 16 * rows
     anywhere = pl.BlockSpec(memory_space=pl.ANY)
+    whole = lambda i: (0, 0)
     return pl.pallas_call(
-        natural_kernel,
-        in_specs=[pl.BlockSpec(memory_space=pltpu.SMEM)] + [anywhere] * 4,
-        out_specs=pl.BlockSpec(memory_space=pltpu.VMEM),
-        out_shape=jax.ShapeDtypeStruct((16 * rows, columns), pieces[0].dtype),
+        project_kernel,
+        grid=(1,),
+        in_specs=[pl.BlockSpec(memory_space=pltpu.SMEM)]
+        + [anywhere] * 4
+        + [pl.BlockSpec((sum(sizes), channels), whole)],
+        out_specs=[pl.BlockSpec((width, channels), whole)]
+        + [pl.BlockSpec((size, width), whole) for size in sizes],
+        out_shape=[pltpu.HBM((width, channels), BF)]
+        + [jax.ShapeDtypeStruct((size, width), BF) for size in sizes],
         scratch_shapes=[pltpu.SemaphoreType.DMA((16,))],
-        compiler_params=params(16),
+        compiler_params=params(24),
         cost_estimate=COST,
-        name="natural_order",
-    )(me, *pieces)
+        name="project_first",
+    )(me, *pieces, hbm(product))
 
 
 def widen(held, bit):
@@ -1265,8 +1277,9 @@
     hist = jnp.concatenate([jnp.zeros((5, channels), F32), conv_state[0]], 0)
     before = jnp.concatenate([hist, jnp.broadcast_to(recur_state, (8, channels))], 0)
     own = (gelu_branch, lru_branch)
-    own, got, thin, inv_one, vec, before = lax.optimization_barrier(
-        (own, swap_own(own), widen(thin, 4), inv_one, vec, before)
+    cot_low = incoming.astype(BF)
+    own, got, thin, inv_one, vec, before, cot_low = lax.optimization_barrier(
+        (own, swap_own(own), widen(thin, 4), inv_one, vec, before, cot_low)
     )
     normed = (flat * inv_one * gain_one).astype(BF)
     corner = swap_got(got[0])
@@ -1279,11 +1292,10 @@
     far = tuple(swap_dp(item, 1) for item in near)
     out_near = stack_pair(out_own, out_got, swap_got(out_got[0]))
     near, far, out_near, thin = lax.optimization_barrier((near, far, out_near, widen(thin, 1)))
-    thin_full = thin.transpose(2, 1, 0, 3, 4, 5).reshape(8, 2, HEAD // 8, channels)
-    thin_full = thin_full.transpose(1, 0, 2, 3).reshape(2, HEAD, channels)
-    heads = jnp.where(same[None], jnp.tile(thin_full, (1, count, 1)), 0).reshape(
-        2 * channels, channels
-    )
+    thin = thin.transpose(2, 1, 0, 3, 4, 5).reshape(8, 2, HEAD // 8, channels)
+    thin = thin.transpose(1, 0, 2, 3).reshape(2, HEAD, channels)
+    heads = jnp.where(same[None], jnp.tile(thin, (1, count, 1)), 0)
+    heads = heads.reshape(2 * channels, channels)
 
     blocks = CHUNK // SMALL
     chain = [jnp.zeros((8, 128), F32)]
@@ -1291,19 +1303,18 @@
         chain, doc_starts, normed, heads, vec, before, near + far, 0, blocks, me=me
     )
     out_far = tuple(swap_dp(item, 1) for item in out_near)
-    out_full = natural_order(out_near + out_far, me)
+    half = CHUNK // 2
+    out_full, *first_parts = run_project(out_near + out_far, me, made[6], [half, half])
     wide_inv = jnp.broadcast_to(inv_one, (length, 128))
 
-    half = CHUNK // 2
     ahead = [(c * CHUNK, CHUNK) for c in range(chunks)]
-    cut = [(0, half), (half, half)]
-    jobs = [(TO_NORM, *rows) for rows in cut + ahead[1:]]
+    halves = [(row, half) for row in range(0, 2 * CHUNK, half)]
+    jobs = [(TO_NORM, *rows) for rows in halves + ahead[2:]]
     second = len(jobs)
     jobs += [(TO_MIDDLE, *rows) for rows in ahead]
     third = len(jobs)
     jobs += [(TO_OUTPUT, *rows) for rows in ahead]
     fourth = len(jobs)
-    halves = [(row, half) for row in range(0, 2 * CHUNK, half)]
     jobs += [(TO_INPUT, *rows) for rows in ahead[:1:-1] + halves[::-1]]
     live = {(FORWARD, index): item for index, item in enumerate(made)}
 
@@ -1331,7 +1342,7 @@
             live[name, 0] = value
 
     def forward(c):
-        live[PART, c + 1], *made = run_forward(
+        part, *made = run_forward(
             chain,
             doc_starts,
             normed,
@@ -1346,6 +1357,10 @@
         )
         for index, item in enumerate(made):
             live[FORWARD, index] = item
+        if c == 1:
+            live[PART, 2], live[PART, 3] = part[:half], part[half:]
+        else:
+            live[PART, c + 2] = part
 
     def ffn(c, *from_jobs):
         names = (ACTS, NORMED, FIRST, INV)
@@ -1410,6 +1425,8 @@
             kept(*names[:2]),
         )
         keep(names, made)
+
+    def input_parts(c):
         sizes = [CHUNK, CHUNK] if c else [half] * 4
         *parts, live[GAIN_ONE, c] = run_nt(
             chain, one(PRE_GRAD), c * CHUNK, sizes, 0, branch_full, 0, 2 * channels, normed
@@ -1470,124 +1487,130 @@
     shape = (8, 3 * width // 8 + 64, channels)
     live[WEIGHTS, 0] = ffn_full
     live[CARRIED, 0] = jnp.zeros((32, channels), F32)
-    for job, (_, first, rows) in enumerate(jobs[:2]):
-        live[PART, job] = nt_dot(live[FORWARD, 6][first : first + rows], out_full).astype(BF)
+    live[PART, 0], live[PART, 1] = first_parts
 
     send(0)
     send(1)
     forward(1)
     send(2)
     summed(0)
+    send(3)
     forward(2)
     summed(1)
-    send(3)
     total(0)
+    send(4)
+    summed(2)
     total(1)
-    summed(2)
-    forward(3)
-    drain()
-    cot_low, chain[0] = lax.optimization_barrier((incoming.astype(BF), chain[0]))
+    arrived(0)
     summed(3)
     total(2)
+    forward(3)
+    arrived(1)
+    drain()
+    summed(4)
+    total(3)
     live[WEIGHTS, 0], chain[0] = lax.optimization_barrier((live[WEIGHTS, 0], chain[0]))
-    send(4)
+    send(5)
     ffn(0, 0, 1)
-    total(3)
-    summed(4)
-    ffn(1, 2)
+    arrived(3)
+    summed(5)
     total(4)
-    summed(5)
-    ffn(2, 3)
-    summed(6)
-    total(5)
-    ffn(3, 4)
-    summed(7)
-    total(6)
-    arrived(5)
-    ahead_parts(0, [CHUNK])
-    send(9)
+    ffn(1, 2, 3)
+    one_sum, two_sum, three_sum = second, third, fourth
+    summed(one_sum)
+    total(one_sum - 1)
+    ffn(2, 4)
+    summed(one_sum + 1)
+    total(one_sum)
+    ffn(3, 5)
+    summed(one_sum + 2)
+    total(one_sum + 1)
+    arrived(one_sum)
+    ahead_parts(0, [CHUNK] * chunks)
+    live.pop((WEIGHTS, 0))
+    send(two_sum)
     unit_grad(0)
-    summed(8)
-    total(7)
-    arrived(6)
+    summed(one_sum + 3)
+    total(one_sum + 2)
     unit_grad(1)
+    arrived(one_sum + 1)
     unit_grad(2)
-    ahead_parts(CHUNK, [CHUNK])
     drain()
-    summed(9)
-    total(8)
+    summed(two_sum)
+    total(one_sum + 3)
     unit_result = scatter(UNIT_GRAD)
-    send(10)
+    send(two_sum + 1)
     middle(0)
     middle(1)
     middle(2)
-    ahead_parts(2 * CHUNK, [CHUNK, CHUNK])
-    live.pop((WEIGHTS, 0))
-    send(11)
-    summed(10)
-    total(9)
+    send(two_sum + 2)
+    summed(two_sum + 1)
+    total(two_sum)
     middle(3)
     backward(2)
-    send(12)
-    summed(11)
-    total(10)
-    arrived(9)
+    input_parts(2)
+    send(two_sum + 3)
+    summed(two_sum + 2)
+    total(two_sum + 1)
+    arrived(two_sum)
     backward(0)
-    gain_part = live.pop((GAIN_ONE, 0)) + live.pop((GAIN_ONE, 2))
-    live[PART, 15] = run_append(chain, live[PART, 15], gain_part)
-    send(13)
-    summed(12)
-    total(11)
-    arrived(10)
+    send(three_sum)
+    summed(two_sum + 3)
+    total(two_sum + 2)
+    arrived(two_sum + 1)
     pack(normed, one(PRE_GRAD), 0)
-    pack(one(MID), live[FORWARD, 6], 2)
-    send(14)
-    summed(13)
-    total(12)
-    arrived(11)
     (live[PACKED, 0],) = run_thin_grad(
         chain, one(GATES_GRAD), live[FORWARD, 2], one(PACKED)
     )
-    rows_out(9)
-    rows_out(10)
-    summed(14)
-    total(13)
-    arrived(12)
+    send(three_sum + 1)
+    summed(three_sum)
+    total(two_sum + 3)
+    arrived(two_sum + 2)
+    input_parts(0)
+    rider = three_sum + 2
+    gain_part = live.pop((GAIN_ONE, 0)) + live.pop((GAIN_ONE, 2))
+    live[PART, rider] = run_append(chain, live[PART, rider], gain_part)
+    pack(one(MID), live[FORWARD, 6], 2)
+    summed(three_sum + 1)
+    total(three_sum)
+    arrived(two_sum + 3)
     unit_result, live[PACKED, 0], chain[0] = lax.optimization_barrier(
         (unit_result, live[PACKED, 0], chain[0])
     )
     rec_result = scatter(PACKED)[0]
-    send(15)
-    rows_out(11)
-    send(16)
-    summed(15)
-    rows_out(12)
-    total(14)
-    send(17)
-    arrived(13)
-    summed(16)
-    rows_out(13)
-    send(18)
-    total(15)
-    summed(17)
-    rows_out(14)
-    total(16)
-    summed(18)
-    arrived(15)
-    small_pack(15)
+    send(rider)
+    rows_out(two_sum)
+    rows_out(two_sum + 1)
+    send(rider + 1)
+    rows_out(two_sum + 2)
+    total(three_sum + 1)
+    arrived(three_sum)
+    summed(rider)
+    send(rider + 2)
+    summed(rider + 1)
+    rows_out(three_sum)
+    send(rider + 3)
+    total(rider)
+    summed(rider + 2)
+    rows_out(two_sum + 3)
+    rows_out(three_sum + 1)
+    total(rider + 1)
+    summed(rider + 3)
+    arrived(rider)
+    small_pack(rider)
     small_start(0)
-    rows_out(15)
-    total(17)
+    rows_out(rider)
+    total(rider + 2)
     small_end()
     small_start(1)
-    rows_out(16)
-    total(18)
+    rows_out(rider + 1)
+    total(rider + 3)
     small_end()
     small_start(2)
-    rows_out(17)
+    rows_out(rider + 2)
     unit_grads = run_widen(chain, unit_result)
     small_end()
-    rows_out(18)
+    rows_out(rider + 3)
 
     branch, states = live[FORWARD, 1], live[FORWARD, 3]
     sums_all = one(SMALL_SUMS)[8:, :channels]

time: 587 us -> 568 us (0.968)
  waiting for transfers between devices: 57.3 us -> 35.1 us
  starting transfers between devices: 147 us -> 155 us
  Pallas kernels: 304 us -> 298 us
    ppermute x19 -> x20, waiting for transfers between devices: 13.1 us -> 0.05 us  [inward(): return lax.ppermute(value, 'tensor', [(0, 1), (3, 2)])]
    pallas_call x79, Pallas kernels: 300 us -> 292 us  [ordered(): pl.pallas_call(body, in_specs=[*in_specs, anywhere], out_specs=[anywhere,...]
    ppermute x19 -> x20, starting transfers between devices: 85.7 us -> 92.4 us  [inward(): return lax.ppermute(value, 'tensor', [(0, 1), (3, 2)])]
    ppermute x19 -> x20, waiting for transfers between devices: 29.8 us -> 24.3 us  [outward(): return lax.ppermute(value, 'tensor', [(1, 0), (2, 3)])]
    unnamed x135 -> x163, local copies, waits for them, and re-layouts: 11.7 us -> 17 us
    ppermute x19 -> x20, starting transfers between devices: 26.2 us -> 27.6 us  [outward(): return lax.ppermute(value, 'tensor', [(1, 0), (2, 3)])]
    ppermute x19 -> x20, starting transfers between devices: 14.9 us -> 14.3 us  [across(): return lax.ppermute(value, 'tensor', [(1, 2), (2, 1)])]
  transfers between devices with their start and end apart: 82 -> 85, of which waited for: 13 -> 12; matrix products, arithmetic and copies ran while one was open for 7% -> 6% of each run, Pallas kernels for 53% -> 53%
where the time goes in v3:
time: 568 us; the launch traced here: 558 us
  Pallas kernels  298 us (52%)
  starting transfers between devices  155 us (27%)
  waiting for transfers between devices  35.1 us (6%)
  other arithmetic  28.9 us (5%)
  local copies, waits for them, and re-layouts  25 us (4%)
  between operations  16.5 us (3%)
    pallas_call x79, Pallas kernels, ordered(): pl.pallas_call(body, in_specs=[*in_specs, anywhere], out_specs=[anywhere,...  292 us
    ppermute x20, starting transfers between devices, inward(): return lax.ppermute(value, 'tensor', [(0, 1), (3, 2)])  92.4 us
    ppermute x20, starting transfers between devices, outward(): return lax.ppermute(value, 'tensor', [(1, 0), (2, 3)])  27.6 us
    ppermute x20, waiting for transfers between devices, outward(): return lax.ppermute(value, 'tensor', [(1, 0), (2, 3)])  24.3 us
    ppermute x22, starting transfers between devices, swap_dp(): return lax.ppermute(value, 'dp', [(i, i ^ bit) for i in range(8)])  20.6 us
    unnamed x163, local copies, waits for them, and re-layouts  17 us
    ppermute x20, starting transfers between devices, across(): return lax.ppermute(value, 'tensor', [(1, 2), (2, 1)])  14.3 us
  transfers between devices with their start and end apart: 85, of which 12 were waited for; matrix products, arithmetic and copies ran while one was open for 6% of the time, Pallas kernels for 53%

profile of v3, /device:TPU:0, one launch (start us, length us, event | category | flops | bytes accessed | tf_op | source)
XLA Modules:
  0.0 558.0 jit_solution(6445538514477971968)
XLA Ops:
  15.9 6.3 %bitcast_convert_fusion.refs_6_.refs_4_.left = bf16[1024,2048]{1,0:T(8,128)(2,1)} fusion(f32[1,1024,2048]{2,1,0:T(8,128)} %param.39), kind=kLoop, calls=%fused_computation.47 | loop fusion | flops 2097152 | bytes 12582912 | tf_op jit(solution)/shard_map/convert_element_type | solution.py:1280
  34.2 6.1 %multiply_convert_fusion.refs_5_.refs_0_.left.normed = bf16[1024,2048]{1,0:T(8,128)(2,1)} fusion(f32[2048]{0:T(1024)S(1)} %copy-done.56, f32[1024]{0:T(1024)S(1)} %add_rsqrt_fusion, f32[1,1024,2048]{2,1,0:T(8,128)} %param.20), kind=kLoop, calls=%fused_computation | loop fusion | flops 6291456 | bytes 12595200 | tf_op jit(solution)/shard_map/convert_element_type | solution.py:1284
  64.8 8.8 %recurrent_forward.4 = (f32[8,128]{1,0:T(8,128)}, bf16[2048,1280]{1,0:T(8,128)(2,1)}, f32[1024,640]{1,0:T(8,128)}, f32[1024,640]{1,0:T(8,128)}, bf16[1024,640]{1...) custom-call(s32[1,3]{1,0:T(1,128)S(1)} %copy-done.46, ...), custom_call_target="tpu_custom_call", output_to_operand_aliasing={{0}: (10, {})} | custom-call | flops 1 | bytes 1 | tf_op jit(solution)/shard_map/recurrent_forward/pallas_call | solution.py:322
  84.7 10.9 %recurrent_forward.5 = (f32[8,128]{1,0:T(8,128)}, bf16[256,2048]{1,0:T(8,128)(2,1)S(1)}, f32[1024,640]{1,0:T(8,128)}, f32[1024,640]{1,0:T(8,128)}, bf16[1024,640...) custom-call(s32[1,3]{1,0:T(1,128)S(1)} %copy-done.46, ...), custom_call_target="tpu_custom_call", output_to_operand_aliasing={{2}: (7, {}), {3}: (8, {}), {4}: (9, {}), {5}: (10, {}), {6... | custom-call | flops 1 | bytes 1 | tf_op jit(solution)/shard_map/recurrent_forward/pallas_call | solution.py:322
  96.5 6.9 %collective-permute-start.20 = (bf16[128,2048]{1,0:T(8,128)(2,1)S(1)}, bf16[128,2048]{1,0:T(8,128)(2,1)S(1)}, u32[]{:S(2)}, u32[]{:S(2)}) collective-permute-start(bf16[128,2048]{1,0:T(8,128)(2,1)S(1)} %get-tuple-element.421.one), channel_id=1, source_target_pairs={{0,1},{3,2},{4,5},{7,6},{8,9},{11,10},{12,13},{15,14},{16,17},{19,... | collective-permute-start | bytes 1572872 | tf_op jit(solution)/shard_map/ppermute | solution.py:1188
  103.4 10.9 %recurrent_forward.6 = (f32[8,128]{1,0:T(8,128)}, bf16[256,2048]{1,0:T(8,128)(2,1)S(1)}, f32[1024,640]{1,0:T(8,128)}, f32[1024,640]{1,0:T(8,128)}, bf16[1024,640...) custom-call(s32[1,3]{1,0:T(1,128)S(1)} %copy-done.46, ...), custom_call_target="tpu_custom_call", output_to_operand_aliasing={{2}: (7, {}), {3}: (8, {}), {4}: (9, {}), {5}: (10, {}), {6... | custom-call | flops 1 | bytes 1 | tf_op jit(solution)/shard_map/recurrent_forward/pallas_call | solution.py:322
  120.6 7.4 %collective-permute-start.27 = (bf16[256,2048]{1,0:T(8,128)(2,1)S(1)}, bf16[256,2048]{1,0:T(8,128)(2,1)S(1)}, u32[]{:S(2)}, u32[]{:S(2)}) collective-permute-start(bf16[256,2048]{1,0:T(8,128)(2,1)S(1)} %get-tuple-element.442.one), channel_id=1, source_target_pairs={{0,1},{3,2},{4,5},{7,6},{8,9},{11,10},{12,13},{15,14},{16,17},{19,... | collective-permute-start | bytes 3145736 | tf_op jit(solution)/shard_map/ppermute | solution.py:1188
  136.2 10.9 %recurrent_forward.7 = (f32[8,128]{1,0:T(8,128)}, bf16[256,2048]{1,0:T(8,128)(2,1)S(1)}, f32[1024,640]{1,0:T(8,128)}, f32[1024,640]{1,0:T(8,128)}, bf16[1024,640...) custom-call(s32[1,3]{1,0:T(1,128)S(1)} %copy-done.46, ...), custom_call_target="tpu_custom_call", output_to_operand_aliasing={{2}: (7, {}), {3}: (8, {}), {4}: (9, {}), {5}: (10, {}), {6... | custom-call | flops 1 | bytes 1 | tf_op jit(solution)/shard_map/recurrent_forward/pallas_call | solution.py:322
  147.1 7.0 %collective-permute-done.30.refs_2_ = bf16[128,2048]{1,0:T(8,128)(2,1)S(1)} collective-permute-done((bf16[128,2048]{1,0:T(8,128)(2,1)S(1)}, bf16[128,2048]{1,0:T(8,128)(2,1)S(1)}, u32[]{:S(2)}, u32[]{:S(2)}) %collective-permute-start.30) | collective-permute-done | bytes 524320 | tf_op jit(solution)/shard_map/ppermute | solution.py:1196
  161.5 15.9 %ffn_chunk.4 = (f32[8,128]{1,0:T(8,128)}, bf16[1024,4608]{1,0:T(8,128)(2,1)}, bf16[1024,2048]{1,0:T(8,128)(2,1)}, bf16[1024,2048]{1,0:T(8,128)(2,1)}, f32[1024,1...) custom-call(s32[1]{0:T(128)} %bitcast.zed_ref, bf16[128,2048]{1,0:T(8,128)(2,1)} %copy-done.34, ...), custom_call_target="tpu_custom_call", output_to_operand_aliasing={{0}: (9, {})} | custom-call | flops 1 | bytes 1 | tf_op jit(solution)/shard_map/ffn_chunk/pallas_call | solution.py:322
  187.5 16.0 %ffn_chunk.5 = (f32[8,128]{1,0:T(8,128)}, bf16[1024,4608]{1,0:T(8,128)(2,1)}, bf16[1024,2048]{1,0:T(8,128)(2,1)}, bf16[1024,2048]{1,0:T(8,128)(2,1)}, f32[1024,1...) custom-call(s32[1]{0:T(128)} %bitcast.zed_ref, ...), custom_call_target="tpu_custom_call", output_to_operand_aliasing={{1}: (9, {}), {2}: (10, {}), {3}: (11, {}), {4}: (12, {}), ... | custom-call | flops 1 | bytes 1 | tf_op jit(solution)/shard_map/ffn_chunk/pallas_call | solution.py:322
  212.1 15.8 %ffn_chunk.6 = (f32[8,128]{1,0:T(8,128)}, bf16[1024,4608]{1,0:T(8,128)(2,1)}, bf16[1024,2048]{1,0:T(8,128)(2,1)}, bf16[1024,2048]{1,0:T(8,128)(2,1)}, f32[1024,1...) custom-call(s32[1]{0:T(128)} %bitcast.zed_ref, ...), custom_call_target="tpu_custom_call", output_to_operand_aliasing={{1}: (7, {}), {2}: (8, {}), {3}: (9, {}), {4}: (10, {}), {0... | custom-call | flops 1 | bytes 1 | tf_op jit(solution)/shard_map/ffn_chunk/pallas_call | solution.py:322
  236.7 15.9 %ffn_chunk.7 = (f32[8,128]{1,0:T(8,128)}, bf16[1024,4608]{1,0:T(8,128)(2,1)}, bf16[1024,2048]{1,0:T(8,128)(2,1)}, bf16[1024,2048]{1,0:T(8,128)(2,1)}, f32[1024,1...) custom-call(s32[1]{0:T(128)} %bitcast.zed_ref, ...), custom_call_target="tpu_custom_call", output_to_operand_aliasing={{1}: (7, {}), {2}: (8, {}), {3}: (9, {}), {4}: (10, {}), {0... | custom-call | flops 1 | bytes 1 | tf_op jit(solution)/shard_map/ffn_chunk/pallas_call | solution.py:322
  258.7 10.3 %rows_by_rows.3 = (f32[8,128]{1,0:T(8,128)}, bf16[256,2048]{1,0:T(8,128)(2,1)S(1)}, bf16[256,2048]{1,0:T(8,128)(2,1)S(1)}, bf16[256,2048]{1,0:T(8,128)(2,1)S(1)}, bf16[256,2048]{1,0:T(8,128)(2,1)S(1)}) custom-call(bf16[1024,4608]{1,0:T(8,128)(2,1)} %get-tuple-element.498.left.right, ...), custom_call_target="tpu_custom_call", output_to_operand_aliasing={{0}: (2, {})} | custom-call | flops 1 | bytes 1 | tf_op jit(solution)/shard_map/rows_by_rows/pallas_call | solution.py:322
  277.1 11.1 %unit_weight_grad.3 = (f32[8,128]{1,0:T(8,128)}, bf16[2048,4608]{1,0:T(8,128)(2,1)}) custom-call(bf16[1024,2048]{1,0:T(8,128)(2,1)} %get-tuple-element.510.left.normed_ref, bf16[1024,4608]{1,0:T(8,128)(2,1)} %get-tuple-element.498.left.right, f32[8,128]{1,0:T(8,128)} %get-tuple-element.513.refs_0_), custom_call_target="tpu_custom_call", output_to_operand_aliasing={{0}: (2, {})} | custom-call | flops 1 | bytes 1 | tf_op jit(solution)/shard_map/unit_weight_grad/pallas_call | solution.py:322
  290.9 11.2 %unit_weight_grad.4 = (f32[8,128]{1,0:T(8,128)}, bf16[2048,4608]{1,0:T(8,128)(2,1)}) custom-call(bf16[1024,2048]{1,0:T(8,128)(2,1)} %get-tuple-element.510.left.normed_ref, bf16[1024,4608]{1,0:T(8,128)(2,1)} %get-tuple-element.498.left.right, bf16[2048,4608]{1,0:T(8,128)(2,1)} %get-tuple-element.518.refs_0_, ...), custom_call_target="tpu_custom_call", output_to_operand_aliasing={{1}: (2, {}), {0}: (3, {})} | custom-call | flops 1 | bytes 1 | tf_op jit(solution)/shard_map/unit_weight_grad/pallas_call | solution.py:322
  302.1 11.5 %unit_weight_grad.5 = (f32[8,128]{1,0:T(8,128)}, bf16[2048,4608]{1,0:T(8,128)(2,1)}) custom-call(bf16[1024,2048]{1,0:T(8,128)(2,1)} %bitcast_convert_fusion.refs_6_.refs_4_.left, bf16[1024,4608]{1,0:T(8,128)(2,1)} %get-tuple-element.498.left.right, bf16[2048,4608]{1,0:T(8,128)(2,1)} %get-tuple-element.526.refs_0_, ...), custom_call_target="tpu_custom_call", output_to_operand_aliasing={{1}: (2, {}), {0}: (3, {})} | custom-call | flops 1 | bytes 1 | tf_op jit(solution)/shard_map/unit_weight_grad/pallas_call | solution.py:322
  354.2 14.7 %recurrent_backward.2 = (f32[8,128]{1,0:T(8,128)}, bf16[1024,1280]{1,0:T(8,128)(2,1)}, bf16[1024,1280]{1,0:T(8,128)(2,1)}, f32[32,640]{1,0:T(8,128)S(1)}) custom-call(s32[1,3]{1,0:T(1,128)S(1)} %copy-done.46, bf16[1024,2048]{1,0:T(8,128)(2,1)} %get-tuple-element.558.grad_ref.left, ...), custom_call_target="tpu_custom_call", output_to_operand_aliasing={{0}: (14, {})} | custom-call | flops 1 | bytes 1 | tf_op jit(solution)/shard_map/recurrent_backward/pallas_call | solution.py:322
  382.1 14.0 %recurrent_backward.3 = (f32[8,128]{1,0:T(8,128)}, bf16[1024,1280]{1,0:T(8,128)(2,1)}, bf16[1024,1280]{1,0:T(8,128)(2,1)}, f32[32,640]{1,0:T(8,128)S(1)}) custom-call(s32[1,3]{1,0:T(1,128)S(1)} %copy-done.46, bf16[1024,2048]{1,0:T(8,128)(2,1)} %get-tuple-element.558.grad_ref.left, ...), custom_call_target="tpu_custom_call", output_to_operand_aliasing={{1}: (14, {}), {2}: (15, {}), {0}: (16, {})} | custom-call | flops 1 | bytes 1 | tf_op jit(solution)/shard_map/recurrent_backward/pallas_call | solution.py:322
  403.8 11.6 %branch_weight_grad.2 = (f32[8,128]{1,0:T(8,128)}, bf16[8,832,640]{2,1,0:T(8,128)(2,1)}) custom-call(bf16[1024,2048]{1,0:T(8,128)(2,1)} %multiply_convert_fusion.refs_5_.refs_0_.left.normed, bf16[1024,1280]{1,0:T(8,128)(2,1)} %get-tuple-element.586.right.left, f32[8,128]{1,0:T(8,128)} %get-tuple-element.591.refs_0_), custom_call_target="tpu_custom_call", output_to_operand_aliasing={{0}: (2, {})} | custom-call | flops 1 | bytes 1 | tf_op jit(solution)/shard_map/branch_weight_grad/pallas_call | solution.py:322
  429.1 6.5 %rows_by_rows.5 = (f32[8,128]{1,0:T(8,128)}, bf16[128,2048]{1,0:T(8,128)(2,1)S(1)}, bf16[128,2048]{1,0:T(8,128)(2,1)S(1)}, bf16[128,2048]{1,0:T(8,128)(2,1)S(1)}...) custom-call(bf16[1024,1280]{1,0:T(8,128)(2,1)} %get-tuple-element.586.right.left, ...), custom_call_target="tpu_custom_call", output_to_operand_aliasing={{0}: (3, {})} | custom-call | flops 1 | bytes 1 | tf_op jit(solution)/shard_map/rows_by_rows/pallas_call | solution.py:322
  438.2 9.2 %branch_weight_grad.3 = (f32[8,128]{1,0:T(8,128)}, bf16[8,832,640]{2,1,0:T(8,128)(2,1)}) custom-call(bf16[1024,2048]{1,0:T(8,128)(2,1)} %get-tuple-element.558.grad_ref.left, bf16[1024,640]{1,0:T(8,128)(2,1)} %get-tuple-element.600.right, bf16[8,832,640]{2,1,0:T(8,128)(2,1)} %get-tuple-element.601.refs_0_, ...), custom_call_target="tpu_custom_call", output_to_operand_aliasing={{1}: (2, {}), {0}: (3, {})} | custom-call | flops 1 | bytes 1 | tf_op jit(solution)/shard_map/branch_weight_grad/pallas_call | solution.py:322
  452.1 7.1 %collective-permute-start.64 = (bf16[144,2048]{1,0:T(8,128)(2,1)}, bf16[144,2048]{1,0:T(8,128)(2,1)S(1)}, u32[]{:S(2)}, u32[]{:S(2)}) collective-permute-start(bf16[144,2048]{1,0:T(8,128)(2,1)} %copy-done.32), channel_id=1, source_target_pairs={{0,1},{3,2},{4,5},{7,6},{8,9},{11,10},{12,13},{15,14},{16,17},{19,... | collective-permute-start | bytes 1769480 | tf_op jit(solution)/shard_map/ppermute | solution.py:1188
  477.2 6.9 %collective-permute-start.67 = (bf16[128,2048]{1,0:T(8,128)(2,1)S(1)}, bf16[128,2048]{1,0:T(8,128)(2,1)S(1)}, u32[]{:S(2)}, u32[]{:S(2)}) collective-permute-start(bf16[128,2048]{1,0:T(8,128)(2,1)S(1)} %copy-done.41), channel_id=1, source_target_pairs={{0,1},{3,2},{4,5},{7,6},{8,9},{11,10},{12,13},{15,14},{16,17},{19,... | collective-permute-start | bytes 1572872 | tf_op jit(solution)/shard_map/ppermute | solution.py:1188
  (446 shorter events, 288.8 us)
Async XLA Ops:
  7.2 149.0 %all-gather.2.cloned.1.call-start = ((), (), s32[]{:S(2)}) async-start(), calls=%async_computation.2 | async-start | bytes 21233664 | tf_op jit(solution)/shard_map/all_gather | solution.py:1290
  48.7 401.4 %reduce-scatter.3.cloned.1.call-start = ((), (), s32[]{:S(2)}) async-start(), calls=%async_computation.3 | async-start | bytes 21233664 | tf_op jit(solution)/shard_map/reduce_scatter | solution.py:1455
  83.1 31.2 %collective-permute-start.22 = (bf16[128,2048]{1,0:T(8,128)(2,1)S(1)}, bf16[128,2048]{1,0:T(8,128)(2,1)S(1)}, u32[]{:S(2)}, u32[]{:S(2)}) collective-permute-start(bf16[128,2048]{1,0:T(8,128)(2,1)S(1)} %get-tuple-element.424.one), channel_id=1, source_target_pairs={{0,1},{3,2},{4,5},{7,6},{8,9},{11,10},{12,13},{15,14},{16,17},{19,... | collective-permute-start | bytes 1572872 | tf_op jit(solution)/shard_map/ppermute | solution.py:1188
  120.6 34.3 %collective-permute-start.27 = (bf16[256,2048]{1,0:T(8,128)(2,1)S(1)}, bf16[256,2048]{1,0:T(8,128)(2,1)S(1)}, u32[]{:S(2)}, u32[]{:S(2)}) collective-permute-start(bf16[256,2048]{1,0:T(8,128)(2,1)S(1)} %get-tuple-element.442.one), channel_id=1, source_target_pairs={{0,1},{3,2},{4,5},{7,6},{8,9},{11,10},{12,13},{15,14},{16,17},{19,... | collective-permute-start | bytes 3145736 | tf_op jit(solution)/shard_map/ppermute | solution.py:1188
  156.2 26.6 %collective-permute-start.31 = (bf16[256,2048]{1,0:T(8,128)(2,1)S(1)}, bf16[256,2048]{1,0:T(8,128)(2,1)}, u32[]{:S(2)}, u32[]{:S(2)}) collective-permute-start(bf16[256,2048]{1,0:T(8,128)(2,1)S(1)} %get-tuple-element.454.one), channel_id=1, source_target_pairs={{0,1},{3,2},{4,5},{7,6},{8,9},{11,10},{12,13},{15,14},{16,17},{19,... | collective-permute-start | bytes 3145736 | tf_op jit(solution)/shard_map/ppermute | solution.py:1188
  158.9 26.8 %collective-permute-start.35 = (bf16[256,2048]{1,0:T(8,128)(2,1)S(1)}, bf16[256,2048]{1,0:T(8,128)(2,1)S(1)}, u32[]{:S(2)}, u32[]{:S(2)}) collective-permute-start(bf16[256,2048]{1,0:T(8,128)(2,1)S(1)} %get-tuple-element.473.one), channel_id=1, source_target_pairs={{1,2},{2,1},{5,6},{6,5},{9,10},{10,9},{13,14},{14,13},{17,18},{18,... | collective-permute-start | bytes 3145736 | tf_op jit(solution)/shard_map/ppermute | solution.py:1192
  177.3 30.8 %collective-permute-start.34 = (bf16[256,2048]{1,0:T(8,128)(2,1)S(1)}, bf16[256,2048]{1,0:T(8,128)(2,1)S(1)}, u32[]{:S(2)}, u32[]{:S(2)}) collective-permute-start(bf16[256,2048]{1,0:T(8,128)(2,1)S(1)} %get-tuple-element.466.one), channel_id=1, source_target_pairs={{0,1},{3,2},{4,5},{7,6},{8,9},{11,10},{12,13},{15,14},{16,17},{19,... | collective-permute-start | bytes 3145736 | tf_op jit(solution)/shard_map/ppermute | solution.py:1188
  203.5 29.2 %collective-permute-start.39 = (bf16[256,2048]{1,0:T(8,128)(2,1)S(1)}, bf16[256,2048]{1,0:T(8,128)(2,1)S(1)}, u32[]{:S(2)}, u32[]{:S(2)}) collective-permute-start(bf16[256,2048]{1,0:T(8,128)(2,1)S(1)} %get-tuple-element.492.one), channel_id=1, source_target_pairs={{0,1},{3,2},{4,5},{7,6},{8,9},{11,10},{12,13},{15,14},{16,17},{19,... | collective-permute-start | bytes 3145736 | tf_op jit(solution)/shard_map/ppermute | solution.py:1188
  209.6 26.2 %collective-permute-start.36 = (bf16[256,2048]{1,0:T(8,128)(2,1)S(1)}, bf16[256,2048]{1,0:T(8,128)(2,1)S(1)}, u32[]{:S(2)}, u32[]{:S(2)}) collective-permute-start(bf16[256,2048]{1,0:T(8,128)(2,1)S(1)} %get-tuple-element.480.refs_0_), channel_id=1, source_target_pairs={{1,0},{2,3},{5,4},{6,7},{9,8},{10,11},{13,12},{14,15},{17,16},{18,... | collective-permute-start | bytes 3145736 | tf_op jit(solution)/shard_map/ppermute | solution.py:1196
  227.9 29.3 %collective-permute-start.42 = (bf16[256,2048]{1,0:T(8,128)(2,1)S(1)}, bf16[256,2048]{1,0:T(8,128)(2,1)S(1)}, u32[]{:S(2)}, u32[]{:S(2)}) collective-permute-start(bf16[256,2048]{1,0:T(8,128)(2,1)S(1)} %get-tuple-element.501.one), channel_id=1, source_target_pairs={{0,1},{3,2},{4,5},{7,6},{8,9},{11,10},{12,13},{15,14},{16,17},{19,... | collective-permute-start | bytes 3145736 | tf_op jit(solution)/shard_map/ppermute | solution.py:1188
  252.6 35.7 %collective-permute-start.43 = (bf16[256,2048]{1,0:T(8,128)(2,1)S(1)}, bf16[256,2048]{1,0:T(8,128)(2,1)S(1)}, u32[]{:S(2)}, u32[]{:S(2)}) collective-permute-start(bf16[256,2048]{1,0:T(8,128)(2,1)S(1)} %get-tuple-element.509.one), channel_id=1, source_target_pairs={{0,1},{3,2},{4,5},{7,6},{8,9},{11,10},{12,13},{15,14},{16,17},{19,... | collective-permute-start | bytes 3145736 | tf_op jit(solution)/shard_map/ppermute | solution.py:1188
  257.6 31.0 %collective-permute-start.45 = (bf16[256,2048]{1,0:T(8,128)(2,1)S(1)}, bf16[256,2048]{1,0:T(8,128)(2,1)S(1)}, u32[]{:S(2)}, u32[]{:S(2)}) collective-permute-start(bf16[256,2048]{1,0:T(8,128)(2,1)S(1)} %get-tuple-element.519.one), channel_id=1, source_target_pairs={{1,2},{2,1},{5,6},{6,5},{9,10},{10,9},{13,14},{14,13},{17,18},{18,... | collective-permute-start | bytes 3145736 | tf_op jit(solution)/shard_map/ppermute | solution.py:1192
  271.0 31.1 %collective-permute-start.44 = (bf16[256,2048]{1,0:T(8,128)(2,1)S(1)}, bf16[256,2048]{1,0:T(8,128)(2,1)S(1)}, u32[]{:S(2)}, u32[]{:S(2)}) collective-permute-start(bf16[256,2048]{1,0:T(8,128)(2,1)S(1)} %get-tuple-element.517.own), channel_id=1, source_target_pairs={{1,0},{2,3},{5,4},{6,7},{9,8},{10,11},{13,12},{14,15},{17,16},{18,... | collective-permute-start | bytes 3145736 | tf_op jit(solution)/shard_map/ppermute | solution.py:1196
  272.3 41.3 %collective-permute-start.46 = (bf16[256,2048]{1,0:T(8,128)(2,1)S(1)}, bf16[256,2048]{1,0:T(8,128)(2,1)S(1)}, u32[]{:S(2)}, u32[]{:S(2)}) collective-permute-start(bf16[256,2048]{1,0:T(8,128)(2,1)S(1)} %get-tuple-element.524.one), channel_id=1, source_target_pairs={{0,1},{3,2},{4,5},{7,6},{8,9},{11,10},{12,13},{15,14},{16,17},{19,... | collective-permute-start | bytes 3145736 | tf_op jit(solution)/shard_map/ppermute | solution.py:1188
  288.9 26.8 %collective-permute-start.48 = (bf16[256,2048]{1,0:T(8,128)(2,1)S(1)}, bf16[256,2048]{1,0:T(8,128)(2,1)S(1)}, u32[]{:S(2)}, u32[]{:S(2)}) collective-permute-start(bf16[256,2048]{1,0:T(8,128)(2,1)S(1)} %get-tuple-element.525.own), channel_id=1, source_target_pairs={{1,0},{2,3},{5,4},{6,7},{9,8},{10,11},{13,12},{14,15},{17,16},{18,... | collective-permute-start | bytes 3145736 | tf_op jit(solution)/shard_map/ppermute | solution.py:1196
  318.4 228.4 %reduce-scatter.5.cloned.1.call-start = ((), (), s32[]{:S(2)}) async-start(), calls=%async_computation.4 | async-start | bytes 9584640 | tf_op jit(solution)/shard_map/reduce_scatter | solution.py:1455
  318.4 27.7 %collective-permute-start.51 = (bf16[256,2048]{1,0:T(8,128)(2,1)}, bf16[256,2048]{1,0:T(8,128)(2,1)S(1)}, u32[]{:S(2)}, u32[]{:S(2)}) collective-permute-start(bf16[256,2048]{1,0:T(8,128)(2,1)} %copy-done.26), channel_id=1, source_target_pairs={{0,1},{3,2},{4,5},{7,6},{8,9},{11,10},{12,13},{15,14},{16,17},{19,... | collective-permute-start | bytes 3145736 | tf_op jit(solution)/shard_map/ppermute | solution.py:1188
  341.4 38.1 %collective-permute-start.55 = (bf16[256,2048]{1,0:T(8,128)(2,1)S(1)}, bf16[256,2048]{1,0:T(8,128)(2,1)S(1)}, u32[]{:S(2)}, u32[]{:S(2)}) collective-permute-start(bf16[256,2048]{1,0:T(8,128)(2,1)S(1)} %copy-done.25), channel_id=1, source_target_pairs={{0,1},{3,2},{4,5},{7,6},{8,9},{11,10},{12,13},{15,14},{16,17},{19,... | collective-permute-start | bytes 3145736 | tf_op jit(solution)/shard_map/ppermute | solution.py:1188
  346.5 34.0 %collective-permute-start.54 = (bf16[256,2048]{1,0:T(8,128)(2,1)S(1)}, bf16[256,2048]{1,0:T(8,128)(2,1)S(1)}, u32[]{:S(2)}, u32[]{:S(2)}) collective-permute-start(bf16[256,2048]{1,0:T(8,128)(2,1)S(1)} %get-tuple-element.574.one), channel_id=1, source_target_pairs={{1,2},{2,1},{5,6},{6,5},{9,10},{10,9},{13,14},{14,13},{17,18},{18,... | collective-permute-start | bytes 3145736 | tf_op jit(solution)/shard_map/ppermute | solution.py:1192
  347.5 34.6 %collective-permute-start.53 = (bf16[256,2048]{1,0:T(8,128)(2,1)S(1)}, bf16[256,2048]{1,0:T(8,128)(2,1)S(1)}, u32[]{:S(2)}, u32[]{:S(2)}) collective-permute-start(bf16[256,2048]{1,0:T(8,128)(2,1)S(1)} %get-tuple-element.573.own), channel_id=1, source_target_pairs={{1,0},{2,3},{5,4},{6,7},{9,8},{10,11},{13,12},{14,15},{17,16},{18,... | collective-permute-start | bytes 3145736 | tf_op jit(solution)/shard_map/ppermute | solution.py:1196
  374.9 26.1 %collective-permute-start.52 = (bf16[256,2048]{1,0:T(8,128)(2,1)S(1)}, bf16[256,2048]{1,0:T(8,128)(2,1)S(1)}, u32[]{:S(2)}, u32[]{:S(2)}) collective-permute-start(bf16[256,2048]{1,0:T(8,128)(2,1)S(1)} %copy-done.23), channel_id=1, source_target_pairs={{0,1},{3,2},{4,5},{7,6},{8,9},{11,10},{12,13},{15,14},{16,17},{19,... | collective-permute-start | bytes 3145736 | tf_op jit(solution)/shard_map/ppermute | solution.py:1188
  396.1 29.0 %collective-permute-start.57 = (bf16[256,2048]{1,0:T(8,128)(2,1)S(1)}, bf16[256,2048]{1,0:T(8,128)(2,1)S(1)}, u32[]{:S(2)}, u32[]{:S(2)}) collective-permute-start(bf16[256,2048]{1,0:T(8,128)(2,1)S(1)} %get-tuple-element.583.one), channel_id=1, source_target_pairs={{0,1},{3,2},{4,5},{7,6},{8,9},{11,10},{12,13},{15,14},{16,17},{19,... | collective-permute-start | bytes 3145736 | tf_op jit(solution)/shard_map/ppermute | solution.py:1188
  420.8 26.6 %collective-permute-start.62 = (bf16[256,2048]{1,0:T(8,128)(2,1)S(1)}, bf16[256,2048]{1,0:T(8,128)(2,1)S(1)}, u32[]{:S(2)}, u32[]{:S(2)}) collective-permute-start(bf16[256,2048]{1,0:T(8,128)(2,1)S(1)} %get-tuple-element.599.one), channel_id=1, source_target_pairs={{0,1},{3,2},{4,5},{7,6},{8,9},{11,10},{12,13},{15,14},{16,17},{19,... | collective-permute-start | bytes 3145736 | tf_op jit(solution)/shard_map/ppermute | solution.py:1188
  474.9 26.6 %collective-permute-start.72 = (bf16[256,2048]{1,0:T(8,128)(2,1)S(1)}, bf16[256,2048]{1,0:T(8,128)(2,1)S(1)}, u32[]{:S(2)}, u32[]{:S(2)}) collective-permute-start(bf16[256,2048]{1,0:T(8,128)(2,1)S(1)} %get-tuple-element.656.own), channel_id=1, source_target_pairs={{1,0},{2,3},{5,4},{6,7},{9,8},{10,11},{13,12},{14,15},{17,16},{18,... | collective-permute-start | bytes 3145736 | tf_op jit(solution)/shard_map/ppermute | solution.py:1196
  (140 other events, 1530.1 us)
Sparse Core Ops, SparseCore 0:
  48.8 99.0 all-gather.1
  318.5 126.2 reduce-scatter.2
  450.2 72.0 reduce-scatter.4

commit v4 on v3

--- a/solution.py
+++ b/solution.py
@@ -734,17 +734,28 @@
         pltpu.make_async_copy(acts, acts_out.at[out_rows], out_sem.at[1]),
     ]
     keep[0].start()
+
+    def finish(t, gate, value, inner_grad):
+        one, two, three = spans[t]
+        act, slope = gelu_parts(gate)
+        acts[:, one] = (inner_grad * value * slope).astype(BF)
+        acts[:, two] = (inner_grad * act).astype(BF)
+        acts[:, three] = (act * value).astype(BF)
+
+    ready = None
     for t in range(tiles):
         for copy in copies[t]:
             copy.wait()
         one, two, three = spans[t]
-        gate = nn_dot(normed[...], weight[:, one])
-        value = nn_dot(normed[...], weight[:, two])
-        inner_grad = nn_dot(cot_ref[...], weight[:, three])
-        act, slope = gelu_parts(gate)
-        acts[:, one] = (inner_grad * value * slope).astype(BF)
-        acts[:, two] = (inner_grad * act).astype(BF)
-        acts[:, three] = (act * value).astype(BF)
+        made = (
+            nn_dot(normed[...], weight[:, one]),
+            nn_dot(normed[...], weight[:, two]),
+            nn_dot(cot_ref[...], weight[:, three]),
+        )
+        if ready is not None:
+            finish(t - 1, *ready)
+        ready = made
+    finish(tiles - 1, *ready)
     keep[1].start()
     for n in range(width // FTILE):
         span = slice(n * FTILE, (n + 1) * FTILE)

time: 568 us -> 571 us (level)
  no operation moved by 1% of the time
where the time goes in v4:
time: 571 us; the launch traced here: 560 us
  Pallas kernels  300 us (53%)
  starting transfers between devices  155 us (27%)
  waiting for transfers between devices  34.9 us (6%)
  other arithmetic  28.9 us (5%)
  local copies, waits for them, and re-layouts  25 us (4%)
  between operations  16.5 us (3%)
    pallas_call x79, Pallas kernels, ordered(): pl.pallas_call(body, in_specs=[*in_specs, anywhere], out_specs=[anywhere,...  294 us
    ppermute x20, starting transfers between devices, inward(): return lax.ppermute(value, 'tensor', [(0, 1), (3, 2)])  92.4 us
    ppermute x20, starting transfers between devices, outward(): return lax.ppermute(value, 'tensor', [(1, 0), (2, 3)])  27.6 us
    ppermute x20, waiting for transfers between devices, outward(): return lax.ppermute(value, 'tensor', [(1, 0), (2, 3)])  24.1 us
    ppermute x22, starting transfers between devices, swap_dp(): return lax.ppermute(value, 'dp', [(i, i ^ bit) for i in range(8)])  20.8 us
    unnamed x163, local copies, waits for them, and re-layouts  17 us
    ppermute x20, starting transfers between devices, across(): return lax.ppermute(value, 'tensor', [(1, 2), (2, 1)])  14.3 us
  transfers between devices with their start and end apart: 85, of which 12 were waited for; matrix products, arithmetic and copies ran while one was open for 6% of the time, Pallas kernels for 53%

profile of v4, /device:TPU:0, one launch (start us, length us, event | category | flops | bytes accessed | tf_op | source)
XLA Modules:
  0.0 560.3 jit_solution(4362660208112605075)
XLA Ops:
  15.9 6.3 %bitcast_convert_fusion.refs_6_.refs_4_.left = bf16[1024,2048]{1,0:T(8,128)(2,1)} fusion(f32[1,1024,2048]{2,1,0:T(8,128)} %param.39), kind=kLoop, calls=%fused_computation.47 | loop fusion | flops 2097152 | bytes 12582912 | tf_op jit(solution)/shard_map/convert_element_type | solution.py:1291
  34.2 6.1 %multiply_convert_fusion.refs_5_.refs_0_.left.normed = bf16[1024,2048]{1,0:T(8,128)(2,1)} fusion(f32[2048]{0:T(1024)S(1)} %copy-done.56, f32[1024]{0:T(1024)S(1)} %add_rsqrt_fusion, f32[1,1024,2048]{2,1,0:T(8,128)} %param.20), kind=kLoop, calls=%fused_computation | loop fusion | flops 6291456 | bytes 12595200 | tf_op jit(solution)/shard_map/convert_element_type | solution.py:1295
  64.8 8.8 %recurrent_forward.4 = (f32[8,128]{1,0:T(8,128)}, bf16[2048,1280]{1,0:T(8,128)(2,1)}, f32[1024,640]{1,0:T(8,128)}, f32[1024,640]{1,0:T(8,128)}, bf16[1024,640]{1...) custom-call(s32[1,3]{1,0:T(1,128)S(1)} %copy-done.46, ...), custom_call_target="tpu_custom_call", output_to_operand_aliasing={{0}: (10, {})} | custom-call | flops 1 | bytes 1 | tf_op jit(solution)/shard_map/recurrent_forward/pallas_call | solution.py:322
  84.7 10.9 %recurrent_forward.5 = (f32[8,128]{1,0:T(8,128)}, bf16[256,2048]{1,0:T(8,128)(2,1)S(1)}, f32[1024,640]{1,0:T(8,128)}, f32[1024,640]{1,0:T(8,128)}, bf16[1024,640...) custom-call(s32[1,3]{1,0:T(1,128)S(1)} %copy-done.46, ...), custom_call_target="tpu_custom_call", output_to_operand_aliasing={{2}: (7, {}), {3}: (8, {}), {4}: (9, {}), {5}: (10, {}), {6... | custom-call | flops 1 | bytes 1 | tf_op jit(solution)/shard_map/recurrent_forward/pallas_call | solution.py:322
  96.5 6.9 %collective-permute-start.20 = (bf16[128,2048]{1,0:T(8,128)(2,1)S(1)}, bf16[128,2048]{1,0:T(8,128)(2,1)S(1)}, u32[]{:S(2)}, u32[]{:S(2)}) collective-permute-start(bf16[128,2048]{1,0:T(8,128)(2,1)S(1)} %get-tuple-element.421.one), channel_id=1, source_target_pairs={{0,1},{3,2},{4,5},{7,6},{8,9},{11,10},{12,13},{15,14},{16,17},{19,... | collective-permute-start | bytes 1572872 | tf_op jit(solution)/shard_map/ppermute | solution.py:1199
  103.4 10.9 %recurrent_forward.6 = (f32[8,128]{1,0:T(8,128)}, bf16[256,2048]{1,0:T(8,128)(2,1)S(1)}, f32[1024,640]{1,0:T(8,128)}, f32[1024,640]{1,0:T(8,128)}, bf16[1024,640...) custom-call(s32[1,3]{1,0:T(1,128)S(1)} %copy-done.46, ...), custom_call_target="tpu_custom_call", output_to_operand_aliasing={{2}: (7, {}), {3}: (8, {}), {4}: (9, {}), {5}: (10, {}), {6... | custom-call | flops 1 | bytes 1 | tf_op jit(solution)/shard_map/recurrent_forward/pallas_call | solution.py:322
  120.6 7.4 %collective-permute-start.27 = (bf16[256,2048]{1,0:T(8,128)(2,1)S(1)}, bf16[256,2048]{1,0:T(8,128)(2,1)S(1)}, u32[]{:S(2)}, u32[]{:S(2)}) collective-permute-start(bf16[256,2048]{1,0:T(8,128)(2,1)S(1)} %get-tuple-element.442.one), channel_id=1, source_target_pairs={{0,1},{3,2},{4,5},{7,6},{8,9},{11,10},{12,13},{15,14},{16,17},{19,... | collective-permute-start | bytes 3145736 | tf_op jit(solution)/shard_map/ppermute | solution.py:1199
  136.2 10.9 %recurrent_forward.7 = (f32[8,128]{1,0:T(8,128)}, bf16[256,2048]{1,0:T(8,128)(2,1)S(1)}, f32[1024,640]{1,0:T(8,128)}, f32[1024,640]{1,0:T(8,128)}, bf16[1024,640...) custom-call(s32[1,3]{1,0:T(1,128)S(1)} %copy-done.46, ...), custom_call_target="tpu_custom_call", output_to_operand_aliasing={{2}: (7, {}), {3}: (8, {}), {4}: (9, {}), {5}: (10, {}), {6... | custom-call | flops 1 | bytes 1 | tf_op jit(solution)/shard_map/recurrent_forward/pallas_call | solution.py:322
  147.1 7.0 %collective-permute-done.30.refs_2_ = bf16[128,2048]{1,0:T(8,128)(2,1)S(1)} collective-permute-done((bf16[128,2048]{1,0:T(8,128)(2,1)S(1)}, bf16[128,2048]{1,0:T(8,128)(2,1)S(1)}, u32[]{:S(2)}, u32[]{:S(2)}) %collective-permute-start.30) | collective-permute-done | bytes 524320 | tf_op jit(solution)/shard_map/ppermute | solution.py:1207
  161.5 16.5 %ffn_chunk.4 = (f32[8,128]{1,0:T(8,128)}, bf16[1024,4608]{1,0:T(8,128)(2,1)}, bf16[1024,2048]{1,0:T(8,128)(2,1)}, bf16[1024,2048]{1,0:T(8,128)(2,1)}, f32[1024,1...) custom-call(s32[1]{0:T(128)} %bitcast.zed_ref, bf16[128,2048]{1,0:T(8,128)(2,1)} %copy-done.34, ...), custom_call_target="tpu_custom_call", output_to_operand_aliasing={{0}: (9, {})} | custom-call | flops 1 | bytes 1 | tf_op jit(solution)/shard_map/ffn_chunk/pallas_call | solution.py:322
  188.1 16.5 %ffn_chunk.5 = (f32[8,128]{1,0:T(8,128)}, bf16[1024,4608]{1,0:T(8,128)(2,1)}, bf16[1024,2048]{1,0:T(8,128)(2,1)}, bf16[1024,2048]{1,0:T(8,128)(2,1)}, f32[1024,1...) custom-call(s32[1]{0:T(128)} %bitcast.zed_ref, ...), custom_call_target="tpu_custom_call", output_to_operand_aliasing={{1}: (9, {}), {2}: (10, {}), {3}: (11, {}), {4}: (12, {}), ... | custom-call | flops 1 | bytes 1 | tf_op jit(solution)/shard_map/ffn_chunk/pallas_call | solution.py:322
  213.3 16.4 %ffn_chunk.6 = (f32[8,128]{1,0:T(8,128)}, bf16[1024,4608]{1,0:T(8,128)(2,1)}, bf16[1024,2048]{1,0:T(8,128)(2,1)}, bf16[1024,2048]{1,0:T(8,128)(2,1)}, f32[1024,1...) custom-call(s32[1]{0:T(128)} %bitcast.zed_ref, ...), custom_call_target="tpu_custom_call", output_to_operand_aliasing={{1}: (7, {}), {2}: (8, {}), {3}: (9, {}), {4}: (10, {}), {0... | custom-call | flops 1 | bytes 1 | tf_op jit(solution)/shard_map/ffn_chunk/pallas_call | solution.py:322
  238.5 16.5 %ffn_chunk.7 = (f32[8,128]{1,0:T(8,128)}, bf16[1024,4608]{1,0:T(8,128)(2,1)}, bf16[1024,2048]{1,0:T(8,128)(2,1)}, bf16[1024,2048]{1,0:T(8,128)(2,1)}, f32[1024,1...) custom-call(s32[1]{0:T(128)} %bitcast.zed_ref, ...), custom_call_target="tpu_custom_call", output_to_operand_aliasing={{1}: (7, {}), {2}: (8, {}), {3}: (9, {}), {4}: (10, {}), {0... | custom-call | flops 1 | bytes 1 | tf_op jit(solution)/shard_map/ffn_chunk/pallas_call | solution.py:322
  261.1 10.3 %rows_by_rows.3 = (f32[8,128]{1,0:T(8,128)}, bf16[256,2048]{1,0:T(8,128)(2,1)S(1)}, bf16[256,2048]{1,0:T(8,128)(2,1)S(1)}, bf16[256,2048]{1,0:T(8,128)(2,1)S(1)}, bf16[256,2048]{1,0:T(8,128)(2,1)S(1)}) custom-call(bf16[1024,4608]{1,0:T(8,128)(2,1)} %get-tuple-element.498.left.right, ...), custom_call_target="tpu_custom_call", output_to_operand_aliasing={{0}: (2, {})} | custom-call | flops 1 | bytes 1 | tf_op jit(solution)/shard_map/rows_by_rows/pallas_call | solution.py:322
  279.5 11.1 %unit_weight_grad.3 = (f32[8,128]{1,0:T(8,128)}, bf16[2048,4608]{1,0:T(8,128)(2,1)}) custom-call(bf16[1024,2048]{1,0:T(8,128)(2,1)} %get-tuple-element.510.left.normed_ref, bf16[1024,4608]{1,0:T(8,128)(2,1)} %get-tuple-element.498.left.right, f32[8,128]{1,0:T(8,128)} %get-tuple-element.513.refs_0_), custom_call_target="tpu_custom_call", output_to_operand_aliasing={{0}: (2, {})} | custom-call | flops 1 | bytes 1 | tf_op jit(solution)/shard_map/unit_weight_grad/pallas_call | solution.py:322
  293.3 11.2 %unit_weight_grad.4 = (f32[8,128]{1,0:T(8,128)}, bf16[2048,4608]{1,0:T(8,128)(2,1)}) custom-call(bf16[1024,2048]{1,0:T(8,128)(2,1)} %get-tuple-element.510.left.normed_ref, bf16[1024,4608]{1,0:T(8,128)(2,1)} %get-tuple-element.498.left.right, bf16[2048,4608]{1,0:T(8,128)(2,1)} %get-tuple-element.518.refs_0_, ...), custom_call_target="tpu_custom_call", output_to_operand_aliasing={{1}: (2, {}), {0}: (3, {})} | custom-call | flops 1 | bytes 1 | tf_op jit(solution)/shard_map/unit_weight_grad/pallas_call | solution.py:322
  304.5 11.5 %unit_weight_grad.5 = (f32[8,128]{1,0:T(8,128)}, bf16[2048,4608]{1,0:T(8,128)(2,1)}) custom-call(bf16[1024,2048]{1,0:T(8,128)(2,1)} %bitcast_convert_fusion.refs_6_.refs_4_.left, bf16[1024,4608]{1,0:T(8,128)(2,1)} %get-tuple-element.498.left.right, bf16[2048,4608]{1,0:T(8,128)(2,1)} %get-tuple-element.526.refs_0_, ...), custom_call_target="tpu_custom_call", output_to_operand_aliasing={{1}: (2, {}), {0}: (3, {})} | custom-call | flops 1 | bytes 1 | tf_op jit(solution)/shard_map/unit_weight_grad/pallas_call | solution.py:322
  356.6 14.7 %recurrent_backward.2 = (f32[8,128]{1,0:T(8,128)}, bf16[1024,1280]{1,0:T(8,128)(2,1)}, bf16[1024,1280]{1,0:T(8,128)(2,1)}, f32[32,640]{1,0:T(8,128)S(1)}) custom-call(s32[1,3]{1,0:T(1,128)S(1)} %copy-done.46, bf16[1024,2048]{1,0:T(8,128)(2,1)} %get-tuple-element.558.grad_ref.left, ...), custom_call_target="tpu_custom_call", output_to_operand_aliasing={{0}: (14, {})} | custom-call | flops 1 | bytes 1 | tf_op jit(solution)/shard_map/recurrent_backward/pallas_call | solution.py:322
  384.5 14.0 %recurrent_backward.3 = (f32[8,128]{1,0:T(8,128)}, bf16[1024,1280]{1,0:T(8,128)(2,1)}, bf16[1024,1280]{1,0:T(8,128)(2,1)}, f32[32,640]{1,0:T(8,128)S(1)}) custom-call(s32[1,3]{1,0:T(1,128)S(1)} %copy-done.46, bf16[1024,2048]{1,0:T(8,128)(2,1)} %get-tuple-element.558.grad_ref.left, ...), custom_call_target="tpu_custom_call", output_to_operand_aliasing={{1}: (14, {}), {2}: (15, {}), {0}: (16, {})} | custom-call | flops 1 | bytes 1 | tf_op jit(solution)/shard_map/recurrent_backward/pallas_call | solution.py:322
  406.2 11.6 %branch_weight_grad.2 = (f32[8,128]{1,0:T(8,128)}, bf16[8,832,640]{2,1,0:T(8,128)(2,1)}) custom-call(bf16[1024,2048]{1,0:T(8,128)(2,1)} %multiply_convert_fusion.refs_5_.refs_0_.left.normed, bf16[1024,1280]{1,0:T(8,128)(2,1)} %get-tuple-element.586.right.left, f32[8,128]{1,0:T(8,128)} %get-tuple-element.591.refs_0_), custom_call_target="tpu_custom_call", output_to_operand_aliasing={{0}: (2, {})} | custom-call | flops 1 | bytes 1 | tf_op jit(solution)/shard_map/branch_weight_grad/pallas_call | solution.py:322
  431.5 6.5 %rows_by_rows.5 = (f32[8,128]{1,0:T(8,128)}, bf16[128,2048]{1,0:T(8,128)(2,1)S(1)}, bf16[128,2048]{1,0:T(8,128)(2,1)S(1)}, bf16[128,2048]{1,0:T(8,128)(2,1)S(1)}...) custom-call(bf16[1024,1280]{1,0:T(8,128)(2,1)} %get-tuple-element.586.right.left, ...), custom_call_target="tpu_custom_call", output_to_operand_aliasing={{0}: (3, {})} | custom-call | flops 1 | bytes 1 | tf_op jit(solution)/shard_map/rows_by_rows/pallas_call | solution.py:322
  440.6 9.2 %branch_weight_grad.3 = (f32[8,128]{1,0:T(8,128)}, bf16[8,832,640]{2,1,0:T(8,128)(2,1)}) custom-call(bf16[1024,2048]{1,0:T(8,128)(2,1)} %get-tuple-element.558.grad_ref.left, bf16[1024,640]{1,0:T(8,128)(2,1)} %get-tuple-element.600.right, bf16[8,832,640]{2,1,0:T(8,128)(2,1)} %get-tuple-element.601.refs_0_, ...), custom_call_target="tpu_custom_call", output_to_operand_aliasing={{1}: (2, {}), {0}: (3, {})} | custom-call | flops 1 | bytes 1 | tf_op jit(solution)/shard_map/branch_weight_grad/pallas_call | solution.py:322
  454.5 7.1 %collective-permute-start.64 = (bf16[144,2048]{1,0:T(8,128)(2,1)}, bf16[144,2048]{1,0:T(8,128)(2,1)S(1)}, u32[]{:S(2)}, u32[]{:S(2)}) collective-permute-start(bf16[144,2048]{1,0:T(8,128)(2,1)} %copy-done.32), channel_id=1, source_target_pairs={{0,1},{3,2},{4,5},{7,6},{8,9},{11,10},{12,13},{15,14},{16,17},{19,... | collective-permute-start | bytes 1769480 | tf_op jit(solution)/shard_map/ppermute | solution.py:1199
  479.5 7.1 %collective-permute-start.67 = (bf16[128,2048]{1,0:T(8,128)(2,1)S(1)}, bf16[128,2048]{1,0:T(8,128)(2,1)S(1)}, u32[]{:S(2)}, u32[]{:S(2)}) collective-permute-start(bf16[128,2048]{1,0:T(8,128)(2,1)S(1)} %copy-done.41), channel_id=1, source_target_pairs={{0,1},{3,2},{4,5},{7,6},{8,9},{11,10},{12,13},{15,14},{16,17},{19,... | collective-permute-start | bytes 1572872 | tf_op jit(solution)/shard_map/ppermute | solution.py:1199
  (446 shorter events, 288.7 us)
Async XLA Ops:
  7.2 149.0 %all-gather.2.cloned.1.call-start = ((), (), s32[]{:S(2)}) async-start(), calls=%async_computation.2 | async-start | bytes 21233664 | tf_op jit(solution)/shard_map/all_gather | solution.py:1301
  48.7 403.8 %reduce-scatter.3.cloned.1.call-start = ((), (), s32[]{:S(2)}) async-start(), calls=%async_computation.3 | async-start | bytes 21233664 | tf_op jit(solution)/shard_map/reduce_scatter | solution.py:1466
  83.1 31.2 %collective-permute-start.22 = (bf16[128,2048]{1,0:T(8,128)(2,1)S(1)}, bf16[128,2048]{1,0:T(8,128)(2,1)S(1)}, u32[]{:S(2)}, u32[]{:S(2)}) collective-permute-start(bf16[128,2048]{1,0:T(8,128)(2,1)S(1)} %get-tuple-element.424.one), channel_id=1, source_target_pairs={{0,1},{3,2},{4,5},{7,6},{8,9},{11,10},{12,13},{15,14},{16,17},{19,... | collective-permute-start | bytes 1572872 | tf_op jit(solution)/shard_map/ppermute | solution.py:1199
  120.6 34.3 %collective-permute-start.27 = (bf16[256,2048]{1,0:T(8,128)(2,1)S(1)}, bf16[256,2048]{1,0:T(8,128)(2,1)S(1)}, u32[]{:S(2)}, u32[]{:S(2)}) collective-permute-start(bf16[256,2048]{1,0:T(8,128)(2,1)S(1)} %get-tuple-element.442.one), channel_id=1, source_target_pairs={{0,1},{3,2},{4,5},{7,6},{8,9},{11,10},{12,13},{15,14},{16,17},{19,... | collective-permute-start | bytes 3145736 | tf_op jit(solution)/shard_map/ppermute | solution.py:1199
  156.2 27.1 %collective-permute-start.31 = (bf16[256,2048]{1,0:T(8,128)(2,1)S(1)}, bf16[256,2048]{1,0:T(8,128)(2,1)}, u32[]{:S(2)}, u32[]{:S(2)}) collective-permute-start(bf16[256,2048]{1,0:T(8,128)(2,1)S(1)} %get-tuple-element.454.one), channel_id=1, source_target_pairs={{0,1},{3,2},{4,5},{7,6},{8,9},{11,10},{12,13},{15,14},{16,17},{19,... | collective-permute-start | bytes 3145736 | tf_op jit(solution)/shard_map/ppermute | solution.py:1199
  158.9 27.4 %collective-permute-start.35 = (bf16[256,2048]{1,0:T(8,128)(2,1)S(1)}, bf16[256,2048]{1,0:T(8,128)(2,1)S(1)}, u32[]{:S(2)}, u32[]{:S(2)}) collective-permute-start(bf16[256,2048]{1,0:T(8,128)(2,1)S(1)} %get-tuple-element.473.one), channel_id=1, source_target_pairs={{1,2},{2,1},{5,6},{6,5},{9,10},{10,9},{13,14},{14,13},{17,18},{18,... | collective-permute-start | bytes 3145736 | tf_op jit(solution)/shard_map/ppermute | solution.py:1203
  177.9 31.4 %collective-permute-start.34 = (bf16[256,2048]{1,0:T(8,128)(2,1)S(1)}, bf16[256,2048]{1,0:T(8,128)(2,1)S(1)}, u32[]{:S(2)}, u32[]{:S(2)}) collective-permute-start(bf16[256,2048]{1,0:T(8,128)(2,1)S(1)} %get-tuple-element.466.one), channel_id=1, source_target_pairs={{0,1},{3,2},{4,5},{7,6},{8,9},{11,10},{12,13},{15,14},{16,17},{19,... | collective-permute-start | bytes 3145736 | tf_op jit(solution)/shard_map/ppermute | solution.py:1199
  204.7 29.8 %collective-permute-start.39 = (bf16[256,2048]{1,0:T(8,128)(2,1)S(1)}, bf16[256,2048]{1,0:T(8,128)(2,1)S(1)}, u32[]{:S(2)}, u32[]{:S(2)}) collective-permute-start(bf16[256,2048]{1,0:T(8,128)(2,1)S(1)} %get-tuple-element.492.one), channel_id=1, source_target_pairs={{0,1},{3,2},{4,5},{7,6},{8,9},{11,10},{12,13},{15,14},{16,17},{19,... | collective-permute-start | bytes 3145736 | tf_op jit(solution)/shard_map/ppermute | solution.py:1199
  210.8 26.8 %collective-permute-start.36 = (bf16[256,2048]{1,0:T(8,128)(2,1)S(1)}, bf16[256,2048]{1,0:T(8,128)(2,1)S(1)}, u32[]{:S(2)}, u32[]{:S(2)}) collective-permute-start(bf16[256,2048]{1,0:T(8,128)(2,1)S(1)} %get-tuple-element.480.refs_0_), channel_id=1, source_target_pairs={{1,0},{2,3},{5,4},{6,7},{9,8},{10,11},{13,12},{14,15},{17,16},{18,... | collective-permute-start | bytes 3145736 | tf_op jit(solution)/shard_map/ppermute | solution.py:1207
  229.7 29.9 %collective-permute-start.42 = (bf16[256,2048]{1,0:T(8,128)(2,1)S(1)}, bf16[256,2048]{1,0:T(8,128)(2,1)S(1)}, u32[]{:S(2)}, u32[]{:S(2)}) collective-permute-start(bf16[256,2048]{1,0:T(8,128)(2,1)S(1)} %get-tuple-element.501.one), channel_id=1, source_target_pairs={{0,1},{3,2},{4,5},{7,6},{8,9},{11,10},{12,13},{15,14},{16,17},{19,... | collective-permute-start | bytes 3145736 | tf_op jit(solution)/shard_map/ppermute | solution.py:1199
  255.0 35.7 %collective-permute-start.43 = (bf16[256,2048]{1,0:T(8,128)(2,1)S(1)}, bf16[256,2048]{1,0:T(8,128)(2,1)S(1)}, u32[]{:S(2)}, u32[]{:S(2)}) collective-permute-start(bf16[256,2048]{1,0:T(8,128)(2,1)S(1)} %get-tuple-element.509.one), channel_id=1, source_target_pairs={{0,1},{3,2},{4,5},{7,6},{8,9},{11,10},{12,13},{15,14},{16,17},{19,... | collective-permute-start | bytes 3145736 | tf_op jit(solution)/shard_map/ppermute | solution.py:1199
  260.0 31.0 %collective-permute-start.45 = (bf16[256,2048]{1,0:T(8,128)(2,1)S(1)}, bf16[256,2048]{1,0:T(8,128)(2,1)S(1)}, u32[]{:S(2)}, u32[]{:S(2)}) collective-permute-start(bf16[256,2048]{1,0:T(8,128)(2,1)S(1)} %get-tuple-element.519.one), channel_id=1, source_target_pairs={{1,2},{2,1},{5,6},{6,5},{9,10},{10,9},{13,14},{14,13},{17,18},{18,... | collective-permute-start | bytes 3145736 | tf_op jit(solution)/shard_map/ppermute | solution.py:1203
  273.4 31.1 %collective-permute-start.44 = (bf16[256,2048]{1,0:T(8,128)(2,1)S(1)}, bf16[256,2048]{1,0:T(8,128)(2,1)S(1)}, u32[]{:S(2)}, u32[]{:S(2)}) collective-permute-start(bf16[256,2048]{1,0:T(8,128)(2,1)S(1)} %get-tuple-element.517.own), channel_id=1, source_target_pairs={{1,0},{2,3},{5,4},{6,7},{9,8},{10,11},{13,12},{14,15},{17,16},{18,... | collective-permute-start | bytes 3145736 | tf_op jit(solution)/shard_map/ppermute | solution.py:1207
  274.7 41.3 %collective-permute-start.46 = (bf16[256,2048]{1,0:T(8,128)(2,1)S(1)}, bf16[256,2048]{1,0:T(8,128)(2,1)S(1)}, u32[]{:S(2)}, u32[]{:S(2)}) collective-permute-start(bf16[256,2048]{1,0:T(8,128)(2,1)S(1)} %get-tuple-element.524.one), channel_id=1, source_target_pairs={{0,1},{3,2},{4,5},{7,6},{8,9},{11,10},{12,13},{15,14},{16,17},{19,... | collective-permute-start | bytes 3145736 | tf_op jit(solution)/shard_map/ppermute | solution.py:1199
  291.3 26.8 %collective-permute-start.48 = (bf16[256,2048]{1,0:T(8,128)(2,1)S(1)}, bf16[256,2048]{1,0:T(8,128)(2,1)S(1)}, u32[]{:S(2)}, u32[]{:S(2)}) collective-permute-start(bf16[256,2048]{1,0:T(8,128)(2,1)S(1)} %get-tuple-element.525.own), channel_id=1, source_target_pairs={{1,0},{2,3},{5,4},{6,7},{9,8},{10,11},{13,12},{14,15},{17,16},{18,... | collective-permute-start | bytes 3145736 | tf_op jit(solution)/shard_map/ppermute | solution.py:1207
  320.7 228.4 %reduce-scatter.5.cloned.1.call-start = ((), (), s32[]{:S(2)}) async-start(), calls=%async_computation.4 | async-start | bytes 9584640 | tf_op jit(solution)/shard_map/reduce_scatter | solution.py:1466
  320.8 27.7 %collective-permute-start.51 = (bf16[256,2048]{1,0:T(8,128)(2,1)}, bf16[256,2048]{1,0:T(8,128)(2,1)S(1)}, u32[]{:S(2)}, u32[]{:S(2)}) collective-permute-start(bf16[256,2048]{1,0:T(8,128)(2,1)} %copy-done.26), channel_id=1, source_target_pairs={{0,1},{3,2},{4,5},{7,6},{8,9},{11,10},{12,13},{15,14},{16,17},{19,... | collective-permute-start | bytes 3145736 | tf_op jit(solution)/shard_map/ppermute | solution.py:1199
  343.7 38.1 %collective-permute-start.55 = (bf16[256,2048]{1,0:T(8,128)(2,1)S(1)}, bf16[256,2048]{1,0:T(8,128)(2,1)S(1)}, u32[]{:S(2)}, u32[]{:S(2)}) collective-permute-start(bf16[256,2048]{1,0:T(8,128)(2,1)S(1)} %copy-done.25), channel_id=1, source_target_pairs={{0,1},{3,2},{4,5},{7,6},{8,9},{11,10},{12,13},{15,14},{16,17},{19,... | collective-permute-start | bytes 3145736 | tf_op jit(solution)/shard_map/ppermute | solution.py:1199
  348.9 34.0 %collective-permute-start.54 = (bf16[256,2048]{1,0:T(8,128)(2,1)S(1)}, bf16[256,2048]{1,0:T(8,128)(2,1)S(1)}, u32[]{:S(2)}, u32[]{:S(2)}) collective-permute-start(bf16[256,2048]{1,0:T(8,128)(2,1)S(1)} %get-tuple-element.574.one), channel_id=1, source_target_pairs={{1,2},{2,1},{5,6},{6,5},{9,10},{10,9},{13,14},{14,13},{17,18},{18,... | collective-permute-start | bytes 3145736 | tf_op jit(solution)/shard_map/ppermute | solution.py:1203
  349.9 34.6 %collective-permute-start.53 = (bf16[256,2048]{1,0:T(8,128)(2,1)S(1)}, bf16[256,2048]{1,0:T(8,128)(2,1)S(1)}, u32[]{:S(2)}, u32[]{:S(2)}) collective-permute-start(bf16[256,2048]{1,0:T(8,128)(2,1)S(1)} %get-tuple-element.573.own), channel_id=1, source_target_pairs={{1,0},{2,3},{5,4},{6,7},{9,8},{10,11},{13,12},{14,15},{17,16},{18,... | collective-permute-start | bytes 3145736 | tf_op jit(solution)/shard_map/ppermute | solution.py:1207
  377.4 26.1 %collective-permute-start.52 = (bf16[256,2048]{1,0:T(8,128)(2,1)S(1)}, bf16[256,2048]{1,0:T(8,128)(2,1)S(1)}, u32[]{:S(2)}, u32[]{:S(2)}) collective-permute-start(bf16[256,2048]{1,0:T(8,128)(2,1)S(1)} %copy-done.23), channel_id=1, source_target_pairs={{0,1},{3,2},{4,5},{7,6},{8,9},{11,10},{12,13},{15,14},{16,17},{19,... | collective-permute-start | bytes 3145736 | tf_op jit(solution)/shard_map/ppermute | solution.py:1199
  398.5 29.0 %collective-permute-start.57 = (bf16[256,2048]{1,0:T(8,128)(2,1)S(1)}, bf16[256,2048]{1,0:T(8,128)(2,1)S(1)}, u32[]{:S(2)}, u32[]{:S(2)}) collective-permute-start(bf16[256,2048]{1,0:T(8,128)(2,1)S(1)} %get-tuple-element.583.one), channel_id=1, source_target_pairs={{0,1},{3,2},{4,5},{7,6},{8,9},{11,10},{12,13},{15,14},{16,17},{19,... | collective-permute-start | bytes 3145736 | tf_op jit(solution)/shard_map/ppermute | solution.py:1199
  423.2 26.5 %collective-permute-start.62 = (bf16[256,2048]{1,0:T(8,128)(2,1)S(1)}, bf16[256,2048]{1,0:T(8,128)(2,1)S(1)}, u32[]{:S(2)}, u32[]{:S(2)}) collective-permute-start(bf16[256,2048]{1,0:T(8,128)(2,1)S(1)} %get-tuple-element.599.one), channel_id=1, source_target_pairs={{0,1},{3,2},{4,5},{7,6},{8,9},{11,10},{12,13},{15,14},{16,17},{19,... | collective-permute-start | bytes 3145736 | tf_op jit(solution)/shard_map/ppermute | solution.py:1199
  477.2 26.8 %collective-permute-start.72 = (bf16[256,2048]{1,0:T(8,128)(2,1)S(1)}, bf16[256,2048]{1,0:T(8,128)(2,1)S(1)}, u32[]{:S(2)}, u32[]{:S(2)}) collective-permute-start(bf16[256,2048]{1,0:T(8,128)(2,1)S(1)} %get-tuple-element.656.own), channel_id=1, source_target_pairs={{1,0},{2,3},{5,4},{6,7},{9,8},{10,11},{13,12},{14,15},{17,16},{18,... | collective-permute-start | bytes 3145736 | tf_op jit(solution)/shard_map/ppermute | solution.py:1207
  (140 other events, 1534.2 us)
Sparse Core Ops, SparseCore 0:
  48.8 99.0 all-gather.1
  320.9 126.2 reduce-scatter.2
  452.6 72.1 reduce-scatter.4
